TPU v7x, 512 devices: a whole 4x8x8 slice. The times are simulated.
512 devices in a mesh: row: 16 (over y, core), col: 32 (over z, x).
Axes of the slice: x: 4, y: 8, z: 8, core: 2. Of those that a mesh axis runs over, the one named last changes fastest.
Arguments:
- tokens: bfloat16 [256, 512, 256], P('row', 'col'), may hold values from -6 to 6
- input_weight: bfloat16 [256, 1024], replicated, may hold values from -0.375 to 0.375
- kernel: float32 [7, 7, 512], replicated, may hold values from -0.875 to 0.875
- direction_decay_table: float32 [4, 512], replicated, may hold values from 9.765625e-05 to 0.0333333333
- pixel_extra_decay: float32 [256, 512], P('row', 'col'), may hold values from 0 to 0.69
- output_weight: bfloat16 [512, 256], replicated, may hold values from -0.25 to 0.25
Outputs:
- mixed: bfloat16 [256, 512, 256], P('row', 'col')
All inputs are finite; a program needn't handle non-finite values.
Results may differ from a plain program's by a relative error of at most 0.0049.
Values may be sent and summed in bfloat16 or wider, within the bound.
No kernel may reach another device: no remote copies, remote signals or barrier semaphores. Data moves between devices by JAX's collectives and lax.ppermute only.
A program may use at most 64 MiB of HBM per device.

v0:
```python
import jax
import jax.numpy as jnp
from jax import lax
from jax.sharding import PartitionSpec as P


def with_halo(x, sides, width):
    for axis, dim in sides:
        size, length = (lax.axis_size(axis), x.shape[dim])
        up = [(i, (i + 1) % size) for i in range(size - 1)]
        down = [(j, i) for i, j in up]
        last = lax.slice_in_dim(x, length - width, length, axis=dim)
        initial = lax.slice_in_dim(x, 0, width, axis=dim)
        before = lax.ppermute(last, axis, up)
        after = lax.ppermute(initial, axis, down)
        x = jnp.concatenate([before, x, after], axis=dim)
    return x


def prefix(part, axis, combine, identity, reverse):
    count = lax.axis_size(axis)
    place = lax.axis_index(axis)
    ahead = count - 1 - place if reverse else place
    gathered = jax.tree.map(lambda a: lax.all_gather(a, axis), part)
    state = jax.tree.map(lambda a, e: jnp.zeros_like(a) + jnp.asarray(e, a.dtype), part, identity)

    def one(hop, state):
        source = count - 1 - hop if reverse else hop
        return combine(
            state, jax.tree.map(lambda a: lax.dynamic_index_in_dim(a, source, 0, False), gathered)
        )

    return lax.fori_loop(0, ahead, one, state)


def combine(former, latter):
    return (former[0] * latter[0], latter[0] * former[1] + latter[1])


def local_scan(values, decay_logarithm, scan_axis, backward):
    decays = jnp.exp(-decay_logarithm)
    inflow = jnp.sqrt(-jnp.expm1(-2.0 * decay_logarithm)) * values
    return lax.associative_scan(combine, (decays, inflow), reverse=backward, axis=scan_axis)[1]


def stencil(padded, kernel):
    tile_rows = padded.shape[0] - 6
    tile_cols = padded.shape[1] - 6
    summed = jnp.zeros((tile_rows, tile_cols, padded.shape[2]), jnp.float32)
    for shift_row in range(7):
        for shift_col in range(7):
            summed = (
                summed
                + kernel[shift_row, shift_col][None, None, :]
                * padded[shift_row : shift_row + tile_rows, shift_col : shift_col + tile_cols]
            )
    return summed


def body(tokens, input_weight, kernel, direction_decay_table, pixel_extra_decay, output_weight):
    hidden_width = output_weight.shape[0]
    tile_rows = tokens.shape[0]
    tile_cols = tokens.shape[1]
    projected = jnp.dot(tokens, input_weight, preferred_element_type=jnp.float32)
    gate_pre = projected[:, :, hidden_width:]
    padded = with_halo(
        projected[:, :, :hidden_width].astype(jnp.bfloat16), (("row", 0), ("col", 1)), 3
    )
    values = jax.nn.silu(stencil(padded.astype(jnp.float32), kernel))
    leftward_log_decay = direction_decay_table[0][None, None, :] + pixel_extra_decay[:, :, None]
    rightward_log_decay = direction_decay_table[1][None, None, :] + pixel_extra_decay[:, :, None]
    state_left = local_scan(values, leftward_log_decay, 1, False)
    state_right = local_scan(values, rightward_log_decay, 1, True)
    unit_carry = jnp.ones((tile_rows, hidden_width), jnp.float32)
    null_carry = jnp.zeros((tile_rows, hidden_width), jnp.float32)
    enter_left = prefix(
        (jnp.exp(-jnp.sum(leftward_log_decay, axis=1)), state_left[:, -1, :]),
        "col",
        combine,
        (unit_carry, null_carry),
        False,
    )[1]
    enter_right = prefix(
        (jnp.exp(-jnp.sum(rightward_log_decay, axis=1)), state_right[:, 0, :]),
        "col",
        combine,
        (unit_carry, null_carry),
        True,
    )[1]
    summed = state_left + jnp.exp(-lax.cumsum(leftward_log_decay, axis=1)) * enter_left[:, None, :]
    summed = summed + (
        state_right
        + jnp.exp(-lax.cumsum(rightward_log_decay, axis=1, reverse=True)) * enter_right[:, None, :]
    )
    downward_log_decay = direction_decay_table[2][None, None, :] + pixel_extra_decay[:, :, None]
    upward_log_decay = direction_decay_table[3][None, None, :] + pixel_extra_decay[:, :, None]
    state_down = local_scan(values, downward_log_decay, 0, False)
    state_up = local_scan(values, upward_log_decay, 0, True)
    unit_lines = jnp.ones((tile_cols, hidden_width), jnp.float32)
    null_lines = jnp.zeros((tile_cols, hidden_width), jnp.float32)
    enter_down = prefix(
        (jnp.exp(-jnp.sum(downward_log_decay, axis=0)), state_down[-1]),
        "row",
        combine,
        (unit_lines, null_lines),
        False,
    )[1]
    enter_up = prefix(
        (jnp.exp(-jnp.sum(upward_log_decay, axis=0)), state_up[0]),
        "row",
        combine,
        (unit_lines, null_lines),
        True,
    )[1]
    summed = summed + (
        state_down + jnp.exp(-lax.cumsum(downward_log_decay, axis=0)) * enter_down[None, :, :]
    )
    summed = summed + (
        state_up
        + jnp.exp(-lax.cumsum(upward_log_decay, axis=0, reverse=True)) * enter_up[None, :, :]
    )
    gated = (summed * jax.nn.silu(gate_pre)).astype(jnp.bfloat16)
    mixed = tokens.astype(jnp.float32) + jnp.dot(
        gated, output_weight, preferred_element_type=jnp.float32
    )
    return mixed.astype(jnp.bfloat16)


def solution(mesh):
    return jax.shard_map(
        body,
        mesh=mesh,
        in_specs=(P("row", "col", None), P(), P(), P(), P("row", "col"), P()),
        out_specs=P("row", "col", None),
        check_vma=False,
    )
```

profile of v0, /device:TPU:24, one launch (start us, length us, event | category | flops | bytes accessed | tf_op | source)
XLA Modules:
  0.0 500.3 jit_solution(13627527970606477325)
XLA Ops:
  7.6 2.2 fusion.154
  9.8 1.9 collective-permute-start
  11.7 3.6 collective-permute-start.1
  15.6 1.7 collective-permute-done.1
  17.3 3.4 collective-permute-start.2
  20.8 1.3 collective-permute-start.3
  22.9 4.3 collective-permute-done.3
  27.4 4.0 fusion.43
  31.5 3.0 fusion.28
  39.1 1.4 pad_maximum_fusion.14
  40.5 2.1 pad.126
  42.6 1.7 fusion.117
  44.3 1.6 add.605
  45.8 1.6 slice.925
  48.8 1.4 slice.834
  50.1 1.4 slice.835
  51.5 1.4 slice.833
  52.9 1.4 slice.837
  54.2 2.0 fusion.136
  56.2 2.3 slice.843
  58.5 2.3 slice.839
  60.9 1.3 slice.841
  62.2 1.3 slice.840
  63.5 1.8 fusion.141
  65.3 1.3 slice.847
  66.6 1.3 slice.846
  67.9 2.2 slice.845
  70.1 2.2 slice.849
  74.8 1.6 fusion.140
  76.5 2.3 slice.838
  78.8 1.3 slice.855
  81.1 1.4 slice.857
  84.4 1.3 slice.864
  85.8 1.4 slice.866
  87.1 1.3 slice.868
  88.5 1.3 slice.871
  91.9 1.4 slice.874
  94.2 1.3 slice.880
  95.5 1.3 slice.881
  96.8 1.3 slice.879
  99.4 1.3 slice.872
  100.7 1.3 slice.889
  102.7 1.4 slice.861
  104.1 1.4 slice.891
  111.8 5.8 %pad.107 = f32[16,16,512]{2,1,0:T(8,128)S(1)} pad(f32[16,8,512]{2,1,0:T(8,128)} %add.560, f32[]{:T(128)} %constant.112.clone.1), padding=0_0_0x1_0_1x0_0_0 | pad | bytes 786436 | tf_op jit(solution)/shard_map/pad | solution.py:43
  119.7 5.9 %pad.106 = f32[16,16,512]{2,1,0:T(8,128)S(1)} pad(f32[16,8,512]{2,1,0:T(8,128)} %pad_maximum_fusion, f32[]{:T(128)} %constant.112.clone.1), padding=0_0_0x0_1_1x0_0_0 | pad | bytes 786436 | tf_op jit(solution)/shard_map/pad | solution.py:43
  126.4 3.0 slice.862
  129.4 3.0 slice.892
  137.2 5.8 %pad.115 = f32[16,16,512]{2,1,0:T(8,128)S(1)} pad(f32[16,8,512]{2,1,0:T(8,128)} %add.575, f32[]{:T(128)} %constant.112.clone.1), padding=0_0_0x1_0_1x0_0_0 | pad | bytes 786436 | tf_op jit(solution)/shard_map/pad | solution.py:43
  145.0 5.8 %pad.114 = f32[16,16,512]{2,1,0:T(8,128)S(1)} pad(f32[16,8,512]{2,1,0:T(8,128)} %pad_maximum_fusion.1, f32[]{:T(128)} %constant.112.clone.1), padding=0_0_0x0_1_1x0_0_0 | pad | bytes 786436 | tf_op jit(solution)/shard_map/pad | solution.py:43
  151.7 3.2 rev.4
  154.9 1.7 slice_multiply_fusion.51
  161.7 19.6 %all_gather.35 = f32[16,16,512]{2,1,0:T(8,128)} all-gather(f32[1,16,512]{2,1,0:T(8,128)S(1)} %slice_add_fusion.5), channel_id=1, replica_groups=mesh['row'=16,'col'=32] {'row'}, dimensions={0}, use_global_device_ids=true | all-gather | bytes 557056 | tf_op jit(solution)/shard_map/all_gather | solution.py:24
  183.1 16.0 %all_gather.33 = f32[16,16,512]{2,1,0:T(8,128)S(1)} all-gather(f32[1,16,512]{2,1,0:T(8,128)S(1)} %slice_add_fusion.7), channel_id=1, replica_groups=mesh['row'=16,'col'=32] {'row'}, dimensions={0}, use_global_device_ids=true | all-gather | bytes 557056 | tf_op jit(solution)/shard_map/all_gather | solution.py:24
  199.2 17.2 %all-gather.4 = f32[256,512]{1,0:T(8,128)S(1)} all-gather(f32[16,512]{1,0:T(8,128)S(1)} %negate_exponential_fusion.1), channel_id=6, replica_groups=mesh['row'=16,'col'=32] {'row'}, dimensions={0}, use_global_device_ids=true | all-gather | bytes 557056 | tf_op jit(solution)/shard_map/all_gather | solution.py:24
  218.9 16.0 %all-gather.5 = f32[256,512]{1,0:T(8,128)S(1)} all-gather(f32[16,512]{1,0:T(8,128)S(1)} %negate_exponential_fusion), channel_id=7, replica_groups=mesh['row'=16,'col'=32] {'row'}, dimensions={0}, use_global_device_ids=true | all-gather | bytes 557056 | tf_op jit(solution)/shard_map/all_gather | solution.py:24
  234.9 7.2 %while.55 = (s32[]{:T(128)}, f32[16,512]{1,0:T(8,128)S(1)}, s32[]{:T(128)}, f32[16,16,512]{2,1,0:T(8,128)S(1)}, f32[16,16,512]{2,1,0:T(8,128)}, /*index=5*/s32[]{:T(128)}, s32[]{:T(128)}, s32[]{:T(128)}, s32[]{:T(128)}) while((s32[]{:T(128)}, f32[16,512]{1,0:T(8,128)S(1)}, s32[]{:T(128)}, f32[16,16,512]{2,1,0:T(8,128)S(1)}, ...), condition=%wide.region_15.16_spmd, body=%wide.region_14.15_spmd.sunk | while | flops 16390 | bytes 131215 | solution.py:33
  242.1 2.3 copy.15
  244.4 54.5 %all-gather.17.cloned.1.call-done = f32[512,1,512]{2,1,0:T(1,128)} async-done(((f32[16,1,512]{2,1,0:T(1,128)}), f32[512,1,512]{2,1,0:T(1,128)}) %all-gather.17.cloned.1.call-update) | async-done | bytes 1048592 | tf_op jit(solution)/shard_map/all_gather | solution.py:24
  298.9 2.4 copy.16
  301.3 80.3 %all-gather.11.cloned.1.call-done = f32[512,512]{1,0:T(8,128)} async-done(((f32[16,512]{1,0:T(8,128)}), f32[512,512]{1,0:T(8,128)}) %all-gather.11.cloned.1.call-update) | async-done | bytes 1048592 | tf_op jit(solution)/shard_map/all_gather | solution.py:24
  381.6 82.6 %all-gather.15.cloned.1.call-done = f32[512,512]{1,0:T(8,128)} async-done(((f32[16,512]{1,0:T(8,128)}), f32[512,512]{1,0:T(8,128)}) %all-gather.15.cloned.1.call-update) | async-done | bytes 1048592 | tf_op jit(solution)/shard_map/all_gather | solution.py:24
  464.2 25.3 %while.53 = (s32[]{:T(128)}, f32[16,512]{1,0:T(8,128)S(1)}, s32[]{:T(128)}, f32[32,16,512]{2,1,0:T(8,128)}, f32[32,16,512]{2,1,0:T(8,128)}, /*index=5*/s32[]{:T(128)}, s32[]{:T(128)}, s32[]{:T(128)}, s32[]{:T(128)}) while((s32[]{:T(128)}, f32[16,512]{1,0:T(8,128)S(1)}, s32[]{:T(128)}, f32[32,16,512]{2,1,0:T(8,128)}, f32[32,16,512]{2,1,0:T(8,128)}, ...), condition=%wide.region_7.8_spmd, body=%wide.region_6.7_spmd.sunk | while | flops 16390 | bytes 131215 | solution.py:33
  489.5 2.3 fusion.16
  (267 shorter events, 77.7 us)
Async XLA Ops:
  6.5 1.0 copy-start
  6.5 8.9 %copy-start.47 = (f32[7,7,512]{2,1,0:T(8,128)S(1)}, f32[7,7,512]{2,1,0:T(8,128)}, u32[]{:S(2)}) copy-start(f32[7,7,512]{2,1,0:T(8,128)} %param.16) | copy-start | bytes 301060
  6.5 235.6 %all-gather.13.cloned.1.call-start = ((), (), s32[]{:S(2)}) async-start(), calls=%async_computation.1 | async-start | bytes 1081344 | tf_op jit(solution)/shard_map/all_gather | solution.py:24
  9.8 12.2 %copy-start.48 = (f32[4,512]{1,0:T(4,128)S(1)}, f32[4,512]{1,0:T(4,128)}, u32[]{:S(2)}) copy-start(f32[4,512]{1,0:T(4,128)} %param.17) | copy-start | bytes 24580
  9.8 5.7 %collective-permute-start = (bf16[3,16,512]{2,1,0:T(8,128)(2,1)S(1)}, bf16[3,16,512]{2,1,0:T(8,128)(2,1)S(1)}, u32[]{:S(2)}, u32[]{:S(2)}) collective-permute-start(bf16[3,16,512]{2,1,0:T(8,128)(2,1)S(1)} %get-tuple-element.320), channel_id=1, source_target_pairs={{0,32},{32,64},{64,96},{96,128},{128,160},{160,192},{192,224},{224... | collective-permute-start | bytes 147464 | tf_op jit(solution)/shard_map/ppermute | solution.py:14
  11.7 5.5 %collective-permute-start.1 = (bf16[3,16,512]{2,1,0:T(8,128)(2,1)S(1)}, bf16[3,16,512]{2,1,0:T(8,128)(2,1)S(1)}, u32[]{:S(2)}, u32[]{:S(2)}) collective-permute-start(bf16[3,16,512]{2,1,0:T(8,128)(2,1)S(1)} %get-tuple-element.321), channel_id=1, source_target_pairs={{32,0},{64,32},{96,64},{128,96},{160,128},{192,160},{224,192},{256... | collective-permute-start | bytes 147464 | tf_op jit(solution)/shard_map/ppermute | solution.py:15
  15.5 11.8 %copy-start.32 = (f32[16,16]{1,0:T(8,128)S(1)}, f32[16,16]{1,0:T(8,128)}, u32[]{:S(2)}) copy-start(f32[16,16]{1,0:T(8,128)} %param.18) | copy-start | bytes 3076
  17.3 5.5 %collective-permute-start.2 = (bf16[22,3,512]{2,1,0:T(4,128)(2,1)S(1)}, bf16[22,3,512]{2,1,0:T(4,128)(2,1)S(1)}, u32[]{:S(2)}, u32[]{:S(2)}) collective-permute-start(bf16[22,3,512]{2,1,0:T(4,128)(2,1)S(1)} %get-tuple-element.322), channel_id=1, source_target_pairs={{0,1},{1,2},{2,3},{3,4},{4,5},{5,6},{6,7},{7,8},{8,9},{9,10},{10,1... | collective-permute-start | bytes 202760 | tf_op jit(solution)/shard_map/ppermute | solution.py:14
  20.8 6.4 %collective-permute-start.3 = (bf16[22,3,512]{2,1,0:T(4,128)(2,1)S(1)}, bf16[22,3,512]{2,1,0:T(4,128)(2,1)S(1)}, u32[]{:S(2)}, u32[]{:S(2)}) collective-permute-start(bf16[22,3,512]{2,1,0:T(4,128)(2,1)S(1)} %get-tuple-element.323), channel_id=1, source_target_pairs={{1,0},{2,1},{3,2},{4,3},{5,4},{6,5},{7,6},{8,7},{9,8},{10,9},{11,1... | collective-permute-start | bytes 202760 | tf_op jit(solution)/shard_map/ppermute | solution.py:15
  31.4 3.0 copy-start.1
  34.5 1.1 copy-start.3
  34.5 1.2 copy-start.4
  35.7 0.7 copy-start.15
  42.6 4.9 copy-start.2
  85.8 4.1 copy-start.16
  87.1 2.7 copy-start.17
  94.2 11.3 %copy-start.20 = (f32[8,8,512]{2,1,0:T(8,128)}, f32[8,8,512]{2,1,0:T(8,128)S(1)}, u32[]{:S(2)}) copy-start(f32[8,8,512]{2,1,0:T(8,128)S(1)} %get-tuple-element.447) | copy-start | bytes 393220
  95.5 11.2 %copy-start.45 = (f32[1,16,512]{2,1,0:T(8,128)S(1)}, f32[1,16,512]{2,1,0:T(8,128)}, u32[]{:S(2)}) copy-start(f32[1,16,512]{2,1,0:T(8,128)} %slice.1063) | copy-start | bytes 98308
  100.7 6.9 %copy-start.21 = (f32[4,16,512]{2,1,0:T(8,128)S(1)}, f32[4,16,512]{2,1,0:T(8,128)}, u32[]{:S(2)}) copy-start(f32[4,16,512]{2,1,0:T(8,128)} %add.605) | copy-start | bytes 393220
  107.7 0.9 copy-start.18
  107.7 1.0 copy-start.19
  107.8 1.0 copy-start.39
  108.9 1.0 copy-start.29
  108.9 1.2 copy-start.43
  109.0 1.2 copy-start.44
  109.1 1.5 copy-start.24
  109.1 1.5 copy-start.25
  109.9 0.8 copy-start.42
  117.7 7.9 %copy-start.6 = (f32[16,16,512]{2,1,0:T(8,128)}, f32[16,16,512]{2,1,0:T(8,128)S(1)}, u32[]{:S(2)}) copy-start(f32[16,16,512]{2,1,0:T(8,128)S(1)} %pad.107) | copy-start | bytes 1572868
  117.7 1.2 copy-start.41
  119.7 12.8 %copy-start.14 = (f32[8,16,512]{2,1,0:T(8,128)S(1)}, f32[8,16,512]{2,1,0:T(8,128)}, u32[]{:S(2)}) copy-start(f32[8,16,512]{2,1,0:T(8,128)} %get-tuple-element.319) | copy-start | bytes 786436
  125.6 9.8 %copy-start.8 = (f32[16,16,512]{2,1,0:T(8,128)}, f32[16,16,512]{2,1,0:T(8,128)S(1)}, u32[]{:S(2)}) copy-start(f32[16,16,512]{2,1,0:T(8,128)S(1)} %pad.106) | copy-start | bytes 1572868
  126.3 6.7 %copy-start.27 = (f32[16,2,512]{2,1,0:T(2,128)S(1)}, f32[16,2,512]{2,1,0:T(2,128)}, u32[]{:S(2)}) copy-start(f32[16,2,512]{2,1,0:T(2,128)} %slice.879) | copy-start | bytes 196612
  126.3 6.7 %copy-start.30 = (f32[16,2,512]{2,1,0:T(2,128)S(1)}, f32[16,2,512]{2,1,0:T(2,128)}, u32[]{:S(2)}) copy-start(f32[16,2,512]{2,1,0:T(2,128)} %slice.880) | copy-start | bytes 196612
  126.3 6.7 %copy-start.31 = (f32[16,2,512]{2,1,0:T(2,128)S(1)}, f32[16,2,512]{2,1,0:T(2,128)}, u32[]{:S(2)}) copy-start(f32[16,2,512]{2,1,0:T(2,128)} %slice.881) | copy-start | bytes 196612
  126.3 172.6 %all-gather.17.cloned.1.call-start = ((), (), s32[]{:S(2)}) async-start(), calls=%async_computation.3 | async-start | bytes 1081344 | tf_op jit(solution)/shard_map/all_gather | solution.py:24
  129.4 6.3 %copy-start.22 = (f32[16,3,512]{2,1,0:T(4,128)S(1)}, f32[16,3,512]{2,1,0:T(4,128)}, u32[]{:S(2)}) copy-start(f32[16,3,512]{2,1,0:T(4,128)} %slice.872) | copy-start | bytes 294916
  129.4 6.3 %copy-start.23 = (f32[16,3,512]{2,1,0:T(4,128)S(1)}, f32[16,3,512]{2,1,0:T(4,128)}, u32[]{:S(2)}) copy-start(f32[16,3,512]{2,1,0:T(4,128)} %slice.889) | copy-start | bytes 294916
  135.4 0.8 copy-start.40
  137.2 6.9 %copy-start.38 = (f32[16,1,512]{2,1,0:T(1,128)S(1)}, f32[16,1,512]{2,1,0:T(1,128)}, u32[]{:S(2)}) copy-start(f32[16,1,512]{2,1,0:T(1,128)} %slice.1028) | copy-start | bytes 98308
  157.2 224.4 %all-gather.11.cloned.1.call-start = ((), (), s32[]{:S(2)}) async-start(), calls=%async_computation | async-start | bytes 1081344 | tf_op jit(solution)/shard_map/all_gather | solution.py:24
  158.4 1.9 copy-start.46
  159.3 1.2 copy-start.36
  159.3 1.2 copy-start.35
  160.3 0.8 copy-start.34
  181.3 1.2 copy-start.37
  182.3 0.8 copy-start.33
  182.4 281.8 %all-gather.15.cloned.1.call-start = ((), (), s32[]{:S(2)}) async-start(), calls=%async_computation.2 | async-start | bytes 1081344 | tf_op jit(solution)/shard_map/all_gather | solution.py:24
  182.5 33.8 %copy-start.12 = (f32[16,16,512]{2,1,0:T(8,128)S(1)}, f32[16,16,512]{2,1,0:T(8,128)}, u32[]{:S(2)}) copy-start(f32[16,16,512]{2,1,0:T(8,128)} %get-tuple-element.418) | copy-start | bytes 1572868
  183.1 34.4 %copy-start.11 = (f32[16,16,512]{2,1,0:T(8,128)S(1)}, f32[16,16,512]{2,1,0:T(8,128)}, u32[]{:S(2)}) copy-start(f32[16,16,512]{2,1,0:T(8,128)} %get-tuple-element.414) | copy-start | bytes 1572868
  298.9 190.6 %copy-start.7 = (f32[16,16,512]{2,1,0:T(8,128)S(1)}, f32[16,16,512]{2,1,0:T(8,128)}, u32[]{:S(2)}) copy-start(f32[16,16,512]{2,1,0:T(8,128)} %copy-done.6) | copy-start | bytes 1572868
  298.9 190.6 %copy-start.9 = (f32[16,16,512]{2,1,0:T(8,128)S(1)}, f32[16,16,512]{2,1,0:T(8,128)}, u32[]{:S(2)}) copy-start(f32[16,16,512]{2,1,0:T(8,128)} %copy-done.8) | copy-start | bytes 1572868
  298.9 190.6 %copy-start.13 = (f32[16,16,512]{2,1,0:T(8,128)S(1)}, f32[16,16,512]{2,1,0:T(8,128)}, u32[]{:S(2)}) copy-start(f32[16,16,512]{2,1,0:T(8,128)} %rev.4) | copy-start | bytes 1572868
  489.5 2.3 copy-start.5
  489.5 2.3 copy-start.10
  491.9 0.9 copy-start.26
  491.9 1.0 copy-start.28
Sparse Core Ops, SparseCore 0:
  126.5 89.6 all-gather.12
  219.4 79.5 all-gather.16
  302.1 79.5 all-gather.10
  384.7 79.5 all-gather.14
where the time goes:
time: 508 us; the launch traced here: 500 us
  waiting for transfers between devices  224 us (44%)
  local copies, waits for them, and re-layouts  99.3 us (20%)
  other arithmetic  79 us (16%)
  blocking collectives  68.8 us (14%)
  between operations  14.1 us (3%)
  starting transfers between devices  10.6 us (2%)
    all_gather x4, waiting for transfers between devices, prefix(): gathered = jax.tree.map(lambda a: lax.all_gather(a, axis), part)  217 us
    all_gather x4, blocking collectives, prefix(): gathered = jax.tree.map(lambda a: lax.all_gather(a, axis), part)  68.8 us
    slice x49, local copies, waits for them, and re-layouts, local_scan(): lax.associative_scan(combine, (decays, inflow), reverse=backward, axis=sc...  58 us
    add x56, other arithmetic, combine(): return (former[0] * latter[0], latter[0] * former[1] + latter[1])  38.6 us
    pad x24, local copies, waits for them, and re-layouts, local_scan(): lax.associative_scan(combine, (decays, inflow), reverse=backward, axis=sc...  28.4 us
  transfers between devices with their start and end apart: 8, of which 6 were waited for; matrix products, arithmetic and copies ran while one was open for 10% of the time, Pallas kernels for 0%

commit v1 on v0

v1 whole, which is shorter than its diff:
```python
import functools

import jax
import jax.numpy as jnp
from jax import lax
from jax.experimental import pallas as pl
from jax.experimental.pallas import tpu as pltpu
from jax.sharding import PartitionSpec as P

T = 16
PX = T * T
PW = 24
LANES = 128
F32 = jnp.float32
BF16 = jnp.bfloat16
VMEM = pltpu.VMEM


def conv_scan_kernel(pad_ref, wv_ref, taps_ref, cst_ref, px_ref,
                     sum_ref, left_ref, right_ref, down_ref, up_ref,
                     v_ref, g_ref, h_ref, val_ref):
    groups = v_ref.shape[0]
    rows = T + 6
    pad = pad_ref[...]
    for half in range(groups // 2):
        p = jnp.dot(pad, wv_ref[:, half * 256:(half + 1) * 256], preferred_element_type=F32)
        p = p.astype(BF16).astype(F32)
        v_ref[2 * half] = p[:, :LANES]
        v_ref[2 * half + 1] = p[:, LANES:]
    px = px_ref[...]
    g_ref[...] = jnp.broadcast_to(px[:, 0:1], (PX, LANES))
    h_ref[...] = jnp.broadcast_to(px[:, 1:2], (PX, LANES))

    def group(ct, carry):
        lanes = pl.ds(pl.multiple_of(ct * LANES, LANES), LANES)
        cst = [cst_ref[pl.ds(k, 1), lanes] for k in range(12)]

        def flow(d, g, h, x):
            q = cst[4 + d] + cst[8 + d] * h
            return cst[d] * g, q * lax.rsqrt(q) * x

        for jt in range(2):
            acc = [jnp.zeros((8, LANES), F32) for _ in range(T)]
            for b in range(7):
                tap = [taps_ref[pl.ds(a * 7 + b, 1), lanes] for a in range(7)]
                tap = [jnp.broadcast_to(t, (8, LANES)) for t in tap]
                for r in range(rows):
                    x = v_ref[ct, pl.ds(r * PW + jt * 8 + b, 8), :]
                    for a in range(7):
                        i = r - a
                        if 0 <= i < T:
                            acc[i] = acc[i] + tap[a] * x
            vals = [x / (1.0 + jnp.exp(-x)) for x in acc]
            for i in range(T):
                val_ref[pl.ds(i * T + jt * 8, 8), :] = vals[i]
            state = jnp.zeros((8, LANES), F32)
            downs = []
            for i in range(T):
                at = pl.ds(i * T + jt * 8, 8)
                d, f = flow(2, g_ref[at, :], h_ref[at, :], vals[i])
                state = d * state + f
                downs.append(state)
            down_ref[ct, pl.ds(jt * 8, 8), :] = state
            state = jnp.zeros((8, LANES), F32)
            for i in reversed(range(T)):
                at = pl.ds(i * T + jt * 8, 8)
                d, f = flow(3, g_ref[at, :], h_ref[at, :], vals[i])
                state = d * state + f
                sum_ref[ct, at, :] = downs[i] + state
            up_ref[ct, pl.ds(jt * 8, 8), :] = state
        for it in range(2):
            state = jnp.zeros((8, LANES), F32)
            lefts = []
            for j in range(T):
                at = pl.ds(it * 8 * T + j, 8, stride=T)
                d, f = flow(0, g_ref[at, :], h_ref[at, :], val_ref[at, :])
                state = d * state + f
                lefts.append(state)
            left_ref[ct, pl.ds(it * 8, 8), :] = state
            state = jnp.zeros((8, LANES), F32)
            for j in reversed(range(T)):
                at = pl.ds(it * 8 * T + j, 8, stride=T)
                d, f = flow(1, g_ref[at, :], h_ref[at, :], val_ref[at, :])
                state = d * state + f
                sum_ref[ct, at, :] = sum_ref[ct, at, :] + (lefts[j] + state)
            right_ref[ct, pl.ds(it * 8, 8), :] = state
        return carry

    lax.fori_loop(0, groups, group, 0)


def finish_kernel(place_ref, rc_ref, rr_ref, cst_ref, px_ref, sum_ref, gate_ref, tok_ref, wo_ref,
                  out_ref, acc_ref, g_ref, enter_ref, gated_ref):
    groups = acc_ref.shape[0]
    px = px_ref[...]
    g_ref[...] = jnp.broadcast_to(px[:, 0:1], (PX, LANES))

    def enter(recv_ref, me, first):
        count = recv_ref.shape[0]
        for side in range(2):
            order = range(count) if side == 0 else reversed(range(count))
            whole = [cst_ref[pl.ds(12 + first + side, 1), ct * LANES:(ct + 1) * LANES]
                     for ct in range(groups)]
            state = [[jnp.zeros((8, LANES), F32) for _ in range(2)] for _ in range(groups)]
            for k in order:
                take = k < me if side == 0 else k > me
                block = recv_ref[k].astype(F32)
                tail = block[64:72]
                for it in range(2):
                    decay = tail[:, 64 * it:64 * it + 1] + tail[:, 64 * it + 32:64 * it + 33]
                    decay = jnp.broadcast_to(decay, (8, LANES))
                    for ct in range(groups):
                        at = ct * T + it * 8
                        new = (whole[ct] * decay) * state[ct][it] + block[at:at + 8]
                        state[ct][it] = jnp.where(take, new, state[ct][it])
            for ct in range(groups):
                for it in range(2):
                    enter_ref[first + side, ct, pl.ds(it * 8, 8), :] = state[ct][it]

    enter(rc_ref, place_ref[1], 0)
    enter(rr_ref, place_ref[0], 2)

    def group(ct, carry):
        lanes = pl.ds(pl.multiple_of(ct * LANES, LANES), LANES)
        base = [cst_ref[pl.ds(k, 1), lanes] for k in range(4)]
        for it in range(2):
            left = enter_ref[0, ct, pl.ds(it * 8, 8), :]
            right = enter_ref[1, ct, pl.ds(it * 8, 8), :]
            lefts = []
            for j in range(T):
                left = left * (base[0] * g_ref[pl.ds(it * 8 * T + j, 8, stride=T), :])
                lefts.append(left)
            for j in reversed(range(T)):
                at = pl.ds(it * 8 * T + j, 8, stride=T)
                right = right * (base[1] * g_ref[at, :])
                acc_ref[ct, at, :] = lefts[j] + right
        for jt in range(2):
            down = enter_ref[2, ct, pl.ds(jt * 8, 8), :]
            up = enter_ref[3, ct, pl.ds(jt * 8, 8), :]
            downs = []
            for i in range(T):
                down = down * (base[2] * g_ref[pl.ds(i * T + jt * 8, 8), :])
                downs.append(down)
            for i in reversed(range(T)):
                at = pl.ds(i * T + jt * 8, 8)
                up = up * (base[3] * g_ref[at, :])
                acc_ref[ct, at, :] = acc_ref[ct, at, :] + sum_ref[ct, at, :] + (downs[i] + up)
        gated_ref[:, lanes] = (acc_ref[ct] * gate_ref[:, lanes]).astype(BF16)
        return carry

    lax.fori_loop(0, groups, group, 0)
    mixed = jnp.dot(gated_ref[...], wo_ref[...], preferred_element_type=F32)
    out_ref[...] = (tok_ref[...].astype(F32) + mixed).astype(BF16)


def neighbours(x, axis, first, last):
    size = lax.axis_size(axis)
    up = [(i, i + 1) for i in range(size - 1)]
    down = [(i + 1, i) for i in range(size - 1)]
    return lax.ppermute(last, axis, up), lax.ppermute(first, axis, down)


def tail_block(product):
    high = product.astype(BF16)
    low = (product - high.astype(F32)).astype(BF16)
    parts = [jnp.broadcast_to(p[:, None], (8, 32))
             for p in (high[:8], low[:8], high[8:], low[8:])]
    return jnp.concatenate(parts, axis=1)


def exchange(former, latter, tail, axis):
    count = lax.axis_size(axis)
    peer = lax.broadcasted_iota(jnp.int32, (count, 1, 1), 0)
    states = jnp.where(peer > lax.axis_index(axis),
                       former.reshape(1, 64, LANES).astype(BF16), latter.reshape(1, 64, LANES).astype(BF16))
    tails = jnp.broadcast_to(tail[None], (count, 8, LANES))
    return lax.all_to_all(jnp.concatenate([states, tails], axis=1), axis, 0, 0, tiled=True)


def body(tokens, input_weight, kernel, direction_decay_table, pixel_extra_decay, output_weight):
    width = output_weight.shape[0]
    groups = width // LANES
    channels = tokens.shape[2]
    table, extra = direction_decay_table, pixel_extra_decay
    above, below = neighbours(tokens, "row", tokens[:3], tokens[T - 3:])
    tall = jnp.concatenate([above, tokens, below], axis=0)
    before, after = neighbours(tall, "col", tall[:, :3], tall[:, T - 3:])
    pad = jnp.concatenate([before, tall, after, jnp.zeros((T + 6, 2, channels), BF16)], axis=1)
    pad = pad.reshape((T + 6) * PW, channels)

    cst = jnp.concatenate([jnp.exp(-table), -jnp.expm1(-2.0 * table), jnp.exp(-2.0 * table),
                           jnp.exp(-float(T) * table)], axis=0)
    px = jnp.stack([jnp.exp(-extra), -jnp.expm1(-2.0 * extra)], axis=-1).reshape(PX, 2)
    flat = tokens.reshape(PX, channels)
    gate = jax.nn.silu(jnp.dot(flat, input_weight[:, width:], preferred_element_type=F32))

    spec = pl.BlockSpec(memory_space=VMEM)
    edge = jax.ShapeDtypeStruct((groups, T, LANES), F32)
    local, left, right, down, up = pl.pallas_call(
        conv_scan_kernel,
        out_shape=(jax.ShapeDtypeStruct((groups, PX, LANES), F32), edge, edge, edge, edge),
        in_specs=[spec] * 5,
        out_specs=(spec,) * 5,
        scratch_shapes=[VMEM((groups, (T + 6) * PW, LANES), F32), VMEM((PX, LANES), F32),
                        VMEM((PX, LANES), F32), VMEM((PX, LANES), F32)],
        compiler_params=pltpu.CompilerParams(vmem_limit_bytes=24 * 2**20),
        name="conv_scan",
    )(pad, input_weight[:, :width], kernel.reshape(49, width), cst, px)

    from_cols = exchange(left, right, tail_block(jnp.exp(-jnp.sum(extra, axis=1))), "col")
    from_rows = exchange(down, up, tail_block(jnp.exp(-jnp.sum(extra, axis=0))), "row")
    place = jnp.stack([lax.axis_index("row"), lax.axis_index("col")]).astype(jnp.int32)

    mixed = pl.pallas_call(
        finish_kernel,
        out_shape=jax.ShapeDtypeStruct((PX, channels), BF16),
        in_specs=[pl.BlockSpec(memory_space=pltpu.SMEM)] + [spec] * 8,
        out_specs=spec,
        scratch_shapes=[VMEM((groups, PX, LANES), F32), VMEM((PX, LANES), F32),
                        VMEM((4, groups, T, LANES), F32), VMEM((PX, width), BF16)],
        compiler_params=pltpu.CompilerParams(vmem_limit_bytes=24 * 2**20),
        name="finish",
    )(place, from_cols, from_rows, cst, px, local, gate, flat, output_weight)
    return mixed.reshape(T, T, channels)


def solution(mesh):
    return jax.shard_map(
        body,
        mesh=mesh,
        in_specs=(P("row", "col", None), P(), P(), P(), P("row", "col"), P()),
        out_specs=P("row", "col", None),
        check_vma=False,
    )
```

time: 508 us -> 83.5 us (0.16)
  the two profiles are of different devices: /device:TPU:24 before, /device:TPU:1 now
where the time goes in v1:
time: 83.5 us; the launch traced here: 83 us
  starting transfers between devices  35.3 us (42%)
  waiting for transfers between devices  32.2 us (39%)
  Pallas kernels  8.08 us (10%)
  other arithmetic  3.82 us (5%)
  local copies, waits for them, and re-layouts  3.06 us (4%)
    all_to_all x2, waiting for transfers between devices, exchange(): lax.all_to_all(jnp.concatenate([states, tails], axis=1), axis, 0, 0, tile...  29.1 us
    all_to_all x2, starting transfers between devices, exchange(): lax.all_to_all(jnp.concatenate([states, tails], axis=1), axis, 0, 0, tile...  21.9 us
    ppermute x4, starting transfers between devices, neighbours(): return (lax.ppermute(last, axis, up), lax.ppermute(first, axis, down))  13.4 us
    pallas_call x1, Pallas kernels, body(): pl.pallas_call(finish_kernel, out_shape=jax.ShapeDtypeStruct((PX, channel...  4.76 us
    pallas_call x1, Pallas kernels, body(): pl.pallas_call(conv_scan_kernel, out_shape=(jax.ShapeDtypeStruct((groups,...  3.31 us
    ppermute x4, waiting for transfers between devices, neighbours(): return (lax.ppermute(last, axis, up), lax.ppermute(first, axis, down))  3.18 us
  transfers between devices with their start and end apart: 6, of which 3 were waited for; matrix products, arithmetic and copies ran while one was open for 6% of the time, Pallas kernels for 0%

profile of v1, /device:TPU:1, one launch (start us, length us, event | category | flops | bytes accessed | tf_op | source)
XLA Modules:
  0.0 83.0 jit_solution(6985213540553523820)
XLA Ops:
  0.0 0.0 copy-start.3
  0.0 0.8 fusion.8
  0.8 0.0 copy-start.2
  0.8 8.9 %collective-permute-start.1 = (bf16[3,16,256]{2,1,0:T(8,128)(2,1)S(1)}, bf16[3,16,256]{2,1,0:T(8,128)(2,1)S(1)}, u32[]{:S(2)}, u32[]{:S(2)}) collective-permute-start(bf16[3,16,256]{2,1,0:T(8,128)(2,1)S(1)} %get-tuple-element.19), channel_id=1, source_target_pairs={{32,0},{64,32},{96,64},{128,96},{160,128},{192,160},{224,192},{256... | collective-permute-start | bytes 73736 | tf_op jit(solution)/shard_map/ppermute | solution.py:160
  9.7 1.9 %collective-permute-start = (bf16[3,16,256]{2,1,0:T(8,128)(2,1)S(1)}, bf16[3,16,256]{2,1,0:T(8,128)(2,1)S(1)}, u32[]{:S(2)}, u32[]{:S(2)}) collective-permute-start(bf16[3,16,256]{2,1,0:T(8,128)(2,1)S(1)} %get-tuple-element.20), channel_id=1, source_target_pairs={{0,32},{32,64},{64,96},{96,128},{128,160},{160,192},{192,224},{224... | collective-permute-start | bytes 73736 | tf_op jit(solution)/shard_map/ppermute | solution.py:160
  11.6 0.8 fusion.6
  12.5 0.1 stack.21
  12.5 0.1 stack.22
  12.6 0.1 fusion.11
  12.7 0.1 fusion.12
  12.8 0.1 fusion.10
  12.9 0.1 fusion.9
  12.9 0.7 negate_exponential_fusion.1
  13.7 0.1 broadcast_in_dim.123
  13.8 0.1 broadcast_in_dim.124
  13.8 0.1 broadcast_in_dim.125
  13.9 0.1 broadcast_in_dim.126
  14.0 0.1 pad_maximum_fusion.5
  14.1 0.0 collective-permute-done
  14.1 0.9 %constant_dynamic-update-slice_fusion.1 = bf16[22,16,256]{2,1,0:T(8,128)(2,1)S(1)} fusion(bf16[22,16,256]{2,1,0:T(8,128)(2,1)S(1)} %constant_dynamic-update-slice_fusion.2, bf16[16,16,256]{2,1,0:T(8,128)(2,1)} %param.6), kind=kLoop, calls=%fused_computation.10 | loop fusion | bytes 262144
  15.0 0.0 collective-permute-done.1
  15.1 1.3 %collective-permute-start.2 = (bf16[22,3,256]{2,1,0:T(4,128)(2,1)S(1)}, bf16[22,3,256]{2,1,0:T(4,128)(2,1)S(1)}, u32[]{:S(2)}, u32[]{:S(2)}) collective-permute-start(bf16[22,3,256]{2,1,0:T(4,128)(2,1)S(1)} %get-tuple-element.17), channel_id=1, source_target_pairs={{0,1},{1,2},{2,3},{3,4},{4,5},{5,6},{6,7},{7,8},{8,9},{9,10},{10,1... | collective-permute-start | bytes 101384 | tf_op jit(solution)/shard_map/ppermute | solution.py:160
  16.4 1.3 %collective-permute-start.3 = (bf16[22,3,256]{2,1,0:T(4,128)(2,1)S(1)}, bf16[22,3,256]{2,1,0:T(4,128)(2,1)S(1)}, u32[]{:S(2)}, u32[]{:S(2)}) collective-permute-start(bf16[22,3,256]{2,1,0:T(4,128)(2,1)S(1)} %get-tuple-element.18), channel_id=1, source_target_pairs={{1,0},{2,1},{3,2},{4,3},{5,4},{6,5},{7,6},{8,7},{9,8},{10,9},{11,1... | collective-permute-start | bytes 101384 | tf_op jit(solution)/shard_map/ppermute | solution.py:160
  17.7 0.0 copy-done.3
  17.7 0.1 copy.9.px_ref
  17.9 0.0 copy-done.2
  17.9 0.1 pad.21.clone
  18.0 0.0 collective-permute-done.2
  18.0 3.2 %collective-permute-done.3 = bf16[22,3,256]{2,1,0:T(4,128)(2,1)S(1)} collective-permute-done((bf16[22,3,256]{2,1,0:T(4,128)(2,1)S(1)}, bf16[22,3,256]{2,1,0:T(4,128)(2,1)S(1)}, u32[]{:S(2)}, u32[]{:S(2)}) %collective-permute-start.3) | collective-permute-done | bytes 33824 | tf_op jit(solution)/shard_map/ppermute | solution.py:160
  21.2 0.2 maximum_maximum_fusion
  21.3 3.3 %conv_scan.1 = (f32[4,256,128]{2,1,0:T(8,128)S(1)}, f32[4,16,128]{2,1,0:T(8,128)S(1)}, f32[4,16,128]{2,1,0:T(8,128)S(1)}, f32[4,16,128]{2,1,0:T(8,128)S(1)}, f32[4,16,128]{2,1,0:T(8,128)S(1)}) custom-call(bf16[528,256]{1,0:T(8,128)(2,1)S(1)} %bitcast.10, bf16[256,512]{1,0:T(8,128)(2,1)S(1)} %slice.46.wv_ref, f32[49,512]{1,0:T(8,128)S(1)} %reshape.74.taps_ref, ...), custom_call_target="tpu_custom_call" | custom-call | tf_op jit(solution)/shard_map/conv_scan/pallas_call | solution.py:199
  24.7 0.1 broadcast_select_fusion.1
  24.8 0.7 pad_maximum_fusion.1
  25.5 7.0 %all-to-all-start.1 = ((bf16[16,72,128]{2,1,0:T(8,128)(2,1)}), bf16[16,72,128]{2,1,0:T(8,128)(2,1)S(1)}, u32[]{:S(2)}, u32[]{:S(2)}) async-start(bf16[16,72,128]{2,1,0:T(8,128)(2,1)} %pad_maximum_fusion.1), calls=%async_computation.1 | async-start | bytes 589824 | tf_op jit(solution)/shard_map/all_to_all | solution.py:177
  32.5 0.1 broadcast_in_dim.75
  32.6 0.1 broadcast_in_dim.74
  32.7 0.1 broadcast_in_dim.118
  32.8 0.1 broadcast_in_dim.76
  32.8 0.1 pad_maximum_fusion.4
  32.9 0.1 broadcast_select_fusion
  33.1 0.9 %pad_maximum_fusion = bf16[32,72,128]{2,1,0:T(8,128)(2,1)} fusion(bf16[32,8,128]{2,1,0:T(8,128)(2,1)S(1)} %broadcast_in_dim.119, bf16[32,64,128]{2,1,0:T(8,128)(2,1)S(1)} %broadcast_select_fusion), kind=kLoop, calls=%fused_computation | loop fusion | flops 1179648 | bytes 1179648 | tf_op jit(solution)/shard_map/concatenate | solution.py:177
  33.9 0.0 copy-start
  33.9 11.0 %all-to-all-done.1.rr_ref = bf16[16,72,128]{2,1,0:T(8,128)(2,1)S(1)} async-done(((bf16[16,72,128]{2,1,0:T(8,128)(2,1)}), bf16[16,72,128]{2,1,0:T(8,128)(2,1)S(1)}, u32[]{:S(2)}, u32[]{:S(2)}) %all-to-all-start.1) | async-done | bytes 294944 | tf_op jit(solution)/shard_map/all_to_all | solution.py:177
  44.9 14.9 %all-to-all-start = ((bf16[32,72,128]{2,1,0:T(8,128)(2,1)}), bf16[32,72,128]{2,1,0:T(8,128)(2,1)S(1)}, u32[]{:S(2)}, u32[]{:S(2)}) async-start(bf16[32,72,128]{2,1,0:T(8,128)(2,1)} %pad_maximum_fusion), calls=%async_computation | async-start | bytes 1179648 | tf_op jit(solution)/shard_map/all_to_all | solution.py:177
  59.8 0.1 pad_add_fusion.place_ref
  59.9 0.0 copy-done
  59.9 0.0 copy-start.1
  59.9 0.3 divide_multiply_fusion.gate_ref
  60.2 18.1 %all-to-all-done.rc_ref = bf16[32,72,128]{2,1,0:T(8,128)(2,1)S(1)} async-done(((bf16[32,72,128]{2,1,0:T(8,128)(2,1)}), bf16[32,72,128]{2,1,0:T(8,128)(2,1)S(1)}, u32[]{:S(2)}, u32[]{:S(2)}) %all-to-all-start) | async-done | bytes 589856 | tf_op jit(solution)/shard_map/all_to_all | solution.py:177
  78.3 0.0 copy-done.1
  78.3 4.8 %finish.1 = bf16[256,256]{1,0:T(8,128)(2,1)} custom-call(s32[2]{0:T(128)S(1)} %pad_add_fusion.place_ref, bf16[32,72,128]{2,1,0:T(8,128)(2,1)S(1)} %all-to-all-done.rc_ref, bf16[16,72,128]{2,1,0:T(8,128)(2,1)S(1)} %all-to-all-done.1.rr_ref, f32[16,512]{1,0:T(8,128)S(1)} %pad_maximum_fusion.2.cst_ref, f32[256,2]{1,0:T(8,128)S(1)} %copy.9.px_ref, ...), custom_call_target="tpu_custom_call" | custom-call | tf_op jit(solution)/shard_map/finish/pallas_call | solution.py:214
  (17 shorter events, 0.2 us)
Async XLA Ops:
  0.0 17.7 %copy-start.3 = (f32[7,7,512]{2,1,0:T(8,128)S(1)}, f32[7,7,512]{2,1,0:T(8,128)}, u32[]{:S(2)}) copy-start(f32[7,7,512]{2,1,0:T(8,128)} %param.8) | copy-start | bytes 301060
  0.8 17.1 %copy-start.2 = (bf16[256,1024]{1,0:T(8,128)(2,1)S(1)}, bf16[256,1024]{1,0:T(8,128)(2,1)}, u32[]{:S(2)}) copy-start(bf16[256,1024]{1,0:T(8,128)(2,1)} %param.7) | copy-start | bytes 1572868
  0.8 14.2 %collective-permute-start.1 = (bf16[3,16,256]{2,1,0:T(8,128)(2,1)S(1)}, bf16[3,16,256]{2,1,0:T(8,128)(2,1)S(1)}, u32[]{:S(2)}, u32[]{:S(2)}) collective-permute-start(bf16[3,16,256]{2,1,0:T(8,128)(2,1)S(1)} %get-tuple-element.19), channel_id=1, source_target_pairs={{32,0},{64,32},{96,64},{128,96},{160,128},{192,160},{224,192},{256... | collective-permute-start | bytes 73736 | tf_op jit(solution)/shard_map/ppermute | solution.py:160
  9.7 4.4 %collective-permute-start = (bf16[3,16,256]{2,1,0:T(8,128)(2,1)S(1)}, bf16[3,16,256]{2,1,0:T(8,128)(2,1)S(1)}, u32[]{:S(2)}, u32[]{:S(2)}) collective-permute-start(bf16[3,16,256]{2,1,0:T(8,128)(2,1)S(1)} %get-tuple-element.20), channel_id=1, source_target_pairs={{0,32},{32,64},{64,96},{96,128},{128,160},{160,192},{192,224},{224... | collective-permute-start | bytes 73736 | tf_op jit(solution)/shard_map/ppermute | solution.py:160
  15.1 2.9 %collective-permute-start.2 = (bf16[22,3,256]{2,1,0:T(4,128)(2,1)S(1)}, bf16[22,3,256]{2,1,0:T(4,128)(2,1)S(1)}, u32[]{:S(2)}, u32[]{:S(2)}) collective-permute-start(bf16[22,3,256]{2,1,0:T(4,128)(2,1)S(1)} %get-tuple-element.17), channel_id=1, source_target_pairs={{0,1},{1,2},{2,3},{3,4},{4,5},{5,6},{6,7},{7,8},{8,9},{9,10},{10,1... | collective-permute-start | bytes 101384 | tf_op jit(solution)/shard_map/ppermute | solution.py:160
  16.4 4.8 %collective-permute-start.3 = (bf16[22,3,256]{2,1,0:T(4,128)(2,1)S(1)}, bf16[22,3,256]{2,1,0:T(4,128)(2,1)S(1)}, u32[]{:S(2)}, u32[]{:S(2)}) collective-permute-start(bf16[22,3,256]{2,1,0:T(4,128)(2,1)S(1)} %get-tuple-element.18), channel_id=1, source_target_pairs={{1,0},{2,1},{3,2},{4,3},{5,4},{6,5},{7,6},{8,7},{9,8},{10,9},{11,1... | collective-permute-start | bytes 101384 | tf_op jit(solution)/shard_map/ppermute | solution.py:160
  25.5 19.4 %all-to-all-start.1 = ((bf16[16,72,128]{2,1,0:T(8,128)(2,1)}), bf16[16,72,128]{2,1,0:T(8,128)(2,1)S(1)}, u32[]{:S(2)}, u32[]{:S(2)}) async-start(bf16[16,72,128]{2,1,0:T(8,128)(2,1)} %pad_maximum_fusion.1), calls=%async_computation.1 | async-start | bytes 589824 | tf_op jit(solution)/shard_map/all_to_all | solution.py:177
  33.9 26.0 %copy-start = (bf16[16,16,256]{2,1,0:T(8,128)(2,1)S(1)}, bf16[16,16,256]{2,1,0:T(8,128)(2,1)}, u32[]{:S(2)}) copy-start(bf16[16,16,256]{2,1,0:T(8,128)(2,1)} %param.6) | copy-start | bytes 393220
  44.9 33.4 %all-to-all-start = ((bf16[32,72,128]{2,1,0:T(8,128)(2,1)}), bf16[32,72,128]{2,1,0:T(8,128)(2,1)S(1)}, u32[]{:S(2)}, u32[]{:S(2)}) async-start(bf16[32,72,128]{2,1,0:T(8,128)(2,1)} %pad_maximum_fusion), calls=%async_computation | async-start | bytes 1179648 | tf_op jit(solution)/shard_map/all_to_all | solution.py:177
  59.9 18.4 %copy-start.1 = (bf16[512,256]{1,0:T(8,128)(2,1)S(1)}, bf16[512,256]{1,0:T(8,128)(2,1)}, u32[]{:S(2)}) copy-start(bf16[512,256]{1,0:T(8,128)(2,1)} %wo_ref.1) | copy-start | bytes 786436

commit v2 on v1

v2 whole, which is shorter than its diff:
```python
import jax
import jax.numpy as jnp
from jax import lax
from jax.experimental import pallas as pl
from jax.experimental.pallas import tpu as pltpu
from jax.sharding import PartitionSpec as P

T = 16
PX = T * T
PW = 24
LANES = 128
XS = 4
FAR = 8
F32 = jnp.float32
BF16 = jnp.bfloat16
VMEM = pltpu.VMEM


def conv_scan_kernel(pad_ref, wv_ref, taps_ref, cst_ref, px_ref, tails_ref,
                     sum_ref, near_ref,
                     v_ref, g_ref, h_ref, val_ref, end_ref):
    groups = v_ref.shape[0]
    rows = T + 6
    pad = pad_ref[...]
    for half in range(groups // 2):
        p = jnp.dot(pad, wv_ref[:, half * 256:(half + 1) * 256], preferred_element_type=F32)
        p = p.astype(BF16).astype(F32)
        v_ref[2 * half] = p[:, :LANES]
        v_ref[2 * half + 1] = p[:, LANES:]
    px = px_ref[...]
    g_ref[...] = jnp.broadcast_to(px[:, 0:1], (PX, LANES))
    h_ref[...] = jnp.broadcast_to(px[:, 1:2], (PX, LANES))

    def group(ct, carry):
        lanes = pl.ds(pl.multiple_of(ct * LANES, LANES), LANES)
        cst = [cst_ref[pl.ds(k, 1), lanes] for k in range(12)]

        def flow(d, g, h, x):
            q = cst[4 + d] + cst[8 + d] * h
            return cst[d] * g, q * lax.rsqrt(q) * x

        for jt in range(2):
            acc = [jnp.zeros((8, LANES), F32) for _ in range(T)]
            for b in range(7):
                tap = [taps_ref[pl.ds(a * 7 + b, 1), lanes] for a in range(7)]
                tap = [jnp.broadcast_to(t, (8, LANES)) for t in tap]
                for r in range(rows):
                    x = v_ref[ct, pl.ds(r * PW + jt * 8 + b, 8), :]
                    for a in range(7):
                        i = r - a
                        if 0 <= i < T:
                            acc[i] = acc[i] + tap[a] * x
            vals = [x / (1.0 + jnp.exp(-x)) for x in acc]
            for i in range(T):
                val_ref[pl.ds(i * T + jt * 8, 8), :] = vals[i]
            state = jnp.zeros((8, LANES), F32)
            downs = []
            for i in range(T):
                at = pl.ds(i * T + jt * 8, 8)
                d, f = flow(2, g_ref[at, :], h_ref[at, :], vals[i])
                state = d * state + f
                downs.append(state)
            end_ref[1, pl.ds(0 + ct * T + jt * 8, 8), :] = state
            state = jnp.zeros((8, LANES), F32)
            for i in reversed(range(T)):
                at = pl.ds(i * T + jt * 8, 8)
                d, f = flow(3, g_ref[at, :], h_ref[at, :], vals[i])
                state = d * state + f
                sum_ref[ct, at, :] = downs[i] + state
            end_ref[1, pl.ds(64 + ct * T + jt * 8, 8), :] = state
        for it in range(2):
            state = jnp.zeros((8, LANES), F32)
            lefts = []
            for j in range(T):
                at = pl.ds(it * 8 * T + j, 8, stride=T)
                d, f = flow(0, g_ref[at, :], h_ref[at, :], val_ref[at, :])
                state = d * state + f
                lefts.append(state)
            end_ref[0, pl.ds(0 + ct * T + it * 8, 8), :] = state
            state = jnp.zeros((8, LANES), F32)
            for j in reversed(range(T)):
                at = pl.ds(it * 8 * T + j, 8, stride=T)
                d, f = flow(1, g_ref[at, :], h_ref[at, :], val_ref[at, :])
                state = d * state + f
                sum_ref[ct, at, :] = sum_ref[ct, at, :] + (lefts[j] + state)
            end_ref[0, pl.ds(64 + ct * T + it * 8, 8), :] = state
        return carry

    lax.fori_loop(0, groups, group, 0)
    for peer in range(2 * XS):
        near_ref[peer, 0:128] = end_ref[peer // XS].astype(BF16)
        near_ref[peer, 128:144] = tails_ref[peer // XS]


def line_decay(block, at):
    decay = jnp.broadcast_to(block[128:144, at:at + 1], (T, LANES))
    return jnp.concatenate([decay] * 4, axis=0)


def pair_decay(block, at, gap):
    return line_decay(block, at) + line_decay(block, at + gap)


def totals_kernel(place_ref, near_ref, whole_ref, far_ref):
    core, y = place_ref[0] % 2, place_ref[0] // 2
    x, z = place_ref[1] % XS, place_ref[1] // XS
    lane = lax.broadcasted_iota(jnp.int32, (T, LANES), 1)

    def spread(first, second):
        parts = []
        for d in (first, second):
            high = d[:T].astype(BF16).astype(F32)
            parts += [high, d[:T] - high]
        return jnp.where(lane < 32, parts[0], jnp.where(
            lane < 64, parts[1], jnp.where(lane < 96, parts[2], parts[3]))).astype(BF16)

    @pl.when(core == 0)
    def _():
        ahead, back = whole_ref[0], whole_ref[1]
        products = []
        for k in range(2):
            blocks = [near_ref[k * XS + i].astype(F32) for i in range(XS)]
            decays = [pair_decay(b, 0, 64) for b in blocks]
            former, product = blocks[0][:64], decays[0]
            for i in range(1, XS):
                former = ahead * decays[i] * former + blocks[i][:64]
                product = product * decays[i]
            latter = blocks[XS - 1][64:128]
            for i in reversed(range(XS - 1)):
                latter = back * decays[i] * latter + blocks[i][64:128]
            products.append(product)
            former, latter = former.astype(BF16), latter.astype(BF16)
            for peer in range(FAR):
                far_ref[peer, 64 * k:64 * k + 64] = jnp.where(peer > z, former, latter)
        tail = spread(products[0], products[1])
        for peer in range(FAR):
            far_ref[peer, 128:144] = tail

    @pl.when(core == 1)
    def _():
        first, second = near_ref[x].astype(F32), near_ref[XS + x].astype(F32)
        decays = [pair_decay(first, 0, 64), pair_decay(second, 0, 64)]
        former = (whole_ref[2] * decays[1] * first[:64] + second[:64]).astype(BF16)
        latter = (whole_ref[3] * decays[0] * second[64:128] + first[64:128]).astype(BF16)
        product = decays[0] * decays[1]
        tail = spread(product, product)
        for peer in range(FAR):
            far_ref[peer, 0:64] = jnp.where(peer > y, former, latter)
            far_ref[peer, 64:128] = jnp.zeros((64, LANES), BF16)
            far_ref[peer, 128:144] = tail


def enter_kernel(place_ref, near_ref, far_ref, whole_ref, keep_ref, give_ref):
    core, y = place_ref[0] % 2, place_ref[0] // 2
    x, z = place_ref[1] % XS, place_ref[1] // XS

    def far_states(me, k, ahead, back):
        blocks = [far_ref[i].astype(F32) for i in range(FAR)]
        decays = [pair_decay(b, 64 * k, 32) for b in blocks]
        fore = jnp.zeros((64, LANES), F32)
        aft = jnp.zeros((64, LANES), F32)
        for i in range(FAR - 1):
            fore = jnp.where(i < me, ahead * decays[i] * fore + blocks[i][64 * k:64 * k + 64], fore)
        for i in reversed(range(1, FAR)):
            aft = jnp.where(i > me, back * decays[i] * aft + blocks[i][64 * k:64 * k + 64], aft)
        return fore, aft

    @pl.when(core == 0)
    def _():
        ahead, back = whole_ref[0], whole_ref[1]
        ahead_far, back_far = ahead, back
        for _ in range(2):
            ahead_far, back_far = ahead_far * ahead_far, back_far * back_far
        for k in range(2):
            fore, aft = far_states(z, k, ahead_far, back_far)
            blocks = [near_ref[k * XS + i].astype(F32) for i in range(XS)]
            decays = [pair_decay(b, 0, 64) for b in blocks]
            for i in range(XS - 1):
                fore = jnp.where(i < x, ahead * decays[i] * fore + blocks[i][:64], fore)
            for i in reversed(range(1, XS)):
                aft = jnp.where(i > x, back * decays[i] * aft + blocks[i][64:128], aft)
            if k == 0:
                keep_ref[0:64], keep_ref[64:128] = fore, aft
            else:
                give_ref[0:64], give_ref[64:128] = fore.astype(BF16), aft.astype(BF16)

    @pl.when(core == 1)
    def _():
        ahead, back = whole_ref[2], whole_ref[3]
        fore, aft = far_states(y, 0, ahead * ahead, back * back)
        first, second = near_ref[x].astype(F32), near_ref[XS + x].astype(F32)
        give_ref[0:64] = fore.astype(BF16)
        give_ref[64:128] = (back * pair_decay(second, 0, 64) * aft + second[64:128]).astype(BF16)
        keep_ref[0:64] = ahead * pair_decay(first, 0, 64) * fore + first[:64]
        keep_ref[64:128] = aft


def finish_kernel(place_ref, keep_ref, got_ref, cst_ref, px_ref, sum_ref, gate_ref, tok_ref, wo_ref,
                  out_ref, acc_ref, g_ref, enter_ref, gated_ref):
    groups = acc_ref.shape[0]
    px = px_ref[...]
    g_ref[...] = jnp.broadcast_to(px[:, 0:1], (PX, LANES))
    first = place_ref[0] % 2 == 0
    keep, got = keep_ref[...], got_ref[...].astype(F32)
    enter_ref[0:128] = jnp.where(first, keep, got)
    enter_ref[128:256] = jnp.where(first, got, keep)

    def entering(d, ct, half):
        return enter_ref[pl.ds(64 * d + ct * T + half * 8, 8), :]

    def group(ct, carry):
        lanes = pl.ds(pl.multiple_of(ct * LANES, LANES), LANES)
        base = [cst_ref[pl.ds(k, 1), lanes] for k in range(4)]
        for it in range(2):
            left, right = entering(0, ct, it), entering(1, ct, it)
            lefts = []
            for j in range(T):
                left = left * (base[0] * g_ref[pl.ds(it * 8 * T + j, 8, stride=T), :])
                lefts.append(left)
            for j in reversed(range(T)):
                at = pl.ds(it * 8 * T + j, 8, stride=T)
                right = right * (base[1] * g_ref[at, :])
                acc_ref[ct, at, :] = lefts[j] + right
        for jt in range(2):
            down, up = entering(2, ct, jt), entering(3, ct, jt)
            downs = []
            for i in range(T):
                down = down * (base[2] * g_ref[pl.ds(i * T + jt * 8, 8), :])
                downs.append(down)
            for i in reversed(range(T)):
                at = pl.ds(i * T + jt * 8, 8)
                up = up * (base[3] * g_ref[at, :])
                acc_ref[ct, at, :] = acc_ref[ct, at, :] + sum_ref[ct, at, :] + (downs[i] + up)
        gated_ref[:, lanes] = (acc_ref[ct] * gate_ref[:, lanes]).astype(BF16)
        return carry

    lax.fori_loop(0, groups, group, 0)
    mixed = jnp.dot(gated_ref[...], wo_ref[...], preferred_element_type=F32)
    out_ref[...] = (tok_ref[...].astype(F32) + mixed).astype(BF16)


def neighbours(x_first, x_last, axis):
    size = lax.axis_size(axis)
    up = [(i, i + 1) for i in range(size - 1)]
    down = [(i + 1, i) for i in range(size - 1)]
    return lax.ppermute(x_last, axis, up), lax.ppermute(x_first, axis, down)


def tail_block(product):
    high = product.astype(BF16)
    low = (product - high.astype(F32)).astype(BF16)
    lane = lax.broadcasted_iota(jnp.int32, (T, LANES), 1)
    return jnp.where(lane < 64, high[:, None], low[:, None])


def near_groups(rows, cols):
    return [[(2 * y + k) * cols + XS * z + x for k in range(2) for x in range(XS)]
            for y in range(rows // 2) for z in range(cols // XS)]


def far_groups(rows, cols):
    along_z = [[2 * y * cols + XS * z + x for z in range(cols // XS)]
               for y in range(rows // 2) for x in range(XS)]
    along_y = [[(2 * y + 1) * cols + c for y in range(rows // 2)] for c in range(cols)]
    return along_z + along_y


def swap(x, groups):
    return lax.all_to_all(x, ("row", "col"), 0, 0, axis_index_groups=groups, tiled=True)


def body(tokens, input_weight, kernel, direction_decay_table, pixel_extra_decay, output_weight):
    width = output_weight.shape[0]
    groups = width // LANES
    channels = tokens.shape[2]
    rows, cols = lax.axis_size("row"), lax.axis_size("col")
    table, extra = direction_decay_table, pixel_extra_decay
    above, below = neighbours(tokens[:3], tokens[T - 3:], "row")

    def strip(at):
        return jnp.concatenate([above[:, at], tokens[:, at], below[:, at]], axis=0)

    before, after = neighbours(strip(slice(0, 3)), strip(slice(T - 3, T)), "col")
    pad = jnp.concatenate([before, strip(slice(None)), after,
                           jnp.zeros((T + 6, PW - T - 6, channels), BF16)], axis=1)
    pad = pad.reshape((T + 6) * PW, channels)

    cst = jnp.concatenate([jnp.exp(-table), -jnp.expm1(-2.0 * table), jnp.exp(-2.0 * table)], axis=0)
    whole = jnp.exp(-float(T) * table).reshape(4, groups, 1, LANES)
    whole = jnp.broadcast_to(whole, (4, groups, T, LANES)).reshape(4, groups * T, LANES)
    px = jnp.stack([jnp.exp(-extra), -jnp.expm1(-2.0 * extra)], axis=-1).reshape(PX, 2)
    tails = jnp.stack([tail_block(jnp.exp(-jnp.sum(extra, axis=1))),
                       tail_block(jnp.exp(-jnp.sum(extra, axis=0)))])
    place = jnp.stack([lax.axis_index("row"), lax.axis_index("col")]).astype(jnp.int32)
    flat = tokens.reshape(PX, channels)
    gate = jax.nn.silu(jnp.dot(flat, input_weight[:, width:], preferred_element_type=F32))
    pad, gate, whole, place = lax.optimization_barrier((pad, gate, whole, place))

    spec = pl.BlockSpec(memory_space=VMEM)
    smem = pl.BlockSpec(memory_space=pltpu.SMEM)
    params = pltpu.CompilerParams(vmem_limit_bytes=16 * 2**20)
    block = jax.ShapeDtypeStruct((2 * XS, 144, LANES), BF16)
    local, near = pl.pallas_call(
        conv_scan_kernel,
        out_shape=(jax.ShapeDtypeStruct((groups, PX, LANES), F32), block),
        in_specs=[spec] * 6,
        out_specs=(spec, spec),
        scratch_shapes=[VMEM((groups, (T + 6) * PW, LANES), F32), VMEM((PX, LANES), F32),
                        VMEM((PX, LANES), F32), VMEM((PX, LANES), F32), VMEM((2, 128, LANES), F32)],
        compiler_params=params,
        name="conv_scan",
    )(pad, input_weight[:, :width], kernel.reshape(49, width), cst, px, tails)
    near = swap(near, near_groups(rows, cols))

    far = pl.pallas_call(
        totals_kernel,
        out_shape=jax.ShapeDtypeStruct((FAR, 144, LANES), BF16),
        in_specs=[smem, spec, spec],
        out_specs=spec,
        compiler_params=params,
        name="totals",
    )(place, near, whole)
    far = swap(far, far_groups(rows, cols))

    keep, give = pl.pallas_call(
        enter_kernel,
        out_shape=(jax.ShapeDtypeStruct((128, LANES), F32), jax.ShapeDtypeStruct((128, LANES), BF16)),
        in_specs=[smem, spec, spec, spec],
        out_specs=(spec, spec),
        compiler_params=params,
        name="enter",
    )(place, near, far, whole)
    got = lax.ppermute(give, "row", [(i, i ^ 1) for i in range(rows)])

    mixed = pl.pallas_call(
        finish_kernel,
        out_shape=jax.ShapeDtypeStruct((PX, channels), BF16),
        in_specs=[smem] + [spec] * 8,
        out_specs=spec,
        scratch_shapes=[VMEM((groups, PX, LANES), F32), VMEM((PX, LANES), F32),
                        VMEM((256, LANES), F32), VMEM((PX, width), BF16)],
        compiler_params=params,
        name="finish",
    )(place, keep, got, cst, px, local, gate, flat, output_weight)
    return mixed.reshape(T, T, channels)


def solution(mesh):
    return jax.shard_map(
        body,
        mesh=mesh,
        in_specs=(P("row", "col", None), P(), P(), P(), P("row", "col"), P()),
        out_specs=P("row", "col", None),
        check_vma=False,
    )
```

time: 83.5 us -> 64.6 us (0.77)
  waiting for transfers between devices: 32.2 us -> 0.85 us
  blocking collectives: 0 us -> 26.5 us
  starting transfers between devices: 35.3 us -> 24.4 us
  other arithmetic: 3.82 us -> 0.55 us
  Pallas kernels: 8.08 us -> 6.73 us
  matrix products: 0.3 us -> 1.31 us
    all_to_all x2 -> x0, waiting for transfers between devices: 29.1 us -> none  [exchange(): lax.all_to_all(jnp.concatenate([states, tails], axis=1), axis, 0, 0, tile...]
    all_to_all x0 -> x2, blocking collectives: none -> 26.5 us  [swap(): lax.all_to_all(x, ('row', 'col'), 0, 0, axis_index_groups=groups, tiled=T...]
    all_to_all x2 -> x0, starting transfers between devices: 21.9 us -> none  [exchange(): lax.all_to_all(jnp.concatenate([states, tails], axis=1), axis, 0, 0, tile...]
    ppermute x4 -> x5, starting transfers between devices: 13.4 us -> 24.4 us  [the longest x4 16 us: neighbours(): return (lax.ppermute(x_last, axis, up), lax.ppermute(x_first, axis, down))]
    pallas_call x1, Pallas kernels: 4.76 us -> 2.01 us  [body(): pl.pallas_call(finish_kernel, out_shape=jax.ShapeDtypeStruct((PX, channel...]
    ppermute x4 -> x5, waiting for transfers between devices: 3.18 us -> 0.85 us  [the longest x1 0.84 us: body(): got = lax.ppermute(give, 'row', [(i, i ^ 1) for i in range(rows)])]
    concatenate x5 -> x3, other arithmetic: 1.94 us -> 0.22 us  [the longest x1 0.18 us: body(): jnp.concatenate([before, strip(slice(None)), after, jnp.zeros((T + 6, PW...]
    pallas_call x0 -> x2, Pallas kernels: none -> 1.39 us  [the longest x1 0.73 us: body(): pl.pallas_call(enter_kernel, out_shape=(jax.ShapeDtypeStruct((128, LANES)...]
  transfers between devices with their start and end apart: 6 -> 5, of which waited for: 3 -> 1; matrix products, arithmetic and copies ran while one was open for 6% -> 3% of each run, Pallas kernels for 0% -> 0%
where the time goes in v2:
time: 64.6 us; the launch traced here: 64.2 us
  blocking collectives  26.5 us (41%)
  starting transfers between devices  24.4 us (38%)
  Pallas kernels  6.73 us (10%)
  local copies, waits for them, and re-layouts  3.46 us (5%)
  matrix products  1.31 us (2%)
  waiting for transfers between devices  0.85 us (1%)
    all_to_all x2, blocking collectives, swap(): lax.all_to_all(x, ('row', 'col'), 0, 0, axis_index_groups=groups, tiled=T...  26.5 us
    ppermute x4, starting transfers between devices, neighbours(): return (lax.ppermute(x_last, axis, up), lax.ppermute(x_first, axis, down))  16 us
    ppermute x1, starting transfers between devices, body(): got = lax.ppermute(give, 'row', [(i, i ^ 1) for i in range(rows)])  8.44 us
    pallas_call x1, Pallas kernels, body(): pl.pallas_call(conv_scan_kernel, out_shape=(jax.ShapeDtypeStruct((groups,...  3.33 us
    unnamed x16, local copies, waits for them, and re-layouts  2.11 us
    pallas_call x1, Pallas kernels, body(): pl.pallas_call(finish_kernel, out_shape=jax.ShapeDtypeStruct((PX, channel...  2.01 us
    dot_general x1, matrix products, body(): jnp.dot(flat, input_weight[:, width:], preferred_element_type=F32)  1.31 us
  transfers between devices with their start and end apart: 5, of which 1 were waited for; matrix products, arithmetic and copies ran while one was open for 3% of the time, Pallas kernels for 0%

profile of v2, /device:TPU:1, one launch (start us, length us, event | category | flops | bytes accessed | tf_op | source)
XLA Modules:
  0.0 64.2 jit_solution(9838297739719908272)
XLA Ops:
  0.0 0.0 copy-start
  0.0 0.8 %fusion.8 = (bf16[3,16,256]{2,1,0:T(8,128)(2,1)S(1)}, bf16[3,16,256]{2,1,0:T(8,128)(2,1)S(1)}) fusion(bf16[16,16,256]{2,1,0:T(8,128)(2,1)} %param.6), kind=kLoop, calls=%fused_computation.27 | loop fusion | bytes 98304 | tf_op jit(solution)/shard_map/slice | solution.py:278
  0.8 8.8 %collective-permute-start.1 = (bf16[3,16,256]{2,0,1:T(4,128)(2,1)S(1)}, bf16[3,16,256]{2,0,1:T(4,128)(2,1)S(1)}, u32[]{:S(2)}, u32[]{:S(2)}) collective-permute-start(bf16[3,16,256]{2,0,1:T(4,128)(2,1)S(1)} %copy.21), channel_id=1, source_target_pairs={{32,0},{64,32},{96,64},{128,96},{160,128},{192,160},{224,192},{256... | collective-permute-start | bytes 73736 | tf_op jit(solution)/shard_map/ppermute | solution.py:246
  9.7 1.9 %collective-permute-start = (bf16[3,16,256]{2,0,1:T(4,128)(2,1)S(1)}, bf16[3,16,256]{2,0,1:T(4,128)(2,1)S(1)}, u32[]{:S(2)}, u32[]{:S(2)}) collective-permute-start(bf16[3,16,256]{2,0,1:T(4,128)(2,1)S(1)} %copy.19), channel_id=1, source_target_pairs={{0,32},{32,64},{64,96},{96,128},{128,160},{160,192},{192,224},{224... | collective-permute-start | bytes 73736 | tf_op jit(solution)/shard_map/ppermute | solution.py:246
  11.6 0.0 copy-done
  11.6 0.0 copy-start.4
  11.7 0.7 %copy-done.4 = f32[16,16]{1,0:T(8,128)S(1)} copy-done((f32[16,16]{1,0:T(8,128)S(1)}, f32[16,16]{1,0:T(8,128)}, u32[]{:S(2)}) %copy-start.4) | copy-done | bytes 1048
  12.3 0.1 fusion.6
  12.4 0.0 copy-start.5
  12.4 0.1 stack.26
  12.5 0.1 stack.27
  12.6 0.5 copy-done.5
  13.2 0.1 broadcast_select_fusion.1
  13.3 0.0 copy-start.2
  13.3 1.3 %divide_multiply_fusion.gate_ref = f32[256,512]{1,0:T(8,128)S(1)} fusion(bf16[256,256]{1,0:T(8,128)(2,1)S(1)} %bitcast.9, bf16[256,1024]{1,0:T(8,128)(2,1)} %param.7), kind=kOutput, calls=%fused_computation | convolution fusion | flops 67633152 | bytes 917504 | tf_op jit(solution)/shard_map/dot_general | solution.py:296
  14.6 0.0 collective-permute-done.1
  14.7 0.0 collective-permute-done
  14.7 1.3 %collective-permute-start.3 = (bf16[22,3,256]{2,0,1:T(8,128)(2,1)S(1)}, bf16[22,3,256]{2,0,1:T(8,128)(2,1)S(1)}, u32[]{:S(2)}, u32[]{:S(2)}) collective-permute-start(bf16[22,3,256]{2,0,1:T(8,128)(2,1)S(1)} %pad_maximum_fusion.1), channel_id=1, source_target_pairs={{1,0},{2,1},{3,2},{4,3},{5,4},{6,5},{7,6},{8,7},{9,8},{10,9},{11,1... | collective-permute-start | bytes 101384 | tf_op jit(solution)/shard_map/ppermute | solution.py:246
  16.1 4.0 %collective-permute-start.2 = (bf16[22,3,256]{2,0,1:T(8,128)(2,1)S(1)}, bf16[22,3,256]{2,0,1:T(8,128)(2,1)S(1)}, u32[]{:S(2)}, u32[]{:S(2)}) collective-permute-start(bf16[22,3,256]{2,0,1:T(8,128)(2,1)S(1)} %pad_maximum_fusion), channel_id=1, source_target_pairs={{0,1},{1,2},{2,3},{3,4},{4,5},{5,6},{6,7},{7,8},{8,9},{9,10},{10,1... | collective-permute-start | bytes 101384 | tf_op jit(solution)/shard_map/ppermute | solution.py:246
  20.1 0.1 pad_add_fusion.place_ref
  20.1 0.0 copy-done.2
  20.1 0.0 copy-start.3
  20.2 0.9 %copy-done.3 = f32[7,7,512]{2,1,0:T(8,128)S(1)} copy-done((f32[7,7,512]{2,1,0:T(8,128)S(1)}, f32[7,7,512]{2,1,0:T(8,128)}, u32[]{:S(2)}) %copy-start.3) | copy-done | bytes 100376
  21.1 0.1 copy.17.px_ref
  21.2 0.1 pad.14.clone
  21.3 0.0 collective-permute-done.3
  21.3 0.0 collective-permute-done.2
  21.4 0.2 maximum_maximum_fusion
  21.6 3.3 %conv_scan.1 = (f32[4,256,128]{2,1,0:T(8,128)S(1)}, bf16[8,144,128]{2,1,0:T(8,128)(2,1)S(1)}) custom-call(bf16[528,256]{1,0:T(8,128)(2,1)S(1)} %bitcast.11, bf16[256,512]{1,0:T(8,128)(2,1)S(1)} %slice.39.wv_ref, f32[49,512]{1,0:T(8,128)S(1)} %reshape.167.taps_ref, f32[12,512]{1,0:T(8,128)S(1)} %pad_maximum_fusion.2.cst_ref, f32[256,2]{1,0:T(8,128)S(1)} %copy.17.px_ref, ...), custom_call_target="tpu_custom_call" | custom-call | tf_op jit(solution)/shard_map/conv_scan/pallas_call | solution.py:303
  24.9 12.2 %all_to_all.10.near_ref = bf16[8,144,128]{2,1,0:T(8,128)(2,1)S(1)} all-to-all(bf16[8,144,128]{2,1,0:T(8,128)(2,1)S(1)} %get-tuple-element.15), channel_id=1, replica_groups={{0,1,2,3,32,33,34,35},{4,5,6,7,36,37,38,39},{8,9,10,11,40,41,42,43},{12..., dimensions={0} | all-to-all | bytes 589824 | tf_op jit(solution)/shard_map/all_to_all | solution.py:269
  37.1 0.7 %totals.1 = bf16[8,144,128]{2,1,0:T(8,128)(2,1)S(1)} custom-call(s32[2]{0:T(128)S(1)} %pad_add_fusion.place_ref, bf16[8,144,128]{2,1,0:T(8,128)(2,1)S(1)} %all_to_all.10.near_ref, f32[4,64,128]{2,1,0:T(8,128)S(1)} %bitcast.7), custom_call_target="tpu_custom_call" | custom-call | tf_op jit(solution)/shard_map/totals/pallas_call | solution.py:315
  37.8 14.3 %all_to_all.11.far_ref = bf16[8,144,128]{2,1,0:T(8,128)(2,1)S(1)} all-to-all(bf16[8,144,128]{2,1,0:T(8,128)(2,1)S(1)} %totals.1), channel_id=1, replica_groups={{0,4,8,12,16,20,24,28},{1,5,9,13,17,21,25,29},{2,6,10,14,18,22,26,30},{..., dimensions={0} | all-to-all | bytes 589824 | tf_op jit(solution)/shard_map/all_to_all | solution.py:269
  52.1 0.0 copy-start.1
  52.1 0.7 %enter.1 = (f32[128,128]{1,0:T(8,128)S(1)}, bf16[128,128]{1,0:T(8,128)(2,1)S(1)}) custom-call(s32[2]{0:T(128)S(1)} %pad_add_fusion.place_ref, bf16[8,144,128]{2,1,0:T(8,128)(2,1)S(1)} %all_to_all.10.near_ref, bf16[8,144,128]{2,1,0:T(8,128)(2,1)S(1)} %all_to_all.11.far_ref, f32[4,64,128]{2,1,0:T(8,128)S(1)} %bitcast.8), custom_call_target="tpu_custom_call" | custom-call | tf_op jit(solution)/shard_map/enter/pallas_call | solution.py:325
  52.9 8.4 %collective-permute-start.4 = (bf16[128,128]{1,0:T(8,128)(2,1)S(1)}, bf16[128,128]{1,0:T(8,128)(2,1)S(1)}, u32[]{:S(2)}, u32[]{:S(2)}) collective-permute-start(bf16[128,128]{1,0:T(8,128)(2,1)S(1)} %get-tuple-element.18), channel_id=1, source_target_pairs={{0,32},{32,0},{64,96},{96,64},{128,160},{160,128},{192,224},{224,1... | collective-permute-start | bytes 98312 | tf_op jit(solution)/shard_map/ppermute | solution.py:333
  61.3 0.8 %collective-permute-done.4.got_ref = bf16[128,128]{1,0:T(8,128)(2,1)S(1)} collective-permute-done((bf16[128,128]{1,0:T(8,128)(2,1)S(1)}, bf16[128,128]{1,0:T(8,128)(2,1)S(1)}, u32[]{:S(2)}, u32[]{:S(2)}) %collective-permute-start.4) | collective-permute-done | bytes 32800 | tf_op jit(solution)/shard_map/ppermute | solution.py:333
  62.2 0.0 copy-done.1
  62.2 2.0 %finish.1 = bf16[256,256]{1,0:T(8,128)(2,1)} custom-call(s32[2]{0:T(128)S(1)} %pad_add_fusion.place_ref, f32[128,128]{1,0:T(8,128)S(1)} %get-tuple-element.17.keep_ref, bf16[128,128]{1,0:T(8,128)(2,1)S(1)} %collective-permute-done.4.got_ref, f32[12,512]{1,0:T(8,128)S(1)} %pad_maximum_fusion.2.cst_ref, f32[256,2]{1,0:T(8,128)S(1)} %copy.17.px_ref, ...), custom_call_target="tpu_custom_call" | custom-call | tf_op jit(solution)/shard_map/finish/pallas_call | solution.py:335
  (24 shorter events, 0.3 us)
Async XLA Ops:
  0.0 11.6 %copy-start = (bf16[16,16,256]{2,1,0:T(8,128)(2,1)S(1)}, bf16[16,16,256]{2,1,0:T(8,128)(2,1)}, u32[]{:S(2)}) copy-start(bf16[16,16,256]{2,1,0:T(8,128)(2,1)} %param.6) | copy-start | bytes 393220
  0.8 13.8 %collective-permute-start.1 = (bf16[3,16,256]{2,0,1:T(4,128)(2,1)S(1)}, bf16[3,16,256]{2,0,1:T(4,128)(2,1)S(1)}, u32[]{:S(2)}, u32[]{:S(2)}) collective-permute-start(bf16[3,16,256]{2,0,1:T(4,128)(2,1)S(1)} %copy.21), channel_id=1, source_target_pairs={{32,0},{64,32},{96,64},{128,96},{160,128},{192,160},{224,192},{256... | collective-permute-start | bytes 73736 | tf_op jit(solution)/shard_map/ppermute | solution.py:246
  9.7 5.0 %collective-permute-start = (bf16[3,16,256]{2,0,1:T(4,128)(2,1)S(1)}, bf16[3,16,256]{2,0,1:T(4,128)(2,1)S(1)}, u32[]{:S(2)}, u32[]{:S(2)}) collective-permute-start(bf16[3,16,256]{2,0,1:T(4,128)(2,1)S(1)} %copy.19), channel_id=1, source_target_pairs={{0,32},{32,64},{64,96},{96,128},{128,160},{160,192},{192,224},{224... | collective-permute-start | bytes 73736 | tf_op jit(solution)/shard_map/ppermute | solution.py:246
  11.6 0.7 %copy-start.4 = (f32[16,16]{1,0:T(8,128)S(1)}, f32[16,16]{1,0:T(8,128)}, u32[]{:S(2)}) copy-start(f32[16,16]{1,0:T(8,128)} %param.10) | copy-start | bytes 3076
  12.4 0.7 %copy-start.5 = (f32[4,512]{1,0:T(4,128)S(1)}, f32[4,512]{1,0:T(4,128)}, u32[]{:S(2)}) copy-start(f32[4,512]{1,0:T(4,128)} %param.9) | copy-start | bytes 24580
  13.3 6.9 %copy-start.2 = (bf16[256,1024]{1,0:T(8,128)(2,1)S(1)}, bf16[256,1024]{1,0:T(8,128)(2,1)}, u32[]{:S(2)}) copy-start(bf16[256,1024]{1,0:T(8,128)(2,1)} %param.7) | copy-start | bytes 1572868
  14.7 6.6 %collective-permute-start.3 = (bf16[22,3,256]{2,0,1:T(8,128)(2,1)S(1)}, bf16[22,3,256]{2,0,1:T(8,128)(2,1)S(1)}, u32[]{:S(2)}, u32[]{:S(2)}) collective-permute-start(bf16[22,3,256]{2,0,1:T(8,128)(2,1)S(1)} %pad_maximum_fusion.1), channel_id=1, source_target_pairs={{1,0},{2,1},{3,2},{4,3},{5,4},{6,5},{7,6},{8,7},{9,8},{10,9},{11,1... | collective-permute-start | bytes 101384 | tf_op jit(solution)/shard_map/ppermute | solution.py:246
  16.1 5.3 %collective-permute-start.2 = (bf16[22,3,256]{2,0,1:T(8,128)(2,1)S(1)}, bf16[22,3,256]{2,0,1:T(8,128)(2,1)S(1)}, u32[]{:S(2)}, u32[]{:S(2)}) collective-permute-start(bf16[22,3,256]{2,0,1:T(8,128)(2,1)S(1)} %pad_maximum_fusion), channel_id=1, source_target_pairs={{0,1},{1,2},{2,3},{3,4},{4,5},{5,6},{6,7},{7,8},{8,9},{9,10},{10,1... | collective-permute-start | bytes 101384 | tf_op jit(solution)/shard_map/ppermute | solution.py:246
  20.1 0.9 %copy-start.3 = (f32[7,7,512]{2,1,0:T(8,128)S(1)}, f32[7,7,512]{2,1,0:T(8,128)}, u32[]{:S(2)}) copy-start(f32[7,7,512]{2,1,0:T(8,128)} %param.8) | copy-start | bytes 301060
  52.1 10.0 %copy-start.1 = (bf16[512,256]{1,0:T(8,128)(2,1)S(1)}, bf16[512,256]{1,0:T(8,128)(2,1)}, u32[]{:S(2)}) copy-start(bf16[512,256]{1,0:T(8,128)(2,1)} %wo_ref.1) | copy-start | bytes 786436
  52.9 9.3 %collective-permute-start.4 = (bf16[128,128]{1,0:T(8,128)(2,1)S(1)}, bf16[128,128]{1,0:T(8,128)(2,1)S(1)}, u32[]{:S(2)}, u32[]{:S(2)}) collective-permute-start(bf16[128,128]{1,0:T(8,128)(2,1)S(1)} %get-tuple-element.18), channel_id=1, source_target_pairs={{0,32},{32,0},{64,96},{96,64},{128,160},{160,128},{192,224},{224,1... | collective-permute-start | bytes 98312 | tf_op jit(solution)/shard_map/ppermute | solution.py:333

commit v3 on v2

--- a/solution.py
+++ b/solution.py
@@ -16,17 +16,60 @@
 VMEM = pltpu.VMEM
 
 
-def conv_scan_kernel(pad_ref, wv_ref, taps_ref, cst_ref, px_ref, tails_ref,
-                     sum_ref, near_ref,
-                     v_ref, g_ref, h_ref, val_ref, end_ref):
+def project(x, wv_ref, store):
+    for half in range(wv_ref.shape[1] // 256):
+        p = jnp.dot(x, wv_ref[:, half * 256:(half + 1) * 256], preferred_element_type=F32)
+        p = p.astype(BF16).astype(F32)
+        store(2 * half, p[:, :LANES])
+        store(2 * half + 1, p[:, LANES:])
+
+
+def add_taps(acc, v_ref, taps_ref, ct, lanes, jt, shifts):
+    for b in shifts:
+        tap = [taps_ref[pl.ds(a * 7 + b, 1), lanes] for a in range(7)]
+        tap = [jnp.broadcast_to(t, (8, LANES)) for t in tap]
+        for r in range(T + 6):
+            x = v_ref[ct, pl.ds(r * PW + jt * 8 + b, 8), :]
+            for a in range(7):
+                i = r - a
+                if 0 <= i < T:
+                    acc[i] = tap[a] * x if acc[i] is None else acc[i] + tap[a] * x
+    return acc
+
+
+def inner_kernel(above_ref, tok_ref, below_ref, wv_ref, taps_ref, v_ref, acc_ref):
     groups = v_ref.shape[0]
-    rows = T + 6
-    pad = pad_ref[...]
-    for half in range(groups // 2):
-        p = jnp.dot(pad, wv_ref[:, half * 256:(half + 1) * 256], preferred_element_type=F32)
-        p = p.astype(BF16).astype(F32)
-        v_ref[2 * half] = p[:, :LANES]
-        v_ref[2 * half + 1] = p[:, LANES:]
+    for ref, first in ((above_ref, 0), (tok_ref, 3), (below_ref, T + 3)):
+        count = ref.shape[0] // T
+
+        def store(ct, p, first=first, count=count):
+            for i in range(count):
+                v_ref[ct, pl.ds((first + i) * PW + 3, T), :] = p[i * T:(i + 1) * T]
+
+        project(ref[...], wv_ref, store)
+
+    def group(ct, carry):
+        lanes = pl.ds(pl.multiple_of(ct * LANES, LANES), LANES)
+        for jt in range(2):
+            acc = add_taps([None] * T, v_ref, taps_ref, ct, lanes, jt, range(3, 7) if jt == 0 else range(4))
+            for i in range(T):
+                acc_ref[ct, pl.ds(i * T + jt * 8, 8), :] = acc[i]
+        return carry
+
+    lax.fori_loop(0, groups, group, 0)
+
+
+def conv_scan_kernel(before_ref, after_ref, wv_ref, taps_ref, cst_ref, px_ref, tails_ref, own_ref, acc_ref,
+                     v_ref, sum_ref, near_ref, g_ref, h_ref, val_ref, end_ref):
+    del own_ref
+    groups = v_ref.shape[0]
+    for ref, first in ((before_ref, 0), (after_ref, T + 3)):
+
+        def store(ct, p, first=first):
+            for j in range(3):
+                v_ref[ct, pl.ds(first + j, PW, stride=PW), :] = p[j * PW:(j + 1) * PW]
+
+        project(ref[...], wv_ref, store)
     px = px_ref[...]
     g_ref[...] = jnp.broadcast_to(px[:, 0:1], (PX, LANES))
     h_ref[...] = jnp.broadcast_to(px[:, 1:2], (PX, LANES))
@@ -40,16 +83,8 @@
             return cst[d] * g, q * lax.rsqrt(q) * x
 
         for jt in range(2):
-            acc = [jnp.zeros((8, LANES), F32) for _ in range(T)]
-            for b in range(7):
-                tap = [taps_ref[pl.ds(a * 7 + b, 1), lanes] for a in range(7)]
-                tap = [jnp.broadcast_to(t, (8, LANES)) for t in tap]
-                for r in range(rows):
-                    x = v_ref[ct, pl.ds(r * PW + jt * 8 + b, 8), :]
-                    for a in range(7):
-                        i = r - a
-                        if 0 <= i < T:
-                            acc[i] = acc[i] + tap[a] * x
+            acc = [acc_ref[ct, pl.ds(i * T + jt * 8, 8), :] for i in range(T)]
+            acc = add_taps(acc, v_ref, taps_ref, ct, lanes, jt, range(3) if jt == 0 else range(4, 7))
             vals = [x / (1.0 + jnp.exp(-x)) for x in acc]
             for i in range(T):
                 val_ref[pl.ds(i * T + jt * 8, 8), :] = vals[i]
@@ -195,46 +230,66 @@
         keep_ref[64:128] = aft
 
 
-def finish_kernel(place_ref, keep_ref, got_ref, cst_ref, px_ref, sum_ref, gate_ref, tok_ref, wo_ref,
+def decay_rows(kind, first, cst_ref, g_ref, store):
+    def group(ct, carry):
+        lanes = pl.ds(pl.multiple_of(ct * LANES, LANES), LANES)
+        ahead, back = cst_ref[pl.ds(2 * kind, 1), lanes], cst_ref[pl.ds(2 * kind + 1, 1), lanes]
+        for half in range(2):
+            fore = first(0, ct, half)
+            aft = first(1, ct, half)
+
+            def at(n):
+                return pl.ds(half * 8 * T + n, 8, stride=T) if kind == 0 else pl.ds(n * T + half * 8, 8)
+
+            fores = []
+            for n in range(T):
+                fore = fore * (ahead * g_ref[at(n), :])
+                fores.append(fore)
+            for n in reversed(range(T)):
+                aft = aft * (back * g_ref[at(n), :])
+                store(ct, at(n), fores[n] + aft)
+        return carry
+
+    lax.fori_loop(0, 4, group, 0)
+
+
+def own_axis_kernel(place_ref, keep_ref, cst_ref, px_ref, sum_ref, acc_ref, g_ref):
+    px = px_ref[...]
+    g_ref[...] = jnp.broadcast_to(px[:, 0:1], (PX, LANES))
+
+    def first(side, ct, half):
+        return keep_ref[pl.ds(64 * side + ct * T + half * 8, 8), :]
+
+    def store(ct, at, x):
+        acc_ref[ct, at, :] = sum_ref[ct, at, :] + x
+
+    for kind in range(2):
+        @pl.when(place_ref[0] % 2 == kind)
+        def _():
+            decay_rows(kind, first, cst_ref, g_ref, store)
+
+
+def finish_kernel(place_ref, got_ref, cst_ref, px_ref, sum_ref, gate_ref, tok_ref, wo_ref,
                   out_ref, acc_ref, g_ref, enter_ref, gated_ref):
     groups = acc_ref.shape[0]
     px = px_ref[...]
     g_ref[...] = jnp.broadcast_to(px[:, 0:1], (PX, LANES))
-    first = place_ref[0] % 2 == 0
-    keep, got = keep_ref[...], got_ref[...].astype(F32)
-    enter_ref[0:128] = jnp.where(first, keep, got)
-    enter_ref[128:256] = jnp.where(first, got, keep)
-
-    def entering(d, ct, half):
-        return enter_ref[pl.ds(64 * d + ct * T + half * 8, 8), :]
-
-    def group(ct, carry):
-        lanes = pl.ds(pl.multiple_of(ct * LANES, LANES), LANES)
-        base = [cst_ref[pl.ds(k, 1), lanes] for k in range(4)]
-        for it in range(2):
-            left, right = entering(0, ct, it), entering(1, ct, it)
-            lefts = []
-            for j in range(T):
-                left = left * (base[0] * g_ref[pl.ds(it * 8 * T + j, 8, stride=T), :])
-                lefts.append(left)
-            for j in reversed(range(T)):
-                at = pl.ds(it * 8 * T + j, 8, stride=T)
-                right = right * (base[1] * g_ref[at, :])
-                acc_ref[ct, at, :] = lefts[j] + right
-        for jt in range(2):
-            down, up = entering(2, ct, jt), entering(3, ct, jt)
-            downs = []
-            for i in range(T):
-                down = down * (base[2] * g_ref[pl.ds(i * T + jt * 8, 8), :])
-                downs.append(down)
-            for i in reversed(range(T)):
-                at = pl.ds(i * T + jt * 8, 8)
-                up = up * (base[3] * g_ref[at, :])
-                acc_ref[ct, at, :] = acc_ref[ct, at, :] + sum_ref[ct, at, :] + (downs[i] + up)
+    enter_ref[...] = got_ref[...].astype(F32)
+
+    def first(side, ct, half):
+        return enter_ref[pl.ds(64 * side + ct * T + half * 8, 8), :]
+
+    def store(ct, at, x):
+        acc_ref[ct, at, :] = sum_ref[ct, at, :] + x
+
+    for kind in range(2):
+        @pl.when(place_ref[0] % 2 != kind)
+        def _():
+            decay_rows(kind, first, cst_ref, g_ref, store)
+
+    for ct in range(groups):
+        lanes = slice(ct * LANES, (ct + 1) * LANES)
         gated_ref[:, lanes] = (acc_ref[ct] * gate_ref[:, lanes]).astype(BF16)
-        return carry
-
-    lax.fori_loop(0, groups, group, 0)
     mixed = jnp.dot(gated_ref[...], wo_ref[...], preferred_element_type=F32)
     out_ref[...] = (tok_ref[...].astype(F32) + mixed).astype(BF16)
 
@@ -278,12 +333,11 @@
     above, below = neighbours(tokens[:3], tokens[T - 3:], "row")
 
     def strip(at):
-        return jnp.concatenate([above[:, at], tokens[:, at], below[:, at]], axis=0)
+        x = jnp.concatenate([above[:, at], tokens[:, at], below[:, at],
+                             jnp.zeros((PW - T - 6, 3, channels), BF16)], axis=0)
+        return x.transpose(1, 0, 2).reshape(3 * PW, channels)
 
     before, after = neighbours(strip(slice(0, 3)), strip(slice(T - 3, T)), "col")
-    pad = jnp.concatenate([before, strip(slice(None)), after,
-                           jnp.zeros((T + 6, PW - T - 6, channels), BF16)], axis=1)
-    pad = pad.reshape((T + 6) * PW, channels)
 
     cst = jnp.concatenate([jnp.exp(-table), -jnp.expm1(-2.0 * table), jnp.exp(-2.0 * table)], axis=0)
     whole = jnp.exp(-float(T) * table).reshape(4, groups, 1, LANES)
@@ -294,22 +348,34 @@
     place = jnp.stack([lax.axis_index("row"), lax.axis_index("col")]).astype(jnp.int32)
     flat = tokens.reshape(PX, channels)
     gate = jax.nn.silu(jnp.dot(flat, input_weight[:, width:], preferred_element_type=F32))
-    pad, gate, whole, place = lax.optimization_barrier((pad, gate, whole, place))
+    before, gate, whole, place = lax.optimization_barrier((before, gate, whole, place))
+    values_weight, taps = input_weight[:, :width], kernel.reshape(49, width)
 
     spec = pl.BlockSpec(memory_space=VMEM)
     smem = pl.BlockSpec(memory_space=pltpu.SMEM)
     params = pltpu.CompilerParams(vmem_limit_bytes=16 * 2**20)
-    block = jax.ShapeDtypeStruct((2 * XS, 144, LANES), BF16)
-    local, near = pl.pallas_call(
+    tile = jax.ShapeDtypeStruct((groups, PX, LANES), F32)
+    padded = jax.ShapeDtypeStruct((groups, PW * PW, LANES), F32)
+    own, partial = pl.pallas_call(
+        inner_kernel,
+        out_shape=(padded, tile),
+        in_specs=[spec] * 5,
+        out_specs=(spec, spec),
+        compiler_params=params,
+        cost_estimate=pl.CostEstimate(flops=2 * 352 * channels * width, bytes_accessed=4 * 2**20, transcendentals=0),
+        name="inner",
+    )(above.reshape(3 * T, channels), flat, below.reshape(3 * T, channels), values_weight, taps)
+    _, local, near = pl.pallas_call(
         conv_scan_kernel,
-        out_shape=(jax.ShapeDtypeStruct((groups, PX, LANES), F32), block),
-        in_specs=[spec] * 6,
-        out_specs=(spec, spec),
-        scratch_shapes=[VMEM((groups, (T + 6) * PW, LANES), F32), VMEM((PX, LANES), F32),
-                        VMEM((PX, LANES), F32), VMEM((PX, LANES), F32), VMEM((2, 128, LANES), F32)],
+        out_shape=(padded, tile, jax.ShapeDtypeStruct((2 * XS, 144, LANES), BF16)),
+        in_specs=[spec] * 9,
+        out_specs=(spec, spec, spec),
+        scratch_shapes=[VMEM((PX, LANES), F32), VMEM((PX, LANES), F32), VMEM((PX, LANES), F32),
+                        VMEM((2, 128, LANES), F32)],
+        input_output_aliases={7: 0},
         compiler_params=params,
         name="conv_scan",
-    )(pad, input_weight[:, :width], kernel.reshape(49, width), cst, px, tails)
+    )(before, after, values_weight, taps, cst, px, tails, own, partial)
     near = swap(near, near_groups(rows, cols))
 
     far = pl.pallas_call(
@@ -332,16 +398,26 @@
     )(place, near, far, whole)
     got = lax.ppermute(give, "row", [(i, i ^ 1) for i in range(rows)])
 
+    acc = pl.pallas_call(
+        own_axis_kernel,
+        out_shape=tile,
+        in_specs=[smem] + [spec] * 4,
+        out_specs=spec,
+        scratch_shapes=[VMEM((PX, LANES), F32)],
+        compiler_params=params,
+        cost_estimate=pl.CostEstimate(flops=6 * PX * width, bytes_accessed=2 * 2**20, transcendentals=0),
+        name="own_axis",
+    )(place, keep, cst, px, local)
     mixed = pl.pallas_call(
         finish_kernel,
         out_shape=jax.ShapeDtypeStruct((PX, channels), BF16),
-        in_specs=[smem] + [spec] * 8,
+        in_specs=[smem] + [spec] * 7,
         out_specs=spec,
         scratch_shapes=[VMEM((groups, PX, LANES), F32), VMEM((PX, LANES), F32),
-                        VMEM((256, LANES), F32), VMEM((PX, width), BF16)],
+                        VMEM((128, LANES), F32), VMEM((PX, width), BF16)],
         compiler_params=params,
         name="finish",
-    )(place, keep, got, cst, px, local, gate, flat, output_weight)
+    )(place, got, cst, px, acc, gate, flat, output_weight)
     return mixed.reshape(T, T, channels)
 
 

time: 64.6 us -> 64.9 us (level)
  starting transfers between devices: 24.4 us -> 20 us
  blocking collectives: 26.5 us -> 29.1 us
  other arithmetic: 0.55 us -> 1.82 us
  local copies, waits for them, and re-layouts: 3.46 us -> 2.2 us
  Pallas kernels: 6.73 us -> 7.85 us
  waiting for transfers between devices: 0.85 us -> 1.77 us
    ppermute x4, starting transfers between devices: 16 us -> 13.3 us  [neighbours(): return (lax.ppermute(x_last, axis, up), lax.ppermute(x_first, axis, down))]
    all_to_all x2, blocking collectives: 26.5 us -> 29.1 us  [swap(): lax.all_to_all(x, ('row', 'col'), 0, 0, axis_index_groups=groups, tiled=T...]
    unnamed x16 -> x12, local copies, waits for them, and re-layouts: 2.11 us -> 0.08 us
    ppermute x1, starting transfers between devices: 8.44 us -> 6.67 us  [body(): got = lax.ppermute(give, 'row', [(i, i ^ 1) for i in range(rows)])]
    ppermute x4, waiting for transfers between devices: 0.01 us -> 1.72 us  [neighbours(): return (lax.ppermute(x_last, axis, up), lax.ppermute(x_first, axis, down))]
    pallas_call x1 -> x3, Pallas kernels: 3.33 us -> 4.44 us  [the longest x1 2.33 us: body(): pl.pallas_call(conv_scan_kernel, out_shape=(padded, tile, jax.ShapeDtypeS...]
    slice x4, local copies, waits for them, and re-layouts: 0.06 us -> 0.94 us  [the longest x1 0.9 us: strip(): tokens[:, at]]
    ppermute x1, waiting for transfers between devices: 0.84 us -> 0.05 us  [body(): got = lax.ppermute(give, 'row', [(i, i ^ 1) for i in range(rows)])]
  transfers between devices with their start and end apart: 5 -> 5, of which waited for: 1 -> 1; matrix products, arithmetic and copies ran while one was open for 3% -> 7% of each run, Pallas kernels for 0% -> 3%
where the time goes in v3:
time: 64.9 us; the launch traced here: 64.4 us
  blocking collectives  29.1 us (45%)
  starting transfers between devices  20 us (31%)
  Pallas kernels  7.85 us (12%)
  local copies, waits for them, and re-layouts  2.2 us (3%)
  other arithmetic  1.82 us (3%)
  waiting for transfers between devices  1.77 us (3%)
  matrix products  1.38 us (2%)
    all_to_all x2, blocking collectives, swap(): lax.all_to_all(x, ('row', 'col'), 0, 0, axis_index_groups=groups, tiled=T...  29.1 us
    ppermute x4, starting transfers between devices, neighbours(): return (lax.ppermute(x_last, axis, up), lax.ppermute(x_first, axis, down))  13.3 us
    ppermute x1, starting transfers between devices, body(): got = lax.ppermute(give, 'row', [(i, i ^ 1) for i in range(rows)])  6.67 us
    pallas_call x1, Pallas kernels, body(): pl.pallas_call(conv_scan_kernel, out_shape=(padded, tile, jax.ShapeDtypeS...  2.33 us
    pallas_call x1, Pallas kernels, body(): pl.pallas_call(finish_kernel, out_shape=jax.ShapeDtypeStruct((PX, channel...  2.02 us
    ppermute x4, waiting for transfers between devices, neighbours(): return (lax.ppermute(x_last, axis, up), lax.ppermute(x_first, axis, down))  1.72 us
    dot_general x1, matrix products, body(): jnp.dot(flat, input_weight[:, width:], preferred_element_type=F32)  1.38 us
    pallas_call x1, Pallas kernels, body(): pl.pallas_call(inner_kernel, out_shape=(padded, tile), in_specs=[spec] *...  1.32 us
  transfers between devices with their start and end apart: 5, of which 1 were waited for; matrix products, arithmetic and copies ran while one was open for 7% of the time, Pallas kernels for 3%

profile of v3, /device:TPU:1, one launch (start us, length us, event | category | flops | bytes accessed | tf_op | source)
XLA Modules:
  0.0 64.4 jit_solution(10613810309991379648)
XLA Ops:
  0.0 0.8 %fusion.8 = (bf16[3,16,256]{2,1,0:T(8,128)(2,1)S(1)}, bf16[3,16,256]{2,1,0:T(8,128)(2,1)S(1)}) fusion(bf16[16,16,256]{2,1,0:T(8,128)(2,1)} %param.6), kind=kLoop, calls=%fused_computation.26 | loop fusion | bytes 98304 | tf_op jit(solution)/shard_map/slice | solution.py:333
  0.8 8.8 %collective-permute-start.1 = (bf16[3,16,256]{2,0,1:T(4,128)(2,1)S(1)}, bf16[3,16,256]{2,0,1:T(4,128)(2,1)S(1)}, u32[]{:S(2)}, u32[]{:S(2)}) collective-permute-start(bf16[3,16,256]{2,0,1:T(4,128)(2,1)S(1)} %copy.25), channel_id=1, source_target_pairs={{32,0},{64,32},{96,64},{128,96},{160,128},{192,160},{224,192},{256... | collective-permute-start | bytes 73736 | tf_op jit(solution)/shard_map/ppermute | solution.py:301
  9.6 1.9 %collective-permute-start = (bf16[3,16,256]{2,0,1:T(4,128)(2,1)S(1)}, bf16[3,16,256]{2,0,1:T(4,128)(2,1)S(1)}, u32[]{:S(2)}, u32[]{:S(2)}) collective-permute-start(bf16[3,16,256]{2,0,1:T(4,128)(2,1)S(1)} %copy.23), channel_id=1, source_target_pairs={{0,32},{32,64},{64,96},{96,128},{128,160},{160,192},{192,224},{224... | collective-permute-start | bytes 73736 | tf_op jit(solution)/shard_map/ppermute | solution.py:301
  11.5 0.9 %fusion.7 = (bf16[16,3,256]{2,1,0:T(4,128)(2,1)S(1)}, bf16[16,3,256]{2,1,0:T(4,128)(2,1)S(1)}) fusion(bf16[16,16,256]{2,1,0:T(8,128)(2,1)} %param.6), kind=kLoop, calls=%fused_computation.25 | loop fusion | bytes 98304 | tf_op jit(solution)/shard_map/slice | solution.py:336
  12.4 0.8 %fusion.6 = (f32[16]{0:T(128)S(1)}, f32[16]{0:T(128)S(1)}, f32[16,16]{1,0:T(8,128)S(1)}, f32[16,16]{1,0:T(8,128)S(1)}) fusion(f32[16,16]{1,0:T(8,128)} %param.10), kind=kLoop, calls=%fused_computation.24 | loop fusion | flops 1248 | bytes 3200 | tf_op jit(solution)/shard_map/reduce_sum | solution.py:346
  13.3 0.1 stack.26
  13.4 0.1 stack.27
  13.4 0.7 %negate_exponential_fusion.1 = (f32[4,512]{1,0:T(4,128)S(1)}, f32[4,512]{1,0:T(4,128)S(1)}, f32[4,512]{1,0:T(4,128)S(1)}, f32[4,512]{1,0:T(4,128)S(1)}) fusion(f32[4,512]{1,0:T(4,128)} %param.9), kind=kLoop, calls=%fused_computation.10 | loop fusion | flops 8192 | bytes 40960 | tf_op jit(solution)/shard_map/exp | solution.py:342
  14.2 0.1 broadcast_select_fusion.1
  14.3 0.0 copy-start.2
  14.3 0.0 copy-start.3
  14.3 1.4 %divide_multiply_fusion.gate_ref = f32[256,512]{1,0:T(8,128)S(1)} fusion(bf16[256,256]{1,0:T(8,128)(2,1)} %bitcast.16, bf16[256,1024]{1,0:T(8,128)(2,1)} %param.7), kind=kOutput, calls=%fused_computation | convolution fusion | flops 67633152 | bytes 917504 | tf_op jit(solution)/shard_map/dot_general | solution.py:350
  15.7 0.0 copy-start
  15.8 0.1 pad.16.clone
  15.8 0.0 collective-permute-done.1
  15.9 0.0 collective-permute-done
  15.9 0.1 maximum_maximum_fusion.1
  16.0 1.3 %collective-permute-start.2 = (bf16[72,256]{1,0:T(8,128)(2,1)S(1)}, bf16[72,256]{1,0:T(8,128)(2,1)S(1)}, u32[]{:S(2)}, u32[]{:S(2)}) collective-permute-start(bf16[72,256]{1,0:T(8,128)(2,1)S(1)} %bitcast.22), channel_id=1, source_target_pairs={{0,1},{1,2},{2,3},{3,4},{4,5},{5,6},{6,7},{7,8},{8,9},{9,10},{10,1... | collective-permute-start | bytes 110600 | tf_op jit(solution)/shard_map/ppermute | solution.py:301
  17.3 1.3 %collective-permute-start.3 = (bf16[72,256]{1,0:T(8,128)(2,1)S(1)}, bf16[72,256]{1,0:T(8,128)(2,1)S(1)}, u32[]{:S(2)}, u32[]{:S(2)}) collective-permute-start(bf16[72,256]{1,0:T(8,128)(2,1)S(1)} %bitcast.21), channel_id=1, source_target_pairs={{1,0},{2,1},{3,2},{4,3},{5,4},{6,5},{7,6},{8,7},{9,8},{10,9},{11,1... | collective-permute-start | bytes 110600 | tf_op jit(solution)/shard_map/ppermute | solution.py:301
  18.6 0.1 pad_add_fusion.place_ref
  18.6 0.0 copy-done.2
  18.7 0.0 copy-done.3
  18.7 0.1 copy.20.px_ref
  18.9 0.0 copy-done
  18.9 1.3 %inner.1 = (f32[4,576,128]{2,1,0:T(8,128)S(1)}, f32[4,256,128]{2,1,0:T(8,128)S(1)}) custom-call(bf16[48,256]{1,0:T(8,128)(2,1)S(1)} %bitcast.20, bf16[256,256]{1,0:T(8,128)(2,1)S(1)} %bitcast.17, bf16[48,256]{1,0:T(8,128)(2,1)S(1)} %bitcast.19, bf16[256,512]{1,0:T(8,128)(2,1)S(1)} %slice.39.wv_ref, f32[49,512]{1,0:T(8,128)S(1)} %reshape.177.taps_ref), custom_call_target="tpu_custom_call" | custom-call | flops 92274688 | bytes 4194304 | tf_op jit(solution)/shard_map/inner/pallas_call | solution.py:359
  20.2 0.0 collective-permute-done.2.before_ref
  20.3 1.7 %collective-permute-done.3.after_ref = bf16[72,256]{1,0:T(8,128)(2,1)S(1)} collective-permute-done((bf16[72,256]{1,0:T(8,128)(2,1)S(1)}, bf16[72,256]{1,0:T(8,128)(2,1)S(1)}, u32[]{:S(2)}, u32[]{:S(2)}) %collective-permute-start.3) | collective-permute-done | bytes 36896 | tf_op jit(solution)/shard_map/ppermute | solution.py:301
  22.0 2.3 %conv_scan.1 = (f32[4,576,128]{2,1,0:T(8,128)S(1)}, f32[4,256,128]{2,1,0:T(8,128)S(1)}, bf16[8,144,128]{2,1,0:T(8,128)(2,1)S(1)}) custom-call(bf16[72,256]{1,0:T(8,128)(2,1)S(1)} %collective-permute-done.2.before_ref, bf16[72,256]{1,0:T(8,128)(2,1)S(1)} %collective-permute-done.3.after_ref, ...), custom_call_target="tpu_custom_call", output_to_operand_aliasing={{0}: (7, {})} | custom-call | tf_op jit(solution)/shard_map/conv_scan/pallas_call | solution.py:368
  24.3 12.8 %all_to_all.10.near_ref = bf16[8,144,128]{2,1,0:T(8,128)(2,1)S(1)} all-to-all(bf16[8,144,128]{2,1,0:T(8,128)(2,1)S(1)} %get-tuple-element.19), channel_id=1, replica_groups={{0,1,2,3,32,33,34,35},{4,5,6,7,36,37,38,39},{8,9,10,11,40,41,42,43},{12..., dimensions={0} | all-to-all | bytes 589824 | tf_op jit(solution)/shard_map/all_to_all | solution.py:324
  37.1 0.7 %totals.1 = bf16[8,144,128]{2,1,0:T(8,128)(2,1)S(1)} custom-call(s32[2]{0:T(128)S(1)} %pad_add_fusion.place_ref, bf16[8,144,128]{2,1,0:T(8,128)(2,1)S(1)} %all_to_all.10.near_ref, f32[4,64,128]{2,1,0:T(8,128)S(1)} %bitcast.14), custom_call_target="tpu_custom_call" | custom-call | tf_op jit(solution)/shard_map/totals/pallas_call | solution.py:381
  37.8 0.0 copy-start.1
  37.8 16.3 %all_to_all.11.far_ref = bf16[8,144,128]{2,1,0:T(8,128)(2,1)S(1)} all-to-all(bf16[8,144,128]{2,1,0:T(8,128)(2,1)S(1)} %totals.1), channel_id=1, replica_groups={{0,4,8,12,16,20,24,28},{1,5,9,13,17,21,25,29},{2,6,10,14,18,22,26,30},{..., dimensions={0} | all-to-all | bytes 589824 | tf_op jit(solution)/shard_map/all_to_all | solution.py:324
  54.1 0.7 %enter.1 = (f32[128,128]{1,0:T(8,128)S(1)}, bf16[128,128]{1,0:T(8,128)(2,1)S(1)}) custom-call(s32[2]{0:T(128)S(1)} %pad_add_fusion.place_ref, bf16[8,144,128]{2,1,0:T(8,128)(2,1)S(1)} %all_to_all.10.near_ref, bf16[8,144,128]{2,1,0:T(8,128)(2,1)S(1)} %all_to_all.11.far_ref, f32[4,64,128]{2,1,0:T(8,128)S(1)} %bitcast.15), custom_call_target="tpu_custom_call" | custom-call | tf_op jit(solution)/shard_map/enter/pallas_call | solution.py:391
  54.9 6.7 %collective-permute-start.4 = (bf16[128,128]{1,0:T(8,128)(2,1)S(1)}, bf16[128,128]{1,0:T(8,128)(2,1)S(1)}, u32[]{:S(2)}, u32[]{:S(2)}) collective-permute-start(bf16[128,128]{1,0:T(8,128)(2,1)S(1)} %get-tuple-element.21), channel_id=1, source_target_pairs={{0,32},{32,0},{64,96},{96,64},{128,160},{160,128},{192,224},{224,1... | collective-permute-start | bytes 98312 | tf_op jit(solution)/shard_map/ppermute | solution.py:399
  61.5 0.8 %own_axis.1.sum_ref = f32[4,256,128]{2,1,0:T(8,128)S(1)} custom-call(s32[2]{0:T(128)S(1)} %pad_add_fusion.place_ref, f32[128,128]{1,0:T(8,128)S(1)} %get-tuple-element.22.keep_ref, f32[12,512]{1,0:T(8,128)S(1)} %pad_maximum_fusion.cst_ref, f32[256,2]{1,0:T(8,128)S(1)} %copy.20.px_ref, f32[4,256,128]{2,1,0:T(8,128)S(1)} %get-tuple-element.23.sum_ref), custom_call_target="tpu_custom_call" | custom-call | flops 786432 | bytes 2097152 | tf_op jit(solution)/shard_map/own_axis/pallas_call | solution.py:401
  62.3 0.0 collective-permute-done.4.got_ref
  62.4 0.0 copy-done.1
  62.4 2.0 %finish.1 = bf16[256,256]{1,0:T(8,128)(2,1)} custom-call(s32[2]{0:T(128)S(1)} %pad_add_fusion.place_ref, bf16[128,128]{1,0:T(8,128)(2,1)S(1)} %collective-permute-done.4.got_ref, f32[12,512]{1,0:T(8,128)S(1)} %pad_maximum_fusion.cst_ref, f32[256,2]{1,0:T(8,128)S(1)} %copy.20.px_ref, f32[4,256,128]{2,1,0:T(8,128)S(1)} %own_axis.1.sum_ref, ...), custom_call_target="tpu_custom_call" | custom-call | tf_op jit(solution)/shard_map/finish/pallas_call | solution.py:411
  (18 shorter events, 0.2 us)
Async XLA Ops:
  0.8 15.1 %collective-permute-start.1 = (bf16[3,16,256]{2,0,1:T(4,128)(2,1)S(1)}, bf16[3,16,256]{2,0,1:T(4,128)(2,1)S(1)}, u32[]{:S(2)}, u32[]{:S(2)}) collective-permute-start(bf16[3,16,256]{2,0,1:T(4,128)(2,1)S(1)} %copy.25), channel_id=1, source_target_pairs={{32,0},{64,32},{96,64},{128,96},{160,128},{192,160},{224,192},{256... | collective-permute-start | bytes 73736 | tf_op jit(solution)/shard_map/ppermute | solution.py:301
  9.6 6.3 %collective-permute-start = (bf16[3,16,256]{2,0,1:T(4,128)(2,1)S(1)}, bf16[3,16,256]{2,0,1:T(4,128)(2,1)S(1)}, u32[]{:S(2)}, u32[]{:S(2)}) collective-permute-start(bf16[3,16,256]{2,0,1:T(4,128)(2,1)S(1)} %copy.23), channel_id=1, source_target_pairs={{0,32},{32,64},{64,96},{96,128},{128,160},{160,192},{192,224},{224... | collective-permute-start | bytes 73736 | tf_op jit(solution)/shard_map/ppermute | solution.py:301
  14.3 4.4 %copy-start.2 = (bf16[256,1024]{1,0:T(8,128)(2,1)S(1)}, bf16[256,1024]{1,0:T(8,128)(2,1)}, u32[]{:S(2)}) copy-start(bf16[256,1024]{1,0:T(8,128)(2,1)} %param.7) | copy-start | bytes 1572868
  14.3 4.4 %copy-start.3 = (f32[7,7,512]{2,1,0:T(8,128)S(1)}, f32[7,7,512]{2,1,0:T(8,128)}, u32[]{:S(2)}) copy-start(f32[7,7,512]{2,1,0:T(8,128)} %param.8) | copy-start | bytes 301060
  15.7 3.2 %copy-start = (bf16[16,16,256]{2,1,0:T(8,128)(2,1)S(1)}, bf16[16,16,256]{2,1,0:T(8,128)(2,1)}, u32[]{:S(2)}) copy-start(bf16[16,16,256]{2,1,0:T(8,128)(2,1)} %param.6) | copy-start | bytes 393220
  16.0 4.3 %collective-permute-start.2 = (bf16[72,256]{1,0:T(8,128)(2,1)S(1)}, bf16[72,256]{1,0:T(8,128)(2,1)S(1)}, u32[]{:S(2)}, u32[]{:S(2)}) collective-permute-start(bf16[72,256]{1,0:T(8,128)(2,1)S(1)} %bitcast.22), channel_id=1, source_target_pairs={{0,1},{1,2},{2,3},{3,4},{4,5},{5,6},{6,7},{7,8},{8,9},{9,10},{10,1... | collective-permute-start | bytes 110600 | tf_op jit(solution)/shard_map/ppermute | solution.py:301
  17.3 4.7 %collective-permute-start.3 = (bf16[72,256]{1,0:T(8,128)(2,1)S(1)}, bf16[72,256]{1,0:T(8,128)(2,1)S(1)}, u32[]{:S(2)}, u32[]{:S(2)}) collective-permute-start(bf16[72,256]{1,0:T(8,128)(2,1)S(1)} %bitcast.21), channel_id=1, source_target_pairs={{1,0},{2,1},{3,2},{4,3},{5,4},{6,5},{7,6},{8,7},{9,8},{10,9},{11,1... | collective-permute-start | bytes 110600 | tf_op jit(solution)/shard_map/ppermute | solution.py:301
  37.8 24.6 %copy-start.1 = (bf16[512,256]{1,0:T(8,128)(2,1)S(1)}, bf16[512,256]{1,0:T(8,128)(2,1)}, u32[]{:S(2)}) copy-start(bf16[512,256]{1,0:T(8,128)(2,1)} %wo_ref.1) | copy-start | bytes 786436
  54.9 7.5 %collective-permute-start.4 = (bf16[128,128]{1,0:T(8,128)(2,1)S(1)}, bf16[128,128]{1,0:T(8,128)(2,1)S(1)}, u32[]{:S(2)}, u32[]{:S(2)}) collective-permute-start(bf16[128,128]{1,0:T(8,128)(2,1)S(1)} %get-tuple-element.21), channel_id=1, source_target_pairs={{0,32},{32,0},{64,96},{96,64},{128,160},{160,128},{192,224},{224,1... | collective-permute-start | bytes 98312 | tf_op jit(solution)/shard_map/ppermute | solution.py:399

commit v4 on v3

--- a/solution.py
+++ b/solution.py
@@ -16,8 +16,13 @@
 VMEM = pltpu.VMEM
 
 
+def position():
+    row, col = lax.axis_index("row"), lax.axis_index("col")
+    return row % 2, row // 2, col % XS, col // XS
+
+
 def project(x, wv_ref, store):
-    for half in range(wv_ref.shape[1] // 256):
+    for half in range(wv_ref.shape[1] // 512):
         p = jnp.dot(x, wv_ref[:, half * 256:(half + 1) * 256], preferred_element_type=F32)
         p = p.astype(BF16).astype(F32)
         store(2 * half, p[:, :LANES])
@@ -26,7 +31,7 @@
 
 def add_taps(acc, v_ref, taps_ref, ct, lanes, jt, shifts):
     for b in shifts:
-        tap = [taps_ref[pl.ds(a * 7 + b, 1), lanes] for a in range(7)]
+        tap = [taps_ref[a, pl.ds(b, 1), lanes] for a in range(7)]
         tap = [jnp.broadcast_to(t, (8, LANES)) for t in tap]
         for r in range(T + 6):
             x = v_ref[ct, pl.ds(r * PW + jt * 8 + b, 8), :]
@@ -37,8 +42,11 @@
     return acc
 
 
-def inner_kernel(above_ref, tok_ref, below_ref, wv_ref, taps_ref, v_ref, acc_ref):
+def inner_kernel(above_ref, tok_ref, below_ref, wv_ref, taps_ref, px_ref, v_ref, acc_ref, g_ref, h_ref):
     groups = v_ref.shape[0]
+    px = px_ref[...]
+    g_ref[...] = jnp.broadcast_to(px[:, 0:1], (PX, LANES))
+    h_ref[...] = jnp.broadcast_to(px[:, 1:2], (PX, LANES))
     for ref, first in ((above_ref, 0), (tok_ref, 3), (below_ref, T + 3)):
         count = ref.shape[0] // T
 
@@ -59,20 +67,19 @@
     lax.fori_loop(0, groups, group, 0)
 
 
-def conv_scan_kernel(before_ref, after_ref, wv_ref, taps_ref, cst_ref, px_ref, tails_ref, own_ref, acc_ref,
-                     v_ref, sum_ref, near_ref, g_ref, h_ref, val_ref, end_ref):
+def conv_scan_kernel(before_ref, after_ref, wv_ref, taps_ref, cst_ref, g_ref, h_ref, tails_ref, own_ref, acc_ref,
+                     v_ref, sum_ref, near_ref, side_ref, val_ref, end_ref):
     del own_ref
     groups = v_ref.shape[0]
-    for ref, first in ((before_ref, 0), (after_ref, T + 3)):
-
-        def store(ct, p, first=first):
-            for j in range(3):
-                v_ref[ct, pl.ds(first + j, PW, stride=PW), :] = p[j * PW:(j + 1) * PW]
-
-        project(ref[...], wv_ref, store)
-    px = px_ref[...]
-    g_ref[...] = jnp.broadcast_to(px[:, 0:1], (PX, LANES))
-    h_ref[...] = jnp.broadcast_to(px[:, 1:2], (PX, LANES))
+    side_ref[0:3 * PW] = before_ref[...].astype(F32)
+    side_ref[3 * PW:] = after_ref[...].astype(F32)
+
+    def store(ct, p):
+        for j in range(6):
+            at = j if j < 3 else T + j
+            v_ref[ct, pl.ds(at, PW, stride=PW), :] = p[j * PW:(j + 1) * PW]
+
+    project(side_ref[...].astype(BF16), wv_ref, store)
 
     def group(ct, carry):
         lanes = pl.ds(pl.multiple_of(ct * LANES, LANES), LANES)
@@ -136,9 +143,8 @@
     return line_decay(block, at) + line_decay(block, at + gap)
 
 
-def totals_kernel(place_ref, near_ref, whole_ref, far_ref):
-    core, y = place_ref[0] % 2, place_ref[0] // 2
-    x, z = place_ref[1] % XS, place_ref[1] // XS
+def totals_kernel(near_ref, whole_ref, far_ref):
+    core, y, x, z = position()
     lane = lax.broadcasted_iota(jnp.int32, (T, LANES), 1)
 
     def spread(first, second):
@@ -185,9 +191,8 @@
             far_ref[peer, 128:144] = tail
 
 
-def enter_kernel(place_ref, near_ref, far_ref, whole_ref, keep_ref, give_ref):
-    core, y = place_ref[0] % 2, place_ref[0] // 2
-    x, z = place_ref[1] % XS, place_ref[1] // XS
+def enter_kernel(near_ref, far_ref, whole_ref, keep_ref, give_ref):
+    core, y, x, z = position()
 
     def far_states(me, k, ahead, back):
         blocks = [far_ref[i].astype(F32) for i in range(FAR)]
@@ -253,10 +258,7 @@
     lax.fori_loop(0, 4, group, 0)
 
 
-def own_axis_kernel(place_ref, keep_ref, cst_ref, px_ref, sum_ref, acc_ref, g_ref):
-    px = px_ref[...]
-    g_ref[...] = jnp.broadcast_to(px[:, 0:1], (PX, LANES))
-
+def own_axis_kernel(keep_ref, cst_ref, g_ref, sum_ref, acc_ref):
     def first(side, ct, half):
         return keep_ref[pl.ds(64 * side + ct * T + half * 8, 8), :]
 
@@ -264,16 +266,14 @@
         acc_ref[ct, at, :] = sum_ref[ct, at, :] + x
 
     for kind in range(2):
-        @pl.when(place_ref[0] % 2 == kind)
+        @pl.when(position()[0] == kind)
         def _():
             decay_rows(kind, first, cst_ref, g_ref, store)
 
 
-def finish_kernel(place_ref, got_ref, cst_ref, px_ref, sum_ref, gate_ref, tok_ref, wo_ref,
-                  out_ref, acc_ref, g_ref, enter_ref, gated_ref):
+def finish_kernel(got_ref, cst_ref, g_ref, sum_ref, gate_ref, tok_ref, wo_ref,
+                  out_ref, acc_ref, enter_ref, gated_ref):
     groups = acc_ref.shape[0]
-    px = px_ref[...]
-    g_ref[...] = jnp.broadcast_to(px[:, 0:1], (PX, LANES))
     enter_ref[...] = got_ref[...].astype(F32)
 
     def first(side, ct, half):
@@ -283,7 +283,7 @@
         acc_ref[ct, at, :] = sum_ref[ct, at, :] + x
 
     for kind in range(2):
-        @pl.when(place_ref[0] % 2 != kind)
+        @pl.when(position()[0] != kind)
         def _():
             decay_rows(kind, first, cst_ref, g_ref, store)
 
@@ -337,87 +337,85 @@
                              jnp.zeros((PW - T - 6, 3, channels), BF16)], axis=0)
         return x.transpose(1, 0, 2).reshape(3 * PW, channels)
 
-    before, after = neighbours(strip(slice(0, 3)), strip(slice(T - 3, T)), "col")
+    first, last = strip(slice(0, 3)), strip(slice(T - 3, T))
+    px = jnp.stack([jnp.exp(-extra), -jnp.expm1(-2.0 * extra)], axis=-1).reshape(PX, 2)
+    tails = jnp.stack([tail_block(jnp.exp(-jnp.sum(extra, axis=1))),
+                       tail_block(jnp.exp(-jnp.sum(extra, axis=0)))])
+    first, last, table, later_weight, px, tails = lax.optimization_barrier(
+        (first, last, table, input_weight, px, tails))
+    before, after = neighbours(first, last, "col")
 
     cst = jnp.concatenate([jnp.exp(-table), -jnp.expm1(-2.0 * table), jnp.exp(-2.0 * table)], axis=0)
     whole = jnp.exp(-float(T) * table).reshape(4, groups, 1, LANES)
     whole = jnp.broadcast_to(whole, (4, groups, T, LANES)).reshape(4, groups * T, LANES)
-    px = jnp.stack([jnp.exp(-extra), -jnp.expm1(-2.0 * extra)], axis=-1).reshape(PX, 2)
-    tails = jnp.stack([tail_block(jnp.exp(-jnp.sum(extra, axis=1))),
-                       tail_block(jnp.exp(-jnp.sum(extra, axis=0)))])
-    place = jnp.stack([lax.axis_index("row"), lax.axis_index("col")]).astype(jnp.int32)
     flat = tokens.reshape(PX, channels)
-    gate = jax.nn.silu(jnp.dot(flat, input_weight[:, width:], preferred_element_type=F32))
-    before, gate, whole, place = lax.optimization_barrier((before, gate, whole, place))
-    values_weight, taps = input_weight[:, :width], kernel.reshape(49, width)
+    gate = jax.nn.silu(jnp.dot(flat, later_weight[:, width:], preferred_element_type=F32))
+    before, after, gate, whole, cst = lax.optimization_barrier((before, after, gate, whole, cst))
 
     spec = pl.BlockSpec(memory_space=VMEM)
-    smem = pl.BlockSpec(memory_space=pltpu.SMEM)
     params = pltpu.CompilerParams(vmem_limit_bytes=16 * 2**20)
     tile = jax.ShapeDtypeStruct((groups, PX, LANES), F32)
     padded = jax.ShapeDtypeStruct((groups, PW * PW, LANES), F32)
-    own, partial = pl.pallas_call(
+    spread = jax.ShapeDtypeStruct((PX, LANES), F32)
+    own, partial, g, h = pl.pallas_call(
         inner_kernel,
-        out_shape=(padded, tile),
-        in_specs=[spec] * 5,
-        out_specs=(spec, spec),
+        out_shape=(padded, tile, spread, spread),
+        in_specs=[spec] * 6,
+        out_specs=(spec,) * 4,
         compiler_params=params,
         cost_estimate=pl.CostEstimate(flops=2 * 352 * channels * width, bytes_accessed=4 * 2**20, transcendentals=0),
         name="inner",
-    )(above.reshape(3 * T, channels), flat, below.reshape(3 * T, channels), values_weight, taps)
+    )(above.reshape(3 * T, channels), flat, below.reshape(3 * T, channels), input_weight, kernel, px)
     _, local, near = pl.pallas_call(
         conv_scan_kernel,
         out_shape=(padded, tile, jax.ShapeDtypeStruct((2 * XS, 144, LANES), BF16)),
-        in_specs=[spec] * 9,
+        in_specs=[spec] * 10,
         out_specs=(spec, spec, spec),
-        scratch_shapes=[VMEM((PX, LANES), F32), VMEM((PX, LANES), F32), VMEM((PX, LANES), F32),
-                        VMEM((2, 128, LANES), F32)],
-        input_output_aliases={7: 0},
+        scratch_shapes=[VMEM((6 * PW, channels), F32), VMEM((PX, LANES), F32), VMEM((2, 128, LANES), F32)],
+        input_output_aliases={8: 0},
         compiler_params=params,
         name="conv_scan",
-    )(before, after, values_weight, taps, cst, px, tails, own, partial)
+    )(before, after, input_weight, kernel, cst, g, h, tails, own, partial)
     near = swap(near, near_groups(rows, cols))
 
     far = pl.pallas_call(
         totals_kernel,
         out_shape=jax.ShapeDtypeStruct((FAR, 144, LANES), BF16),
-        in_specs=[smem, spec, spec],
+        in_specs=[spec, spec],
         out_specs=spec,
         compiler_params=params,
         name="totals",
-    )(place, near, whole)
+    )(near, whole)
     far = swap(far, far_groups(rows, cols))
 
     keep, give = pl.pallas_call(
         enter_kernel,
         out_shape=(jax.ShapeDtypeStruct((128, LANES), F32), jax.ShapeDtypeStruct((128, LANES), BF16)),
-        in_specs=[smem, spec, spec, spec],
+        in_specs=[spec, spec, spec],
         out_specs=(spec, spec),
         compiler_params=params,
         name="enter",
-    )(place, near, far, whole)
+    )(near, far, whole)
     got = lax.ppermute(give, "row", [(i, i ^ 1) for i in range(rows)])
 
     acc = pl.pallas_call(
         own_axis_kernel,
         out_shape=tile,
-        in_specs=[smem] + [spec] * 4,
+        in_specs=[spec] * 4,
         out_specs=spec,
-        scratch_shapes=[VMEM((PX, LANES), F32)],
         compiler_params=params,
         cost_estimate=pl.CostEstimate(flops=6 * PX * width, bytes_accessed=2 * 2**20, transcendentals=0),
         name="own_axis",
-    )(place, keep, cst, px, local)
+    )(keep, cst, g, local)
     mixed = pl.pallas_call(
         finish_kernel,
         out_shape=jax.ShapeDtypeStruct((PX, channels), BF16),
-        in_specs=[smem] + [spec] * 7,
+        in_specs=[spec] * 7,
         out_specs=spec,
-        scratch_shapes=[VMEM((groups, PX, LANES), F32), VMEM((PX, LANES), F32),
-                        VMEM((128, LANES), F32), VMEM((PX, width), BF16)],
+        scratch_shapes=[VMEM((groups, PX, LANES), F32), VMEM((128, LANES), F32), VMEM((PX, width), BF16)],
         compiler_params=params,
         name="finish",
-    )(place, got, cst, px, acc, gate, flat, output_weight)
+    )(got, cst, g, acc, gate, flat, output_weight)
     return mixed.reshape(T, T, channels)
 
 

time: 64.9 us -> 62.4 us (0.961)
  the two profiles are of different devices: /device:TPU:1 before, /device:TPU:33 now
where the time goes in v4:
time: 62.4 us; the launch traced here: 61.9 us
  blocking collectives  28 us (45%)
  starting transfers between devices  21.8 us (35%)
  Pallas kernels  5.48 us (9%)
  local copies, waits for them, and re-layouts  2.16 us (3%)
  other arithmetic  1.74 us (3%)
  matrix products  1.38 us (2%)
  waiting for transfers between devices  1.08 us (2%)
    all_to_all x2, blocking collectives, swap(): lax.all_to_all(x, ('row', 'col'), 0, 0, axis_index_groups=groups, tiled=T...  28 us
    ppermute x1, starting transfers between devices, body(): got = lax.ppermute(give, 'row', [(i, i ^ 1) for i in range(rows)])  11.8 us
    ppermute x4, starting transfers between devices, neighbours(): return (lax.ppermute(x_last, axis, up), lax.ppermute(x_first, axis, down))  9.97 us
    pallas_call x1, Pallas kernels, body(): pl.pallas_call(conv_scan_kernel, out_shape=(padded, tile, jax.ShapeDtypeS...  2.32 us
    pallas_call x1, Pallas kernels, body(): pl.pallas_call(finish_kernel, out_shape=jax.ShapeDtypeStruct((PX, channel...  1.39 us
    dot_general x1, matrix products, body(): jnp.dot(flat, later_weight[:, width:], preferred_element_type=F32)  1.38 us
    pallas_call x1, Pallas kernels, body(): pl.pallas_call(inner_kernel, out_shape=(padded, tile, spread, spread), in...  1.34 us
  transfers between devices with their start and end apart: 5, of which 2 were waited for; matrix products, arithmetic and copies ran while one was open for 6% of the time, Pallas kernels for 2%

profile of v4, /device:TPU:33, one launch (start us, length us, event | category | flops | bytes accessed | tf_op | source)
XLA Modules:
  0.0 61.9 jit_solution(1402597197066916480)
XLA Ops:
  0.0 0.8 %fusion.5 = (bf16[3,16,256]{2,1,0:T(8,128)(2,1)S(1)}, bf16[3,16,256]{2,1,0:T(8,128)(2,1)S(1)}) fusion(bf16[16,16,256]{2,1,0:T(8,128)(2,1)} %param.6), kind=kLoop, calls=%fused_computation.25 | loop fusion | bytes 98304 | tf_op jit(solution)/shard_map/slice | solution.py:333
  0.8 2.6 %collective-permute-start.1 = (bf16[3,16,256]{2,0,1:T(4,128)(2,1)S(1)}, bf16[3,16,256]{2,0,1:T(4,128)(2,1)S(1)}, u32[]{:S(2)}, u32[]{:S(2)}) collective-permute-start(bf16[3,16,256]{2,0,1:T(4,128)(2,1)S(1)} %copy.27), channel_id=1, source_target_pairs={{32,0},{64,32},{96,64},{128,96},{160,128},{192,160},{224,192},{256... | collective-permute-start | bytes 73736 | tf_op jit(solution)/shard_map/ppermute | solution.py:301
  3.4 3.0 %collective-permute-start = (bf16[3,16,256]{2,0,1:T(4,128)(2,1)S(1)}, bf16[3,16,256]{2,0,1:T(4,128)(2,1)S(1)}, u32[]{:S(2)}, u32[]{:S(2)}) collective-permute-start(bf16[3,16,256]{2,0,1:T(4,128)(2,1)S(1)} %copy.25), channel_id=1, source_target_pairs={{0,32},{32,64},{64,96},{96,128},{128,160},{160,192},{192,224},{224... | collective-permute-start | bytes 73736 | tf_op jit(solution)/shard_map/ppermute | solution.py:301
  6.4 0.9 %fusion.4 = (bf16[16,3,256]{2,1,0:T(4,128)(2,1)S(1)}, bf16[16,3,256]{2,1,0:T(4,128)(2,1)S(1)}) fusion(bf16[16,16,256]{2,1,0:T(8,128)(2,1)} %param.6), kind=kLoop, calls=%fused_computation.24 | loop fusion | bytes 98304 | tf_op jit(solution)/shard_map/slice | solution.py:336
  7.3 0.8 %fusion.3 = (f32[16]{0:T(128)S(1)}, f32[16]{0:T(128)S(1)}, f32[16,16]{1,0:T(8,128)S(1)}, f32[16,16]{1,0:T(8,128)S(1)}) fusion(f32[16,16]{1,0:T(8,128)} %param.10), kind=kLoop, calls=%fused_computation.23 | loop fusion | flops 1248 | bytes 3200 | tf_op jit(solution)/shard_map/reduce_sum | solution.py:342
  8.1 0.1 stack.14
  8.2 0.1 stack.15
  8.3 0.1 broadcast_select_fusion.1
  8.4 0.1 pad.14.clone
  8.5 0.0 collective-permute-done.1
  8.5 0.0 collective-permute-done
  8.6 0.1 maximum_maximum_fusion.1
  8.7 0.7 %negate_exponential_fusion = (f32[4,512]{1,0:T(4,128)S(1)}, f32[4,512]{1,0:T(4,128)S(1)}, f32[4,512]{1,0:T(4,128)S(1)}, f32[4,512]{1,0:T(4,128)S(1)}) fusion(f32[4,512]{1,0:T(4,128)} %param.9), kind=kLoop, calls=%fused_computation.8 | loop fusion | flops 8192 | bytes 40960 | tf_op jit(solution)/shard_map/exp | solution.py:348
  9.4 3.1 %collective-permute-start.2 = (bf16[72,256]{1,0:T(8,128)(2,1)S(1)}, bf16[72,256]{1,0:T(8,128)(2,1)S(1)}, u32[]{:S(2)}, u32[]{:S(2)}) collective-permute-start(bf16[72,256]{1,0:T(8,128)(2,1)S(1)} %bitcast.24), channel_id=1, source_target_pairs={{0,1},{1,2},{2,3},{3,4},{4,5},{5,6},{6,7},{7,8},{8,9},{9,10},{10,1... | collective-permute-start | bytes 110600 | tf_op jit(solution)/shard_map/ppermute | solution.py:301
  12.5 1.3 %collective-permute-start.3 = (bf16[72,256]{1,0:T(8,128)(2,1)S(1)}, bf16[72,256]{1,0:T(8,128)(2,1)S(1)}, u32[]{:S(2)}, u32[]{:S(2)}) collective-permute-start(bf16[72,256]{1,0:T(8,128)(2,1)S(1)} %bitcast.23), channel_id=1, source_target_pairs={{1,0},{2,1},{3,2},{4,3},{5,4},{6,5},{7,6},{8,7},{9,8},{10,9},{11,1... | collective-permute-start | bytes 110600 | tf_op jit(solution)/shard_map/ppermute | solution.py:301
  13.8 0.0 copy-start
  13.8 0.0 copy-start.1
  13.8 0.0 copy-start.2
  13.8 1.4 %divide_multiply_fusion.gate_ref = f32[256,512]{1,0:T(8,128)S(1)} fusion(bf16[256,256]{1,0:T(8,128)(2,1)} %bitcast.18, bf16[256,1024]{1,0:T(8,128)(2,1)} %wv_ref.3), kind=kOutput, calls=%fused_computation.1 | convolution fusion | flops 67633152 | bytes 917504 | tf_op jit(solution)/shard_map/dot_general | solution.py:352
  15.3 0.1 copy.23.px_ref
  15.4 0.0 copy-done
  15.4 0.0 copy-done.1
  15.4 0.0 copy-done.2
  15.5 1.3 %inner.1 = (f32[4,576,128]{2,1,0:T(8,128)S(1)}, f32[4,256,128]{2,1,0:T(8,128)S(1)}, f32[256,128]{1,0:T(8,128)S(1)}, f32[256,128]{1,0:T(8,128)S(1)}) custom-call(bf16[48,256]{1,0:T(8,128)(2,1)S(1)} %bitcast.22, bf16[256,256]{1,0:T(8,128)(2,1)S(1)} %bitcast.19, bf16[48,256]{1,0:T(8,128)(2,1)S(1)} %bitcast.21, bf16[256,1024]{1,0:T(8,128)(2,1)S(1)} %copy-done, ...), custom_call_target="tpu_custom_call" | custom-call | flops 92274688 | bytes 4194304 | tf_op jit(solution)/shard_map/inner/pallas_call | solution.py:360
  16.8 0.0 collective-permute-done.2.before_ref
  16.8 0.4 collective-permute-done.3.after_ref
  17.2 2.3 %conv_scan.1 = (f32[4,576,128]{2,1,0:T(8,128)S(1)}, f32[4,256,128]{2,1,0:T(8,128)S(1)}, bf16[8,144,128]{2,1,0:T(8,128)(2,1)S(1)}) custom-call(bf16[72,256]{1,0:T(8,128)(2,1)S(1)} %collective-permute-done.2.before_ref, bf16[72,256]{1,0:T(8,128)(2,1)S(1)} %collective-permute-done.3.after_ref, ...), custom_call_target="tpu_custom_call", output_to_operand_aliasing={{0}: (8, {})} | custom-call | tf_op jit(solution)/shard_map/conv_scan/pallas_call | solution.py:369
  19.5 16.8 %all_to_all.10.near_ref = bf16[8,144,128]{2,1,0:T(8,128)(2,1)S(1)} all-to-all(bf16[8,144,128]{2,1,0:T(8,128)(2,1)S(1)} %get-tuple-element.37), channel_id=1, replica_groups={{0,1,2,3,32,33,34,35},{4,5,6,7,36,37,38,39},{8,9,10,11,40,41,42,43},{12..., dimensions={0} | all-to-all | bytes 589824 | tf_op jit(solution)/shard_map/all_to_all | solution.py:324
  36.4 0.1 totals.1
  36.5 0.0 copy-start.3
  36.5 11.2 %all_to_all.11.far_ref = bf16[8,144,128]{2,1,0:T(8,128)(2,1)S(1)} all-to-all(bf16[8,144,128]{2,1,0:T(8,128)(2,1)S(1)} %totals.1), channel_id=1, replica_groups={{0,4,8,12,16,20,24,28},{1,5,9,13,17,21,25,29},{2,6,10,14,18,22,26,30},{..., dimensions={0} | all-to-all | bytes 589824 | tf_op jit(solution)/shard_map/all_to_all | solution.py:324
  47.7 0.2 enter.1
  47.9 11.8 %collective-permute-start.4 = (bf16[128,128]{1,0:T(8,128)(2,1)S(1)}, bf16[128,128]{1,0:T(8,128)(2,1)S(1)}, u32[]{:S(2)}, u32[]{:S(2)}) collective-permute-start(bf16[128,128]{1,0:T(8,128)(2,1)S(1)} %get-tuple-element.39), channel_id=1, source_target_pairs={{0,32},{32,0},{64,96},{96,64},{128,160},{160,128},{192,224},{224,1... | collective-permute-start | bytes 98312 | tf_op jit(solution)/shard_map/ppermute | solution.py:399
  59.7 0.2 own_axis.1.sum_ref
  59.8 0.7 %collective-permute-done.4.got_ref = bf16[128,128]{1,0:T(8,128)(2,1)S(1)} collective-permute-done((bf16[128,128]{1,0:T(8,128)(2,1)S(1)}, bf16[128,128]{1,0:T(8,128)(2,1)S(1)}, u32[]{:S(2)}, u32[]{:S(2)}) %collective-permute-start.4) | collective-permute-done | bytes 32800 | tf_op jit(solution)/shard_map/ppermute | solution.py:399
  60.5 0.0 copy-done.3
  60.5 1.4 %finish.1 = bf16[256,256]{1,0:T(8,128)(2,1)} custom-call(bf16[128,128]{1,0:T(8,128)(2,1)S(1)} %collective-permute-done.4.got_ref, f32[12,512]{1,0:T(8,128)S(1)} %pad_maximum_fusion.cst_ref, f32[256,128]{1,0:T(8,128)S(1)} %get-tuple-element.32.g_ref, f32[4,256,128]{2,1,0:T(8,128)S(1)} %own_axis.1.sum_ref, f32[256,512]{1,0:T(8,128)S(1)} %divide_multiply_fusion.gate_ref, ...), custom_call_target="tpu_custom_call" | custom-call | tf_op jit(solution)/shard_map/finish/pallas_call | solution.py:410
  (16 shorter events, 0.1 us)
Async XLA Ops:
  0.8 7.7 %collective-permute-start.1 = (bf16[3,16,256]{2,0,1:T(4,128)(2,1)S(1)}, bf16[3,16,256]{2,0,1:T(4,128)(2,1)S(1)}, u32[]{:S(2)}, u32[]{:S(2)}) collective-permute-start(bf16[3,16,256]{2,0,1:T(4,128)(2,1)S(1)} %copy.27), channel_id=1, source_target_pairs={{32,0},{64,32},{96,64},{128,96},{160,128},{192,160},{224,192},{256... | collective-permute-start | bytes 73736 | tf_op jit(solution)/shard_map/ppermute | solution.py:301
  3.4 5.1 %collective-permute-start = (bf16[3,16,256]{2,0,1:T(4,128)(2,1)S(1)}, bf16[3,16,256]{2,0,1:T(4,128)(2,1)S(1)}, u32[]{:S(2)}, u32[]{:S(2)}) collective-permute-start(bf16[3,16,256]{2,0,1:T(4,128)(2,1)S(1)} %copy.25), channel_id=1, source_target_pairs={{0,32},{32,64},{64,96},{96,128},{128,160},{160,192},{192,224},{224... | collective-permute-start | bytes 73736 | tf_op jit(solution)/shard_map/ppermute | solution.py:301
  9.4 7.4 %collective-permute-start.2 = (bf16[72,256]{1,0:T(8,128)(2,1)S(1)}, bf16[72,256]{1,0:T(8,128)(2,1)S(1)}, u32[]{:S(2)}, u32[]{:S(2)}) collective-permute-start(bf16[72,256]{1,0:T(8,128)(2,1)S(1)} %bitcast.24), channel_id=1, source_target_pairs={{0,1},{1,2},{2,3},{3,4},{4,5},{5,6},{6,7},{7,8},{8,9},{9,10},{10,1... | collective-permute-start | bytes 110600 | tf_op jit(solution)/shard_map/ppermute | solution.py:301
  12.5 4.7 %collective-permute-start.3 = (bf16[72,256]{1,0:T(8,128)(2,1)S(1)}, bf16[72,256]{1,0:T(8,128)(2,1)S(1)}, u32[]{:S(2)}, u32[]{:S(2)}) collective-permute-start(bf16[72,256]{1,0:T(8,128)(2,1)S(1)} %bitcast.23), channel_id=1, source_target_pairs={{1,0},{2,1},{3,2},{4,3},{5,4},{6,5},{7,6},{8,7},{9,8},{10,9},{11,1... | collective-permute-start | bytes 110600 | tf_op jit(solution)/shard_map/ppermute | solution.py:301
  13.8 1.6 %copy-start = (bf16[256,1024]{1,0:T(8,128)(2,1)S(1)}, bf16[256,1024]{1,0:T(8,128)(2,1)}, u32[]{:S(2)}) copy-start(bf16[256,1024]{1,0:T(8,128)(2,1)} %wv_ref.3) | copy-start | bytes 1572868
  13.8 1.6 %copy-start.1 = (bf16[16,16,256]{2,1,0:T(8,128)(2,1)S(1)}, bf16[16,16,256]{2,1,0:T(8,128)(2,1)}, u32[]{:S(2)}) copy-start(bf16[16,16,256]{2,1,0:T(8,128)(2,1)} %param.6) | copy-start | bytes 393220
  13.8 1.6 %copy-start.2 = (f32[7,7,512]{2,1,0:T(8,128)S(1)}, f32[7,7,512]{2,1,0:T(8,128)}, u32[]{:S(2)}) copy-start(f32[7,7,512]{2,1,0:T(8,128)} %taps_ref.3) | copy-start | bytes 301060
  36.5 24.0 %copy-start.3 = (bf16[512,256]{1,0:T(8,128)(2,1)S(1)}, bf16[512,256]{1,0:T(8,128)(2,1)}, u32[]{:S(2)}) copy-start(bf16[512,256]{1,0:T(8,128)(2,1)} %wo_ref.1) | copy-start | bytes 786436
  47.9 12.7 %collective-permute-start.4 = (bf16[128,128]{1,0:T(8,128)(2,1)S(1)}, bf16[128,128]{1,0:T(8,128)(2,1)S(1)}, u32[]{:S(2)}, u32[]{:S(2)}) collective-permute-start(bf16[128,128]{1,0:T(8,128)(2,1)S(1)} %get-tuple-element.39), channel_id=1, source_target_pairs={{0,32},{32,0},{64,96},{96,64},{128,160},{160,128},{192,224},{224,1... | collective-permute-start | bytes 98312 | tf_op jit(solution)/shard_map/ppermute | solution.py:399

commit v5 on v4

--- a/solution.py
+++ b/solution.py
@@ -42,11 +42,46 @@
     return acc
 
 
-def inner_kernel(above_ref, tok_ref, below_ref, wv_ref, taps_ref, px_ref, v_ref, acc_ref, g_ref, h_ref):
+def fall(x):
+    series = x * (1.0 - x / 2.0 * (1.0 - x / 3.0 * (1.0 - x / 4.0 * (1.0 - x / 5.0 * (1.0 - x / 6.0)))))
+    return jnp.where(x < 0.1, series, 1.0 - jnp.exp(-x))
+
+
+def spread_decays(table_ref, extra_ref, cst_ref, whole_ref, g_ref, h_ref, tails_ref):
+    table = table_ref[...]
+    cst_ref[0:4] = jnp.exp(-table)
+    cst_ref[4:8] = fall(2.0 * table)
+    cst_ref[8:12] = jnp.exp(-2.0 * table)
+    cst_ref[12:16] = jnp.exp(-float(T) * table)
+    for d in range(4):
+        for ct in range(table.shape[1] // LANES):
+            whole_ref[d, ct * T:(ct + 1) * T] = jnp.broadcast_to(
+                cst_ref[12 + d:13 + d, ct * LANES:(ct + 1) * LANES], (T, LANES))
+    extra = extra_ref[...]
+    diagonal = lax.broadcasted_iota(jnp.int32, (T, T), 0) == lax.broadcasted_iota(jnp.int32, (T, T), 1)
+    down = jnp.zeros((T, LANES), F32)
+    for i in range(T):
+        line = jnp.broadcast_to(extra[i:i + 1], (T, T))
+        line = jnp.sum(jnp.where(diagonal, line, 0.0), axis=1, keepdims=True)
+        line = jnp.broadcast_to(line, (T, LANES))
+        g_ref[i * T:(i + 1) * T] = jnp.exp(-line)
+        h_ref[i * T:(i + 1) * T] = fall(2.0 * line)
+        down = down + line
+    across = jnp.broadcast_to(jnp.sum(extra, axis=1, keepdims=True), (T, LANES))
+    lane = lax.broadcasted_iota(jnp.int32, (T, LANES), 1)
+    for k, total in enumerate((across, down)):
+        decay = jnp.exp(-total)
+        high = decay.astype(BF16).astype(F32)
+        tails_ref[k] = jnp.where(lane < 64, high, decay - high).astype(BF16)
+
+
+def inner_kernel(above_ref, tok_ref, below_ref, weight_ref, taps_ref, table_ref, extra_ref,
+                 acc_ref, gate_ref, cst_ref, whole_ref, g_ref, h_ref, tails_ref, v_ref):
     groups = v_ref.shape[0]
-    px = px_ref[...]
-    g_ref[...] = jnp.broadcast_to(px[:, 0:1], (PX, LANES))
-    h_ref[...] = jnp.broadcast_to(px[:, 1:2], (PX, LANES))
+    spread_decays(table_ref, extra_ref, cst_ref, whole_ref, g_ref, h_ref, tails_ref)
+    for ct in range(groups):
+        for j in (0, 1, 2, T + 3, T + 4, T + 5):
+            v_ref[ct, pl.ds(j, PW, stride=PW), :] = jnp.zeros((PW, LANES), F32)
     for ref, first in ((above_ref, 0), (tok_ref, 3), (below_ref, T + 3)):
         count = ref.shape[0] // T
 
@@ -54,12 +89,17 @@
             for i in range(count):
                 v_ref[ct, pl.ds((first + i) * PW + 3, T), :] = p[i * T:(i + 1) * T]
 
-        project(ref[...], wv_ref, store)
+        project(ref[...], weight_ref, store)
+    width = groups * LANES
+    for half in range(width // 256):
+        at = slice(width + half * 256, width + (half + 1) * 256)
+        pre = jnp.dot(tok_ref[...], weight_ref[:, at], preferred_element_type=F32)
+        gate_ref[:, half * 256:(half + 1) * 256] = pre / (1.0 + jnp.exp(-pre))
 
     def group(ct, carry):
         lanes = pl.ds(pl.multiple_of(ct * LANES, LANES), LANES)
         for jt in range(2):
-            acc = add_taps([None] * T, v_ref, taps_ref, ct, lanes, jt, range(3, 7) if jt == 0 else range(4))
+            acc = add_taps([None] * T, v_ref, taps_ref, ct, lanes, jt, range(7))
             for i in range(T):
                 acc_ref[ct, pl.ds(i * T + jt * 8, 8), :] = acc[i]
         return carry
@@ -67,19 +107,17 @@
     lax.fori_loop(0, groups, group, 0)
 
 
-def conv_scan_kernel(before_ref, after_ref, wv_ref, taps_ref, cst_ref, g_ref, h_ref, tails_ref, own_ref, acc_ref,
-                     v_ref, sum_ref, near_ref, side_ref, val_ref, end_ref):
+def conv_scan_kernel(before_ref, after_ref, wv_ref, taps_ref, cst_ref, g_ref, h_ref, tails_ref, own_ref,
+                     acc_ref, sum_ref, near_ref, side_ref, line_ref, val_ref, end_ref):
     del own_ref
-    groups = v_ref.shape[0]
+    groups = line_ref.shape[0]
     side_ref[0:3 * PW] = before_ref[...].astype(F32)
     side_ref[3 * PW:] = after_ref[...].astype(F32)
 
-    def store(ct, p):
-        for j in range(6):
-            at = j if j < 3 else T + j
-            v_ref[ct, pl.ds(at, PW, stride=PW), :] = p[j * PW:(j + 1) * PW]
-
-    project(side_ref[...].astype(BF16), wv_ref, store)
+    def keep_line(ct, p):
+        line_ref[ct] = p
+
+    project(side_ref[...].astype(BF16), wv_ref, keep_line)
 
     def group(ct, carry):
         lanes = pl.ds(pl.multiple_of(ct * LANES, LANES), LANES)
@@ -89,9 +127,24 @@
             q = cst[4 + d] + cst[8 + d] * h
             return cst[d] * g, q * lax.rsqrt(q) * x
 
+        for side in range(2):
+            outs = range(3) if side == 0 else range(T - 3, T)
+            added = {}
+            for a in range(7):
+                for k in range(3):
+                    column = k if side == 0 else T + 3 + k
+                    reads = [line_ref[ct, pl.ds((3 * side + k) * PW + it * 8 + a, 8), :] for it in range(2)]
+                    for j in outs:
+                        if 0 <= column - j < 7:
+                            tap = taps_ref[a, pl.ds(column - j, 1), lanes]
+                            for it in range(2):
+                                term = tap * reads[it]
+                                added[j, it] = added[j, it] + term if (j, it) in added else term
+            for (j, it), x in added.items():
+                at = pl.ds(it * 8 * T + j, 8, stride=T)
+                acc_ref[ct, at, :] = acc_ref[ct, at, :] + x
         for jt in range(2):
             acc = [acc_ref[ct, pl.ds(i * T + jt * 8, 8), :] for i in range(T)]
-            acc = add_taps(acc, v_ref, taps_ref, ct, lanes, jt, range(3) if jt == 0 else range(4, 7))
             vals = [x / (1.0 + jnp.exp(-x)) for x in acc]
             for i in range(T):
                 val_ref[pl.ds(i * T + jt * 8, 8), :] = vals[i]
@@ -301,13 +354,6 @@
     return lax.ppermute(x_last, axis, up), lax.ppermute(x_first, axis, down)
 
 
-def tail_block(product):
-    high = product.astype(BF16)
-    low = (product - high.astype(F32)).astype(BF16)
-    lane = lax.broadcasted_iota(jnp.int32, (T, LANES), 1)
-    return jnp.where(lane < 64, high[:, None], low[:, None])
-
-
 def near_groups(rows, cols):
     return [[(2 * y + k) * cols + XS * z + x for k in range(2) for x in range(XS)]
             for y in range(rows // 2) for z in range(cols // XS)]
@@ -330,6 +376,7 @@
     channels = tokens.shape[2]
     rows, cols = lax.axis_size("row"), lax.axis_size("col")
     table, extra = direction_decay_table, pixel_extra_decay
+    flat = tokens.reshape(PX, channels)
     above, below = neighbours(tokens[:3], tokens[T - 3:], "row")
 
     def strip(at):
@@ -337,45 +384,35 @@
                              jnp.zeros((PW - T - 6, 3, channels), BF16)], axis=0)
         return x.transpose(1, 0, 2).reshape(3 * PW, channels)
 
-    first, last = strip(slice(0, 3)), strip(slice(T - 3, T))
-    px = jnp.stack([jnp.exp(-extra), -jnp.expm1(-2.0 * extra)], axis=-1).reshape(PX, 2)
-    tails = jnp.stack([tail_block(jnp.exp(-jnp.sum(extra, axis=1))),
-                       tail_block(jnp.exp(-jnp.sum(extra, axis=0)))])
-    first, last, table, later_weight, px, tails = lax.optimization_barrier(
-        (first, last, table, input_weight, px, tails))
-    before, after = neighbours(first, last, "col")
-
-    cst = jnp.concatenate([jnp.exp(-table), -jnp.expm1(-2.0 * table), jnp.exp(-2.0 * table)], axis=0)
-    whole = jnp.exp(-float(T) * table).reshape(4, groups, 1, LANES)
-    whole = jnp.broadcast_to(whole, (4, groups, T, LANES)).reshape(4, groups * T, LANES)
-    flat = tokens.reshape(PX, channels)
-    gate = jax.nn.silu(jnp.dot(flat, later_weight[:, width:], preferred_element_type=F32))
-    before, after, gate, whole, cst = lax.optimization_barrier((before, after, gate, whole, cst))
+    before, after = neighbours(strip(slice(0, 3)), strip(slice(T - 3, T)), "col")
 
     spec = pl.BlockSpec(memory_space=VMEM)
     params = pltpu.CompilerParams(vmem_limit_bytes=16 * 2**20)
     tile = jax.ShapeDtypeStruct((groups, PX, LANES), F32)
-    padded = jax.ShapeDtypeStruct((groups, PW * PW, LANES), F32)
     spread = jax.ShapeDtypeStruct((PX, LANES), F32)
-    own, partial, g, h = pl.pallas_call(
+    own, gate, cst, whole, g, h, tails = pl.pallas_call(
         inner_kernel,
-        out_shape=(padded, tile, spread, spread),
-        in_specs=[spec] * 6,
-        out_specs=(spec,) * 4,
-        compiler_params=params,
-        cost_estimate=pl.CostEstimate(flops=2 * 352 * channels * width, bytes_accessed=4 * 2**20, transcendentals=0),
+        out_shape=(tile, jax.ShapeDtypeStruct((PX, width), F32), jax.ShapeDtypeStruct((16, width), F32),
+                   jax.ShapeDtypeStruct((4, groups * T, LANES), F32), spread, spread,
+                   jax.ShapeDtypeStruct((2, T, LANES), BF16)),
+        in_specs=[spec] * 7,
+        out_specs=(spec,) * 7,
+        scratch_shapes=[VMEM((groups, PW * PW, LANES), F32)],
+        compiler_params=params,
+        cost_estimate=pl.CostEstimate(flops=2 * 608 * channels * width, bytes_accessed=4 * 2**20, transcendentals=0),
         name="inner",
-    )(above.reshape(3 * T, channels), flat, below.reshape(3 * T, channels), input_weight, kernel, px)
+    )(above.reshape(3 * T, channels), flat, below.reshape(3 * T, channels), input_weight, kernel, table, extra)
     _, local, near = pl.pallas_call(
         conv_scan_kernel,
-        out_shape=(padded, tile, jax.ShapeDtypeStruct((2 * XS, 144, LANES), BF16)),
-        in_specs=[spec] * 10,
+        out_shape=(tile, tile, jax.ShapeDtypeStruct((2 * XS, 144, LANES), BF16)),
+        in_specs=[spec] * 9,
         out_specs=(spec, spec, spec),
-        scratch_shapes=[VMEM((6 * PW, channels), F32), VMEM((PX, LANES), F32), VMEM((2, 128, LANES), F32)],
+        scratch_shapes=[VMEM((6 * PW, channels), F32), VMEM((groups, 6 * PW, LANES), F32),
+                        VMEM((PX, LANES), F32), VMEM((2, 128, LANES), F32)],
         input_output_aliases={8: 0},
         compiler_params=params,
         name="conv_scan",
-    )(before, after, input_weight, kernel, cst, g, h, tails, own, partial)
+    )(before, after, input_weight, kernel, cst, g, h, tails, own)
     near = swap(near, near_groups(rows, cols))
 
     far = pl.pallas_call(

time: 62.4 us -> 61.1 us (0.979)
  other arithmetic: 1.74 us -> 0.08 us
  matrix products: 1.38 us -> 0 us
  blocking collectives: 28 us -> 29.1 us
  Pallas kernels: 5.48 us -> 6.23 us
    dot_general x1 -> x0, matrix products: 1.38 us -> none  [body(): jnp.dot(flat, later_weight[:, width:], preferred_element_type=F32)]
    all_to_all x2, blocking collectives: 28 us -> 29.1 us  [swap(): lax.all_to_all(x, ('row', 'col'), 0, 0, axis_index_groups=groups, tiled=T...]
    slice x1, local copies, waits for them, and re-layouts: 0.9 us -> 0.03 us  [strip(): tokens[:, at]]
    reduce_sum x1 -> x0, other arithmetic: 0.83 us -> none  [body(): jnp.sum(extra, axis=1)]
    unnamed x12 -> x16, local copies, waits for them, and re-layouts: 0.08 us -> 0.85 us
    pallas_call x2, Pallas kernels: 3.65 us -> 4.41 us  [the longest x1 2.62 us: body(): pl.pallas_call(inner_kernel, out_shape=(tile, jax.ShapeDtypeStruct((PX, w...]
    exp x1 -> x0, other arithmetic: 0.72 us -> none  [body(): jnp.exp(-table)]
  transfers between devices with their start and end apart: 5 -> 5, of which waited for: 2 -> 2; matrix products, arithmetic and copies ran while one was open for 6% -> 0% of each run, Pallas kernels for 2% -> 5%
where the time goes in v5:
time: 61.1 us; the launch traced here: 60.7 us
  blocking collectives  29.1 us (48%)
  starting transfers between devices  21.8 us (36%)
  Pallas kernels  6.23 us (10%)
  local copies, waits for them, and re-layouts  1.81 us (3%)
  waiting for transfers between devices  1.52 us (2%)
    all_to_all x2, blocking collectives, swap(): lax.all_to_all(x, ('row', 'col'), 0, 0, axis_index_groups=groups, tiled=T...  29.1 us
    ppermute x1, starting transfers between devices, body(): got = lax.ppermute(give, 'row', [(i, i ^ 1) for i in range(rows)])  11.8 us
    ppermute x4, starting transfers between devices, neighbours(): return (lax.ppermute(x_last, axis, up), lax.ppermute(x_first, axis, down))  9.97 us
    pallas_call x1, Pallas kernels, body(): pl.pallas_call(inner_kernel, out_shape=(tile, jax.ShapeDtypeStruct((PX, w...  2.62 us
    pallas_call x1, Pallas kernels, body(): pl.pallas_call(conv_scan_kernel, out_shape=(tile, tile, jax.ShapeDtypeStr...  1.79 us
    pallas_call x1, Pallas kernels, body(): pl.pallas_call(finish_kernel, out_shape=jax.ShapeDtypeStruct((PX, channel...  1.37 us
  transfers between devices with their start and end apart: 5, of which 2 were waited for; matrix products, arithmetic and copies ran while one was open for 0% of the time, Pallas kernels for 5%

profile of v5, /device:TPU:33, one launch (start us, length us, event | category | flops | bytes accessed | tf_op | source)
XLA Modules:
  0.0 60.7 jit_solution(3696688798712212743)
XLA Ops:
  0.0 0.0 copy-start.1
  0.0 0.0 copy-start
  0.0 0.8 %fusion.1 = (bf16[3,16,256]{2,1,0:T(8,128)(2,1)S(1)}, bf16[3,16,256]{2,1,0:T(8,128)(2,1)S(1)}) fusion(bf16[16,16,256]{2,1,0:T(8,128)(2,1)} %param.6), kind=kLoop, calls=%fused_computation.3 | loop fusion | bytes 98304 | tf_op jit(solution)/shard_map/slice | solution.py:380
  0.8 2.6 %collective-permute-start.1 = (bf16[3,16,256]{2,0,1:T(4,128)(2,1)S(1)}, bf16[3,16,256]{2,0,1:T(4,128)(2,1)S(1)}, u32[]{:S(2)}, u32[]{:S(2)}) collective-permute-start(bf16[3,16,256]{2,0,1:T(4,128)(2,1)S(1)} %copy.18), channel_id=1, source_target_pairs={{32,0},{64,32},{96,64},{128,96},{160,128},{192,160},{224,192},{256... | collective-permute-start | bytes 73736 | tf_op jit(solution)/shard_map/ppermute | solution.py:354
  3.5 3.0 %collective-permute-start = (bf16[3,16,256]{2,0,1:T(4,128)(2,1)S(1)}, bf16[3,16,256]{2,0,1:T(4,128)(2,1)S(1)}, u32[]{:S(2)}, u32[]{:S(2)}) collective-permute-start(bf16[3,16,256]{2,0,1:T(4,128)(2,1)S(1)} %copy.16), channel_id=1, source_target_pairs={{0,32},{32,64},{64,96},{96,128},{128,160},{160,192},{192,224},{224... | collective-permute-start | bytes 73736 | tf_op jit(solution)/shard_map/ppermute | solution.py:354
  6.5 0.0 copy-done.1
  6.5 0.1 pad.7.clone
  6.6 0.0 collective-permute-done.1
  6.6 0.8 %collective-permute-done = bf16[3,16,256]{2,0,1:T(4,128)(2,1)S(1)} collective-permute-done((bf16[3,16,256]{2,0,1:T(4,128)(2,1)S(1)}, bf16[3,16,256]{2,0,1:T(4,128)(2,1)S(1)}, u32[]{:S(2)}, u32[]{:S(2)}) %collective-permute-start) | collective-permute-done | bytes 24608 | tf_op jit(solution)/shard_map/ppermute | solution.py:354
  7.5 0.0 copy-start.2
  7.5 0.1 maximum_maximum_fusion.1
  7.6 3.1 %collective-permute-start.2 = (bf16[72,256]{1,0:T(8,128)(2,1)S(1)}, bf16[72,256]{1,0:T(8,128)(2,1)S(1)}, u32[]{:S(2)}, u32[]{:S(2)}) collective-permute-start(bf16[72,256]{1,0:T(8,128)(2,1)S(1)} %bitcast.15), channel_id=1, source_target_pairs={{0,1},{1,2},{2,3},{3,4},{4,5},{5,6},{6,7},{7,8},{8,9},{9,10},{10,1... | collective-permute-start | bytes 110600 | tf_op jit(solution)/shard_map/ppermute | solution.py:354
  10.7 1.3 %collective-permute-start.3 = (bf16[72,256]{1,0:T(8,128)(2,1)S(1)}, bf16[72,256]{1,0:T(8,128)(2,1)S(1)}, u32[]{:S(2)}, u32[]{:S(2)}) collective-permute-start(bf16[72,256]{1,0:T(8,128)(2,1)S(1)} %bitcast.14), channel_id=1, source_target_pairs={{1,0},{2,1},{3,2},{4,3},{5,4},{6,5},{7,6},{8,7},{9,8},{10,9},{11,1... | collective-permute-start | bytes 110600 | tf_op jit(solution)/shard_map/ppermute | solution.py:354
  12.0 0.0 copy-start.4
  12.0 0.0 copy-start.5
  12.0 0.0 copy-done
  12.0 0.0 copy-done.2
  12.1 0.6 %copy-done.4 = f32[4,512]{1,0:T(4,128)S(1)} copy-done((f32[4,512]{1,0:T(4,128)S(1)}, f32[4,512]{1,0:T(4,128)}, u32[]{:S(2)}) %copy-start.4) | copy-done | bytes 8216
  12.7 0.0 copy-done.5
  12.7 2.6 %inner.1 = (f32[4,256,128]{2,1,0:T(8,128)S(1)}, f32[256,512]{1,0:T(8,128)S(1)}, f32[16,512]{1,0:T(8,128)S(1)}, f32[4,64,128]{2,1,0:T(8,128)S(1)}, f32[256,128]{1...) custom-call(bf16[48,256]{1,0:T(8,128)(2,1)S(1)} %bitcast.13, bf16[256,256]{1,0:T(8,128)(2,1)S(1)} %bitcast.10, ...), custom_call_target="tpu_custom_call" | custom-call | flops 159383552 | bytes 4194304 | tf_op jit(solution)/shard_map/inner/pallas_call | solution.py:393
  15.3 0.0 collective-permute-done.2.before_ref
  15.3 0.0 collective-permute-done.3.after_ref
  15.4 1.8 %conv_scan.1 = (f32[4,256,128]{2,1,0:T(8,128)S(1)}, f32[4,256,128]{2,1,0:T(8,128)S(1)}, bf16[8,144,128]{2,1,0:T(8,128)(2,1)S(1)}) custom-call(bf16[72,256]{1,0:T(8,128)(2,1)S(1)} %collective-permute-done.2.before_ref, bf16[72,256]{1,0:T(8,128)(2,1)S(1)} %collective-permute-done.3.after_ref, ...), custom_call_target="tpu_custom_call", output_to_operand_aliasing={{0}: (8, {})} | custom-call | tf_op jit(solution)/shard_map/conv_scan/pallas_call | solution.py:405
  17.2 18.0 %all_to_all.10.near_ref = bf16[8,144,128]{2,1,0:T(8,128)(2,1)S(1)} all-to-all(bf16[8,144,128]{2,1,0:T(8,128)(2,1)S(1)} %get-tuple-element.21), channel_id=1, replica_groups={{0,1,2,3,32,33,34,35},{4,5,6,7,36,37,38,39},{8,9,10,11,40,41,42,43},{12..., dimensions={0} | all-to-all | bytes 589824 | tf_op jit(solution)/shard_map/all_to_all | solution.py:370
  35.2 0.1 totals.1
  35.3 11.0 %all_to_all.11.far_ref = bf16[8,144,128]{2,1,0:T(8,128)(2,1)S(1)} all-to-all(bf16[8,144,128]{2,1,0:T(8,128)(2,1)S(1)} %totals.1), channel_id=1, replica_groups={{0,4,8,12,16,20,24,28},{1,5,9,13,17,21,25,29},{2,6,10,14,18,22,26,30},{..., dimensions={0} | all-to-all | bytes 589824 | tf_op jit(solution)/shard_map/all_to_all | solution.py:370
  46.4 0.2 enter.1
  46.5 11.8 %collective-permute-start.4 = (bf16[128,128]{1,0:T(8,128)(2,1)S(1)}, bf16[128,128]{1,0:T(8,128)(2,1)S(1)}, u32[]{:S(2)}, u32[]{:S(2)}) collective-permute-start(bf16[128,128]{1,0:T(8,128)(2,1)S(1)} %get-tuple-element.23), channel_id=1, source_target_pairs={{0,32},{32,0},{64,96},{96,64},{128,160},{160,128},{192,224},{224,1... | collective-permute-start | bytes 98312 | tf_op jit(solution)/shard_map/ppermute | solution.py:436
  58.3 0.0 copy-start.3
  58.4 0.2 own_axis.1.sum_ref
  58.5 0.7 %collective-permute-done.4.got_ref = bf16[128,128]{1,0:T(8,128)(2,1)S(1)} collective-permute-done((bf16[128,128]{1,0:T(8,128)(2,1)S(1)}, bf16[128,128]{1,0:T(8,128)(2,1)S(1)}, u32[]{:S(2)}, u32[]{:S(2)}) %collective-permute-start.4) | collective-permute-done | bytes 32800 | tf_op jit(solution)/shard_map/ppermute | solution.py:436
  59.2 0.1 copy-done.3
  59.3 1.4 %finish.1 = bf16[256,256]{1,0:T(8,128)(2,1)} custom-call(bf16[128,128]{1,0:T(8,128)(2,1)S(1)} %collective-permute-done.4.got_ref, f32[16,512]{1,0:T(8,128)S(1)} %get-tuple-element.16.cst_ref, f32[256,128]{1,0:T(8,128)S(1)} %get-tuple-element.17.g_ref, f32[4,256,128]{2,1,0:T(8,128)S(1)} %own_axis.1.sum_ref, f32[256,512]{1,0:T(8,128)S(1)} %get-tuple-element.26.gate_ref, ...), custom_call_target="tpu_custom_call" | custom-call | tf_op jit(solution)/shard_map/finish/pallas_call | solution.py:447
  (10 shorter events, 0.1 us)
Async XLA Ops:
  0.0 6.5 %copy-start.1 = (bf16[16,16,256]{2,1,0:T(8,128)(2,1)S(1)}, bf16[16,16,256]{2,1,0:T(8,128)(2,1)}, u32[]{:S(2)}) copy-start(bf16[16,16,256]{2,1,0:T(8,128)(2,1)} %param.6) | copy-start | bytes 393220
  0.0 12.0 %copy-start = (bf16[256,1024]{1,0:T(8,128)(2,1)S(1)}, bf16[256,1024]{1,0:T(8,128)(2,1)}, u32[]{:S(2)}) copy-start(bf16[256,1024]{1,0:T(8,128)(2,1)} %wv_ref.1) | copy-start | bytes 1572868
  0.8 5.8 %collective-permute-start.1 = (bf16[3,16,256]{2,0,1:T(4,128)(2,1)S(1)}, bf16[3,16,256]{2,0,1:T(4,128)(2,1)S(1)}, u32[]{:S(2)}, u32[]{:S(2)}) collective-permute-start(bf16[3,16,256]{2,0,1:T(4,128)(2,1)S(1)} %copy.18), channel_id=1, source_target_pairs={{32,0},{64,32},{96,64},{128,96},{160,128},{192,160},{224,192},{256... | collective-permute-start | bytes 73736 | tf_op jit(solution)/shard_map/ppermute | solution.py:354
  3.5 4.0 %collective-permute-start = (bf16[3,16,256]{2,0,1:T(4,128)(2,1)S(1)}, bf16[3,16,256]{2,0,1:T(4,128)(2,1)S(1)}, u32[]{:S(2)}, u32[]{:S(2)}) collective-permute-start(bf16[3,16,256]{2,0,1:T(4,128)(2,1)S(1)} %copy.16), channel_id=1, source_target_pairs={{0,32},{32,64},{64,96},{96,128},{128,160},{160,192},{192,224},{224... | collective-permute-start | bytes 73736 | tf_op jit(solution)/shard_map/ppermute | solution.py:354
  7.5 4.6 %copy-start.2 = (f32[7,7,512]{2,1,0:T(8,128)S(1)}, f32[7,7,512]{2,1,0:T(8,128)}, u32[]{:S(2)}) copy-start(f32[7,7,512]{2,1,0:T(8,128)} %taps_ref.3) | copy-start | bytes 301060
  7.6 7.8 %collective-permute-start.2 = (bf16[72,256]{1,0:T(8,128)(2,1)S(1)}, bf16[72,256]{1,0:T(8,128)(2,1)S(1)}, u32[]{:S(2)}, u32[]{:S(2)}) collective-permute-start(bf16[72,256]{1,0:T(8,128)(2,1)S(1)} %bitcast.15), channel_id=1, source_target_pairs={{0,1},{1,2},{2,3},{3,4},{4,5},{5,6},{6,7},{7,8},{8,9},{9,10},{10,1... | collective-permute-start | bytes 110600 | tf_op jit(solution)/shard_map/ppermute | solution.py:354
  10.7 4.7 %collective-permute-start.3 = (bf16[72,256]{1,0:T(8,128)(2,1)S(1)}, bf16[72,256]{1,0:T(8,128)(2,1)S(1)}, u32[]{:S(2)}, u32[]{:S(2)}) collective-permute-start(bf16[72,256]{1,0:T(8,128)(2,1)S(1)} %bitcast.14), channel_id=1, source_target_pairs={{1,0},{2,1},{3,2},{4,3},{5,4},{6,5},{7,6},{8,7},{9,8},{10,9},{11,1... | collective-permute-start | bytes 110600 | tf_op jit(solution)/shard_map/ppermute | solution.py:354
  12.0 0.7 %copy-start.4 = (f32[4,512]{1,0:T(4,128)S(1)}, f32[4,512]{1,0:T(4,128)}, u32[]{:S(2)}) copy-start(f32[4,512]{1,0:T(4,128)} %table_ref.1) | copy-start | bytes 24580
  12.0 0.7 %copy-start.5 = (f32[16,16]{1,0:T(8,128)S(1)}, f32[16,16]{1,0:T(8,128)}, u32[]{:S(2)}) copy-start(f32[16,16]{1,0:T(8,128)} %extra_ref.1) | copy-start | bytes 3076
  46.5 12.7 %collective-permute-start.4 = (bf16[128,128]{1,0:T(8,128)(2,1)S(1)}, bf16[128,128]{1,0:T(8,128)(2,1)S(1)}, u32[]{:S(2)}, u32[]{:S(2)}) collective-permute-start(bf16[128,128]{1,0:T(8,128)(2,1)S(1)} %get-tuple-element.23), channel_id=1, source_target_pairs={{0,32},{32,0},{64,96},{96,64},{128,160},{160,128},{192,224},{224,1... | collective-permute-start | bytes 98312 | tf_op jit(solution)/shard_map/ppermute | solution.py:436
  58.3 1.0 %copy-start.3 = (bf16[512,256]{1,0:T(8,128)(2,1)S(1)}, bf16[512,256]{1,0:T(8,128)(2,1)}, u32[]{:S(2)}) copy-start(bf16[512,256]{1,0:T(8,128)(2,1)} %wo_ref.1) | copy-start | bytes 786436

commit v6 on v5

--- a/solution.py
+++ b/solution.py
@@ -47,7 +47,7 @@
     return jnp.where(x < 0.1, series, 1.0 - jnp.exp(-x))
 
 
-def spread_decays(table_ref, extra_ref, cst_ref, whole_ref, g_ref, h_ref, tails_ref):
+def spread_decays(table_ref, extra_ref, cst_ref, whole_ref, g_ref, tails_ref, flow_refs, h_ref):
     table = table_ref[...]
     cst_ref[0:4] = jnp.exp(-table)
     cst_ref[4:8] = fall(2.0 * table)
@@ -74,11 +74,21 @@
         high = decay.astype(BF16).astype(F32)
         tails_ref[k] = jnp.where(lane < 64, high, decay - high).astype(BF16)
 
+    def group(ct, carry):
+        lanes = pl.ds(pl.multiple_of(ct * LANES, LANES), LANES)
+        for d in range(4):
+            base, slope = cst_ref[pl.ds(4 + d, 1), lanes], cst_ref[pl.ds(8 + d, 1), lanes]
+            q = base + slope * h_ref[...]
+            flow_refs[d // 2][d % 2, ct] = q * lax.rsqrt(q)
+        return carry
+
+    lax.fori_loop(0, flow_refs[0].shape[1], group, 0)
+
 
 def inner_kernel(above_ref, tok_ref, below_ref, weight_ref, taps_ref, table_ref, extra_ref,
-                 acc_ref, gate_ref, cst_ref, whole_ref, g_ref, h_ref, tails_ref, v_ref):
+                 acc_ref, gate_ref, cst_ref, whole_ref, g_ref, tails_ref, along_ref, down_ref, v_ref, h_ref):
     groups = v_ref.shape[0]
-    spread_decays(table_ref, extra_ref, cst_ref, whole_ref, g_ref, h_ref, tails_ref)
+    spread_decays(table_ref, extra_ref, cst_ref, whole_ref, g_ref, tails_ref, (along_ref, down_ref), h_ref)
     for ct in range(groups):
         for j in (0, 1, 2, T + 3, T + 4, T + 5):
             v_ref[ct, pl.ds(j, PW, stride=PW), :] = jnp.zeros((PW, LANES), F32)
@@ -107,8 +117,8 @@
     lax.fori_loop(0, groups, group, 0)
 
 
-def conv_scan_kernel(before_ref, after_ref, wv_ref, taps_ref, cst_ref, g_ref, h_ref, tails_ref, own_ref,
-                     acc_ref, sum_ref, near_ref, side_ref, line_ref, val_ref, end_ref):
+def conv_scan_kernel(before_ref, after_ref, wv_ref, taps_ref, cst_ref, g_ref, along_ref, down_ref, tails_ref,
+                     own_ref, acc_ref, sum_ref, near_ref, side_ref, line_ref, val_ref, end_ref):
     del own_ref
     groups = line_ref.shape[0]
     side_ref[0:3 * PW] = before_ref[...].astype(F32)
@@ -121,11 +131,10 @@
 
     def group(ct, carry):
         lanes = pl.ds(pl.multiple_of(ct * LANES, LANES), LANES)
-        cst = [cst_ref[pl.ds(k, 1), lanes] for k in range(12)]
-
-        def flow(d, g, h, x):
-            q = cst[4 + d] + cst[8 + d] * h
-            return cst[d] * g, q * lax.rsqrt(q) * x
+        cst = [cst_ref[pl.ds(k, 1), lanes] for k in range(4)]
+
+        def flow(d, at, x):
+            return cst[d] * g_ref[at, :], (along_ref, down_ref)[d // 2][d % 2, ct, at, :] * x
 
         for side in range(2):
             outs = range(3) if side == 0 else range(T - 3, T)
@@ -152,14 +161,14 @@
             downs = []
             for i in range(T):
                 at = pl.ds(i * T + jt * 8, 8)
-                d, f = flow(2, g_ref[at, :], h_ref[at, :], vals[i])
+                d, f = flow(2, at, vals[i])
                 state = d * state + f
                 downs.append(state)
             end_ref[1, pl.ds(0 + ct * T + jt * 8, 8), :] = state
             state = jnp.zeros((8, LANES), F32)
             for i in reversed(range(T)):
                 at = pl.ds(i * T + jt * 8, 8)
-                d, f = flow(3, g_ref[at, :], h_ref[at, :], vals[i])
+                d, f = flow(3, at, vals[i])
                 state = d * state + f
                 sum_ref[ct, at, :] = downs[i] + state
             end_ref[1, pl.ds(64 + ct * T + jt * 8, 8), :] = state
@@ -168,14 +177,14 @@
             lefts = []
             for j in range(T):
                 at = pl.ds(it * 8 * T + j, 8, stride=T)
-                d, f = flow(0, g_ref[at, :], h_ref[at, :], val_ref[at, :])
+                d, f = flow(0, at, val_ref[at, :])
                 state = d * state + f
                 lefts.append(state)
             end_ref[0, pl.ds(0 + ct * T + it * 8, 8), :] = state
             state = jnp.zeros((8, LANES), F32)
             for j in reversed(range(T)):
                 at = pl.ds(it * 8 * T + j, 8, stride=T)
-                d, f = flow(1, g_ref[at, :], h_ref[at, :], val_ref[at, :])
+                d, f = flow(1, at, val_ref[at, :])
                 state = d * state + f
                 sum_ref[ct, at, :] = sum_ref[ct, at, :] + (lefts[j] + state)
             end_ref[0, pl.ds(64 + ct * T + it * 8, 8), :] = state
@@ -389,15 +398,16 @@
     spec = pl.BlockSpec(memory_space=VMEM)
     params = pltpu.CompilerParams(vmem_limit_bytes=16 * 2**20)
     tile = jax.ShapeDtypeStruct((groups, PX, LANES), F32)
-    spread = jax.ShapeDtypeStruct((PX, LANES), F32)
-    own, gate, cst, whole, g, h, tails = pl.pallas_call(
+    factor = jax.ShapeDtypeStruct((2, groups, PX, LANES), F32)
+    own, gate, cst, whole, g, tails, along, downward = pl.pallas_call(
         inner_kernel,
         out_shape=(tile, jax.ShapeDtypeStruct((PX, width), F32), jax.ShapeDtypeStruct((16, width), F32),
-                   jax.ShapeDtypeStruct((4, groups * T, LANES), F32), spread, spread,
-                   jax.ShapeDtypeStruct((2, T, LANES), BF16)),
+                   jax.ShapeDtypeStruct((4, groups * T, LANES), F32),
+                   jax.ShapeDtypeStruct((PX, LANES), F32), jax.ShapeDtypeStruct((2, T, LANES), BF16),
+                   factor, factor),
         in_specs=[spec] * 7,
-        out_specs=(spec,) * 7,
-        scratch_shapes=[VMEM((groups, PW * PW, LANES), F32)],
+        out_specs=(spec,) * 8,
+        scratch_shapes=[VMEM((groups, PW * PW, LANES), F32), VMEM((PX, LANES), F32)],
         compiler_params=params,
         cost_estimate=pl.CostEstimate(flops=2 * 608 * channels * width, bytes_accessed=4 * 2**20, transcendentals=0),
         name="inner",
@@ -405,14 +415,14 @@
     _, local, near = pl.pallas_call(
         conv_scan_kernel,
         out_shape=(tile, tile, jax.ShapeDtypeStruct((2 * XS, 144, LANES), BF16)),
-        in_specs=[spec] * 9,
+        in_specs=[spec] * 10,
         out_specs=(spec, spec, spec),
         scratch_shapes=[VMEM((6 * PW, channels), F32), VMEM((groups, 6 * PW, LANES), F32),
                         VMEM((PX, LANES), F32), VMEM((2, 128, LANES), F32)],
-        input_output_aliases={8: 0},
+        input_output_aliases={9: 0},
         compiler_params=params,
         name="conv_scan",
-    )(before, after, input_weight, kernel, cst, g, h, tails, own)
+    )(before, after, input_weight, kernel, cst, g, along, downward, tails, own)
     near = swap(near, near_groups(rows, cols))
 
     far = pl.pallas_call(

time: 61.1 us -> 61 us (level)
  no operation moved by 1% of the time
where the time goes in v6:
time: 61 us; the launch traced here: 60.6 us
  blocking collectives  28.6 us (47%)
  starting transfers between devices  21.8 us (36%)
  Pallas kernels  6.63 us (11%)
  local copies, waits for them, and re-layouts  1.81 us (3%)
  waiting for transfers between devices  1.49 us (2%)
    all_to_all x2, blocking collectives, swap(): lax.all_to_all(x, ('row', 'col'), 0, 0, axis_index_groups=groups, tiled=T...  28.6 us
    ppermute x1, starting transfers between devices, body(): got = lax.ppermute(give, 'row', [(i, i ^ 1) for i in range(rows)])  11.8 us
    ppermute x4, starting transfers between devices, neighbours(): return (lax.ppermute(x_last, axis, up), lax.ppermute(x_first, axis, down))  9.97 us
    pallas_call x1, Pallas kernels, body(): pl.pallas_call(inner_kernel, out_shape=(tile, jax.ShapeDtypeStruct((PX, w...  3.07 us
    pallas_call x1, Pallas kernels, body(): pl.pallas_call(conv_scan_kernel, out_shape=(tile, tile, jax.ShapeDtypeStr...  1.74 us
    pallas_call x1, Pallas kernels, body(): pl.pallas_call(finish_kernel, out_shape=jax.ShapeDtypeStruct((PX, channel...  1.38 us
  transfers between devices with their start and end apart: 5, of which 2 were waited for; matrix products, arithmetic and copies ran while one was open for 0% of the time, Pallas kernels for 5%

profile of v6, /device:TPU:33, one launch (start us, length us, event | category | flops | bytes accessed | tf_op | source)
XLA Modules:
  0.0 60.6 jit_solution(15753828725910464084)
XLA Ops:
  0.0 0.0 copy-start.1
  0.0 0.0 copy-start
  0.0 0.8 %fusion.1 = (bf16[3,16,256]{2,1,0:T(8,128)(2,1)S(1)}, bf16[3,16,256]{2,1,0:T(8,128)(2,1)S(1)}) fusion(bf16[16,16,256]{2,1,0:T(8,128)(2,1)} %param.6), kind=kLoop, calls=%fused_computation.3 | loop fusion | bytes 98304 | tf_op jit(solution)/shard_map/slice | solution.py:389
  0.8 2.6 %collective-permute-start.1 = (bf16[3,16,256]{2,0,1:T(4,128)(2,1)S(1)}, bf16[3,16,256]{2,0,1:T(4,128)(2,1)S(1)}, u32[]{:S(2)}, u32[]{:S(2)}) collective-permute-start(bf16[3,16,256]{2,0,1:T(4,128)(2,1)S(1)} %copy.18), channel_id=1, source_target_pairs={{32,0},{64,32},{96,64},{128,96},{160,128},{192,160},{224,192},{256... | collective-permute-start | bytes 73736 | tf_op jit(solution)/shard_map/ppermute | solution.py:363
  3.5 3.0 %collective-permute-start = (bf16[3,16,256]{2,0,1:T(4,128)(2,1)S(1)}, bf16[3,16,256]{2,0,1:T(4,128)(2,1)S(1)}, u32[]{:S(2)}, u32[]{:S(2)}) collective-permute-start(bf16[3,16,256]{2,0,1:T(4,128)(2,1)S(1)} %copy.16), channel_id=1, source_target_pairs={{0,32},{32,64},{64,96},{96,128},{128,160},{160,192},{192,224},{224... | collective-permute-start | bytes 73736 | tf_op jit(solution)/shard_map/ppermute | solution.py:363
  6.5 0.0 copy-done.1
  6.5 0.1 pad.7.clone
  6.6 0.0 collective-permute-done.1
  6.6 0.8 %collective-permute-done = bf16[3,16,256]{2,0,1:T(4,128)(2,1)S(1)} collective-permute-done((bf16[3,16,256]{2,0,1:T(4,128)(2,1)S(1)}, bf16[3,16,256]{2,0,1:T(4,128)(2,1)S(1)}, u32[]{:S(2)}, u32[]{:S(2)}) %collective-permute-start) | collective-permute-done | bytes 24608 | tf_op jit(solution)/shard_map/ppermute | solution.py:363
  7.5 0.0 copy-start.2
  7.5 0.1 maximum_maximum_fusion.1
  7.6 3.1 %collective-permute-start.2 = (bf16[72,256]{1,0:T(8,128)(2,1)S(1)}, bf16[72,256]{1,0:T(8,128)(2,1)S(1)}, u32[]{:S(2)}, u32[]{:S(2)}) collective-permute-start(bf16[72,256]{1,0:T(8,128)(2,1)S(1)} %bitcast.15), channel_id=1, source_target_pairs={{0,1},{1,2},{2,3},{3,4},{4,5},{5,6},{6,7},{7,8},{8,9},{9,10},{10,1... | collective-permute-start | bytes 110600 | tf_op jit(solution)/shard_map/ppermute | solution.py:363
  10.7 1.3 %collective-permute-start.3 = (bf16[72,256]{1,0:T(8,128)(2,1)S(1)}, bf16[72,256]{1,0:T(8,128)(2,1)S(1)}, u32[]{:S(2)}, u32[]{:S(2)}) collective-permute-start(bf16[72,256]{1,0:T(8,128)(2,1)S(1)} %bitcast.14), channel_id=1, source_target_pairs={{1,0},{2,1},{3,2},{4,3},{5,4},{6,5},{7,6},{8,7},{9,8},{10,9},{11,1... | collective-permute-start | bytes 110600 | tf_op jit(solution)/shard_map/ppermute | solution.py:363
  12.0 0.0 copy-start.4
  12.0 0.0 copy-start.5
  12.0 0.0 copy-done
  12.0 0.0 copy-done.2
  12.1 0.6 %copy-done.4 = f32[4,512]{1,0:T(4,128)S(1)} copy-done((f32[4,512]{1,0:T(4,128)S(1)}, f32[4,512]{1,0:T(4,128)}, u32[]{:S(2)}) %copy-start.4) | copy-done | bytes 8216
  12.7 0.0 copy-done.5
  12.7 3.1 %inner.1 = (f32[4,256,128]{2,1,0:T(8,128)S(1)}, f32[256,512]{1,0:T(8,128)S(1)}, f32[16,512]{1,0:T(8,128)S(1)}, f32[4,64,128]{2,1,0:T(8,128)S(1)}, f32[256,128]{1...) custom-call(bf16[48,256]{1,0:T(8,128)(2,1)S(1)} %bitcast.13, ...), custom_call_target="tpu_custom_call" | custom-call | flops 159383552 | bytes 4194304 | tf_op jit(solution)/shard_map/inner/pallas_call | solution.py:402
  15.8 0.0 collective-permute-done.2.before_ref
  15.8 0.0 collective-permute-done.3.after_ref
  15.8 1.7 %conv_scan.1 = (f32[4,256,128]{2,1,0:T(8,128)S(1)}, f32[4,256,128]{2,1,0:T(8,128)S(1)}, bf16[8,144,128]{2,1,0:T(8,128)(2,1)S(1)}) custom-call(bf16[72,256]{1,0:T(8,128)(2,1)S(1)} %collective-permute-done.2.before_ref, bf16[72,256]{1,0:T(8,128)(2,1)S(1)} %collective-permute-done.3.after_ref, ...), custom_call_target="tpu_custom_call", output_to_operand_aliasing={{0}: (9, {})} | custom-call | tf_op jit(solution)/shard_map/conv_scan/pallas_call | solution.py:415
  17.6 17.6 %all_to_all.10.near_ref = bf16[8,144,128]{2,1,0:T(8,128)(2,1)S(1)} all-to-all(bf16[8,144,128]{2,1,0:T(8,128)(2,1)S(1)} %get-tuple-element.23), channel_id=1, replica_groups={{0,1,2,3,32,33,34,35},{4,5,6,7,36,37,38,39},{8,9,10,11,40,41,42,43},{12..., dimensions={0} | all-to-all | bytes 589824 | tf_op jit(solution)/shard_map/all_to_all | solution.py:379
  35.1 0.1 totals.1
  35.3 11.0 %all_to_all.11.far_ref = bf16[8,144,128]{2,1,0:T(8,128)(2,1)S(1)} all-to-all(bf16[8,144,128]{2,1,0:T(8,128)(2,1)S(1)} %totals.1), channel_id=1, replica_groups={{0,4,8,12,16,20,24,28},{1,5,9,13,17,21,25,29},{2,6,10,14,18,22,26,30},{..., dimensions={0} | all-to-all | bytes 589824 | tf_op jit(solution)/shard_map/all_to_all | solution.py:379
  46.3 0.2 enter.1
  46.5 11.8 %collective-permute-start.4 = (bf16[128,128]{1,0:T(8,128)(2,1)S(1)}, bf16[128,128]{1,0:T(8,128)(2,1)S(1)}, u32[]{:S(2)}, u32[]{:S(2)}) collective-permute-start(bf16[128,128]{1,0:T(8,128)(2,1)S(1)} %get-tuple-element.25), channel_id=1, source_target_pairs={{0,32},{32,0},{64,96},{96,64},{128,160},{160,128},{192,224},{224,1... | collective-permute-start | bytes 98312 | tf_op jit(solution)/shard_map/ppermute | solution.py:446
  58.3 0.0 copy-start.3
  58.3 0.2 own_axis.1.sum_ref
  58.5 0.7 %collective-permute-done.4.got_ref = bf16[128,128]{1,0:T(8,128)(2,1)S(1)} collective-permute-done((bf16[128,128]{1,0:T(8,128)(2,1)S(1)}, bf16[128,128]{1,0:T(8,128)(2,1)S(1)}, u32[]{:S(2)}, u32[]{:S(2)}) %collective-permute-start.4) | collective-permute-done | bytes 32800 | tf_op jit(solution)/shard_map/ppermute | solution.py:446
  59.1 0.1 copy-done.3
  59.2 1.4 %finish.1 = bf16[256,256]{1,0:T(8,128)(2,1)} custom-call(bf16[128,128]{1,0:T(8,128)(2,1)S(1)} %collective-permute-done.4.got_ref, f32[16,512]{1,0:T(8,128)S(1)} %get-tuple-element.17.cst_ref, f32[256,128]{1,0:T(8,128)S(1)} %get-tuple-element.18.g_ref, f32[4,256,128]{2,1,0:T(8,128)S(1)} %own_axis.1.sum_ref, f32[256,512]{1,0:T(8,128)S(1)} %get-tuple-element.28.gate_ref, ...), custom_call_target="tpu_custom_call" | custom-call | tf_op jit(solution)/shard_map/finish/pallas_call | solution.py:457
  (10 shorter events, 0.1 us)
Async XLA Ops:
  0.0 6.5 %copy-start.1 = (bf16[16,16,256]{2,1,0:T(8,128)(2,1)S(1)}, bf16[16,16,256]{2,1,0:T(8,128)(2,1)}, u32[]{:S(2)}) copy-start(bf16[16,16,256]{2,1,0:T(8,128)(2,1)} %param.6) | copy-start | bytes 393220
  0.0 12.0 %copy-start = (bf16[256,1024]{1,0:T(8,128)(2,1)S(1)}, bf16[256,1024]{1,0:T(8,128)(2,1)}, u32[]{:S(2)}) copy-start(bf16[256,1024]{1,0:T(8,128)(2,1)} %wv_ref.1) | copy-start | bytes 1572868
  0.8 5.8 %collective-permute-start.1 = (bf16[3,16,256]{2,0,1:T(4,128)(2,1)S(1)}, bf16[3,16,256]{2,0,1:T(4,128)(2,1)S(1)}, u32[]{:S(2)}, u32[]{:S(2)}) collective-permute-start(bf16[3,16,256]{2,0,1:T(4,128)(2,1)S(1)} %copy.18), channel_id=1, source_target_pairs={{32,0},{64,32},{96,64},{128,96},{160,128},{192,160},{224,192},{256... | collective-permute-start | bytes 73736 | tf_op jit(solution)/shard_map/ppermute | solution.py:363
  3.5 4.0 %collective-permute-start = (bf16[3,16,256]{2,0,1:T(4,128)(2,1)S(1)}, bf16[3,16,256]{2,0,1:T(4,128)(2,1)S(1)}, u32[]{:S(2)}, u32[]{:S(2)}) collective-permute-start(bf16[3,16,256]{2,0,1:T(4,128)(2,1)S(1)} %copy.16), channel_id=1, source_target_pairs={{0,32},{32,64},{64,96},{96,128},{128,160},{160,192},{192,224},{224... | collective-permute-start | bytes 73736 | tf_op jit(solution)/shard_map/ppermute | solution.py:363
  7.5 4.6 %copy-start.2 = (f32[7,7,512]{2,1,0:T(8,128)S(1)}, f32[7,7,512]{2,1,0:T(8,128)}, u32[]{:S(2)}) copy-start(f32[7,7,512]{2,1,0:T(8,128)} %taps_ref.3) | copy-start | bytes 301060
  7.6 8.2 %collective-permute-start.2 = (bf16[72,256]{1,0:T(8,128)(2,1)S(1)}, bf16[72,256]{1,0:T(8,128)(2,1)S(1)}, u32[]{:S(2)}, u32[]{:S(2)}) collective-permute-start(bf16[72,256]{1,0:T(8,128)(2,1)S(1)} %bitcast.15), channel_id=1, source_target_pairs={{0,1},{1,2},{2,3},{3,4},{4,5},{5,6},{6,7},{7,8},{8,9},{9,10},{10,1... | collective-permute-start | bytes 110600 | tf_op jit(solution)/shard_map/ppermute | solution.py:363
  10.7 5.1 %collective-permute-start.3 = (bf16[72,256]{1,0:T(8,128)(2,1)S(1)}, bf16[72,256]{1,0:T(8,128)(2,1)S(1)}, u32[]{:S(2)}, u32[]{:S(2)}) collective-permute-start(bf16[72,256]{1,0:T(8,128)(2,1)S(1)} %bitcast.14), channel_id=1, source_target_pairs={{1,0},{2,1},{3,2},{4,3},{5,4},{6,5},{7,6},{8,7},{9,8},{10,9},{11,1... | collective-permute-start | bytes 110600 | tf_op jit(solution)/shard_map/ppermute | solution.py:363
  12.0 0.7 %copy-start.4 = (f32[4,512]{1,0:T(4,128)S(1)}, f32[4,512]{1,0:T(4,128)}, u32[]{:S(2)}) copy-start(f32[4,512]{1,0:T(4,128)} %table_ref.1) | copy-start | bytes 24580
  12.0 0.7 %copy-start.5 = (f32[16,16]{1,0:T(8,128)S(1)}, f32[16,16]{1,0:T(8,128)}, u32[]{:S(2)}) copy-start(f32[16,16]{1,0:T(8,128)} %extra_ref.1) | copy-start | bytes 3076
  46.5 12.7 %collective-permute-start.4 = (bf16[128,128]{1,0:T(8,128)(2,1)S(1)}, bf16[128,128]{1,0:T(8,128)(2,1)S(1)}, u32[]{:S(2)}, u32[]{:S(2)}) collective-permute-start(bf16[128,128]{1,0:T(8,128)(2,1)S(1)} %get-tuple-element.25), channel_id=1, source_target_pairs={{0,32},{32,0},{64,96},{96,64},{128,160},{160,128},{192,224},{224,1... | collective-permute-start | bytes 98312 | tf_op jit(solution)/shard_map/ppermute | solution.py:446
  58.3 1.0 %copy-start.3 = (bf16[512,256]{1,0:T(8,128)(2,1)S(1)}, bf16[512,256]{1,0:T(8,128)(2,1)}, u32[]{:S(2)}) copy-start(bf16[512,256]{1,0:T(8,128)(2,1)} %wo_ref.1) | copy-start | bytes 786436

commit v7 on v5

--- a/solution.py
+++ b/solution.py
@@ -33,7 +33,7 @@
     for b in shifts:
         tap = [taps_ref[a, pl.ds(b, 1), lanes] for a in range(7)]
         tap = [jnp.broadcast_to(t, (8, LANES)) for t in tap]
-        for r in range(T + 6):
+        for r in range(3, T + 3):
             x = v_ref[ct, pl.ds(r * PW + jt * 8 + b, 8), :]
             for a in range(7):
                 i = r - a
@@ -75,19 +75,42 @@
         tails_ref[k] = jnp.where(lane < 64, high, decay - high).astype(BF16)
 
 
-def inner_kernel(above_ref, tok_ref, below_ref, weight_ref, taps_ref, table_ref, extra_ref,
-                 acc_ref, gate_ref, cst_ref, whole_ref, g_ref, h_ref, tails_ref, v_ref):
+def own_kernel(tok_ref, weight_ref, taps_ref, acc_ref, v_ref):
+    groups = v_ref.shape[0]
+    for ct in range(groups):
+        for j in (0, 1, 2, T + 3, T + 4, T + 5):
+            v_ref[ct, pl.ds(j, PW, stride=PW), :] = jnp.zeros((PW, LANES), F32)
+
+    def store(ct, p):
+        for i in range(T):
+            v_ref[ct, pl.ds((3 + i) * PW + 3, T), :] = p[i * T:(i + 1) * T]
+
+    project(tok_ref[...], weight_ref, store)
+
+    def group(ct, carry):
+        lanes = pl.ds(pl.multiple_of(ct * LANES, LANES), LANES)
+        for jt in range(2):
+            acc = add_taps([None] * T, v_ref, taps_ref, ct, lanes, jt, range(7))
+            for i in range(T):
+                acc_ref[ct, pl.ds(i * T + jt * 8, 8), :] = acc[i]
+        return carry
+
+    lax.fori_loop(0, groups, group, 0)
+
+
+def rows_kernel(above_ref, below_ref, tok_ref, weight_ref, taps_ref, table_ref, extra_ref, own_ref,
+                acc_ref, gate_ref, cst_ref, whole_ref, g_ref, h_ref, tails_ref, v_ref):
+    del own_ref
     groups = v_ref.shape[0]
     spread_decays(table_ref, extra_ref, cst_ref, whole_ref, g_ref, h_ref, tails_ref)
     for ct in range(groups):
         for j in (0, 1, 2, T + 3, T + 4, T + 5):
-            v_ref[ct, pl.ds(j, PW, stride=PW), :] = jnp.zeros((PW, LANES), F32)
-    for ref, first in ((above_ref, 0), (tok_ref, 3), (below_ref, T + 3)):
-        count = ref.shape[0] // T
-
-        def store(ct, p, first=first, count=count):
-            for i in range(count):
-                v_ref[ct, pl.ds((first + i) * PW + 3, T), :] = p[i * T:(i + 1) * T]
+            v_ref[ct, pl.ds(j, 8, stride=PW), :] = jnp.zeros((8, LANES), F32)
+    for ref, first in ((above_ref, 0), (below_ref, 3)):
+
+        def store(ct, p, first=first):
+            for k in range(3):
+                v_ref[ct, pl.ds((first + k) * PW + 3, T), :] = p[k * T:(k + 1) * T]
 
         project(ref[...], weight_ref, store)
     width = groups * LANES
@@ -99,8 +122,16 @@
     def group(ct, carry):
         lanes = pl.ds(pl.multiple_of(ct * LANES, LANES), LANES)
         for jt in range(2):
-            acc = add_taps([None] * T, v_ref, taps_ref, ct, lanes, jt, range(7))
-            for i in range(T):
+            outs = (0, 1, 2, T - 3, T - 2, T - 1)
+            acc = {i: acc_ref[ct, pl.ds(i * T + jt * 8, 8), :] for i in outs}
+            for b in range(7):
+                for k in range(6):
+                    row = k if k < 3 else T + k
+                    x = v_ref[ct, pl.ds(k * PW + jt * 8 + b, 8), :]
+                    for i in outs:
+                        if 0 <= row - i < 7:
+                            acc[i] = acc[i] + taps_ref[row - i, pl.ds(b, 1), lanes] * x
+            for i in outs:
                 acc_ref[ct, pl.ds(i * T + jt * 8, 8), :] = acc[i]
         return carry
 
@@ -384,24 +415,36 @@
                              jnp.zeros((PW - T - 6, 3, channels), BF16)], axis=0)
         return x.transpose(1, 0, 2).reshape(3 * PW, channels)
 
-    before, after = neighbours(strip(slice(0, 3)), strip(slice(T - 3, T)), "col")
-
     spec = pl.BlockSpec(memory_space=VMEM)
     params = pltpu.CompilerParams(vmem_limit_bytes=16 * 2**20)
     tile = jax.ShapeDtypeStruct((groups, PX, LANES), F32)
     spread = jax.ShapeDtypeStruct((PX, LANES), F32)
+    own = pl.pallas_call(
+        own_kernel,
+        out_shape=tile,
+        in_specs=[spec] * 3,
+        out_specs=spec,
+        scratch_shapes=[VMEM((groups, PW * PW, LANES), F32)],
+        compiler_params=params,
+        cost_estimate=pl.CostEstimate(flops=2 * PX * channels * width, bytes_accessed=3 * 2**20, transcendentals=0),
+        name="own",
+    )(flat, input_weight, kernel)
+    first, last, own = lax.optimization_barrier((strip(slice(0, 3)), strip(slice(T - 3, T)), own))
+    before, after = neighbours(first, last, "col")
+
     own, gate, cst, whole, g, h, tails = pl.pallas_call(
-        inner_kernel,
+        rows_kernel,
         out_shape=(tile, jax.ShapeDtypeStruct((PX, width), F32), jax.ShapeDtypeStruct((16, width), F32),
                    jax.ShapeDtypeStruct((4, groups * T, LANES), F32), spread, spread,
                    jax.ShapeDtypeStruct((2, T, LANES), BF16)),
-        in_specs=[spec] * 7,
+        in_specs=[spec] * 8,
         out_specs=(spec,) * 7,
-        scratch_shapes=[VMEM((groups, PW * PW, LANES), F32)],
-        compiler_params=params,
-        cost_estimate=pl.CostEstimate(flops=2 * 608 * channels * width, bytes_accessed=4 * 2**20, transcendentals=0),
-        name="inner",
-    )(above.reshape(3 * T, channels), flat, below.reshape(3 * T, channels), input_weight, kernel, table, extra)
+        scratch_shapes=[VMEM((groups, 8 * PW, LANES), F32)],
+        input_output_aliases={7: 0},
+        compiler_params=params,
+        cost_estimate=pl.CostEstimate(flops=2 * PX * channels * width, bytes_accessed=2**20, transcendentals=0),
+        name="rows",
+    )(above.reshape(3 * T, channels), below.reshape(3 * T, channels), flat, input_weight, kernel, table, extra, own)
     _, local, near = pl.pallas_call(
         conv_scan_kernel,
         out_shape=(tile, tile, jax.ShapeDtypeStruct((2 * XS, 144, LANES), BF16)),

time: 61.1 us -> 61.8 us (1.011)
  the two profiles are of different devices: /device:TPU:33 before, /device:TPU:1 now
where the time goes in v7:
time: 61.8 us; the launch traced here: 61.3 us
  blocking collectives  29.5 us (48%)
  starting transfers between devices  19.6 us (32%)
  Pallas kernels  6.47 us (10%)
  local copies, waits for them, and re-layouts  2.86 us (5%)
  waiting for transfers between devices  2.56 us (4%)
    all_to_all x2, blocking collectives, swap(): lax.all_to_all(x, ('row', 'col'), 0, 0, axis_index_groups=groups, tiled=T...  29.5 us
    ppermute x4, starting transfers between devices, neighbours(): return (lax.ppermute(x_last, axis, up), lax.ppermute(x_first, axis, down))  13.4 us
    ppermute x1, starting transfers between devices, body(): got = lax.ppermute(give, 'row', [(i, i ^ 1) for i in range(rows)])  6.22 us
    pallas_call x1, Pallas kernels, body(): pl.pallas_call(own_kernel, out_shape=tile, in_specs=[spec] * 3, out_specs...  2.1 us
    unnamed x18, local copies, waits for them, and re-layouts  1.91 us
    ppermute x4, waiting for transfers between devices, neighbours(): return (lax.ppermute(x_last, axis, up), lax.ppermute(x_first, axis, down))  1.91 us
    pallas_call x1, Pallas kernels, body(): pl.pallas_call(conv_scan_kernel, out_shape=(tile, tile, jax.ShapeDtypeStr...  1.79 us
    pallas_call x1, Pallas kernels, body(): pl.pallas_call(finish_kernel, out_shape=jax.ShapeDtypeStruct((PX, channel...  1.38 us
  transfers between devices with their start and end apart: 5, of which 2 were waited for; matrix products, arithmetic and copies ran while one was open for 0% of the time, Pallas kernels for 5%

profile of v7, /device:TPU:1, one launch (start us, length us, event | category | flops | bytes accessed | tf_op | source)
XLA Modules:
  0.0 61.3 jit_solution(5665180618184193679)
XLA Ops:
  0.0 0.0 copy-start.2
  0.0 0.8 %fusion.1 = (bf16[3,16,256]{2,1,0:T(8,128)(2,1)S(1)}, bf16[3,16,256]{2,1,0:T(8,128)(2,1)S(1)}) fusion(bf16[16,16,256]{2,1,0:T(8,128)(2,1)} %param.6), kind=kLoop, calls=%fused_computation.3 | loop fusion | bytes 98304 | tf_op jit(solution)/shard_map/slice | solution.py:411
  0.8 8.8 %collective-permute-start.1 = (bf16[3,16,256]{2,0,1:T(4,128)(2,1)S(1)}, bf16[3,16,256]{2,0,1:T(4,128)(2,1)S(1)}, u32[]{:S(2)}, u32[]{:S(2)}) collective-permute-start(bf16[3,16,256]{2,0,1:T(4,128)(2,1)S(1)} %copy.19), channel_id=1, source_target_pairs={{32,0},{64,32},{96,64},{128,96},{160,128},{192,160},{224,192},{256... | collective-permute-start | bytes 73736 | tf_op jit(solution)/shard_map/ppermute | solution.py:385
  9.7 0.0 copy-start.3
  9.7 2.1 %collective-permute-start = (bf16[3,16,256]{2,0,1:T(4,128)(2,1)S(1)}, bf16[3,16,256]{2,0,1:T(4,128)(2,1)S(1)}, u32[]{:S(2)}, u32[]{:S(2)}) collective-permute-start(bf16[3,16,256]{2,0,1:T(4,128)(2,1)S(1)} %copy.17), channel_id=1, source_target_pairs={{0,32},{32,64},{64,96},{96,128},{128,160},{160,192},{192,224},{224... | collective-permute-start | bytes 73736 | tf_op jit(solution)/shard_map/ppermute | solution.py:385
  11.7 0.0 copy-done.2
  11.8 0.1 pad.7.clone
  11.9 0.0 copy-done.3
  11.9 0.0 copy-start
  11.9 1.0 %copy-done = bf16[256,1024]{1,0:T(8,128)(2,1)S(1)} copy-done((bf16[256,1024]{1,0:T(8,128)(2,1)S(1)}, bf16[256,1024]{1,0:T(8,128)(2,1)}, u32[]{:S(2)}) %copy-start) | copy-done | bytes 524312
  12.9 2.1 %own.1.own_ref = f32[4,256,128]{2,1,0:T(8,128)S(1)} custom-call(bf16[256,256]{1,0:T(8,128)(2,1)S(1)} %bitcast.10, bf16[256,1024]{1,0:T(8,128)(2,1)S(1)} %copy-done, f32[7,7,512]{2,1,0:T(8,128)S(1)} %copy-done.3), custom_call_target="tpu_custom_call" | custom-call | flops 67108864 | bytes 3145728 | tf_op jit(solution)/shard_map/own/pallas_call | solution.py:422
  15.0 0.0 collective-permute-done.1
  15.1 0.0 collective-permute-done
  15.1 0.1 maximum_maximum_fusion.1
  15.2 1.3 %collective-permute-start.2 = (bf16[72,256]{1,0:T(8,128)(2,1)S(1)}, bf16[72,256]{1,0:T(8,128)(2,1)S(1)}, u32[]{:S(2)}, u32[]{:S(2)}) collective-permute-start(bf16[72,256]{1,0:T(8,128)(2,1)S(1)} %bitcast.16), channel_id=1, source_target_pairs={{0,1},{1,2},{2,3},{3,4},{4,5},{5,6},{6,7},{7,8},{8,9},{9,10},{10,1... | collective-permute-start | bytes 110600 | tf_op jit(solution)/shard_map/ppermute | solution.py:385
  16.5 1.3 %collective-permute-start.3 = (bf16[72,256]{1,0:T(8,128)(2,1)S(1)}, bf16[72,256]{1,0:T(8,128)(2,1)S(1)}, u32[]{:S(2)}, u32[]{:S(2)}) collective-permute-start(bf16[72,256]{1,0:T(8,128)(2,1)S(1)} %bitcast.15), channel_id=1, source_target_pairs={{1,0},{2,1},{3,2},{4,3},{5,4},{6,5},{7,6},{8,7},{9,8},{10,9},{11,1... | collective-permute-start | bytes 110600 | tf_op jit(solution)/shard_map/ppermute | solution.py:385
  17.8 0.0 copy-start.5
  17.8 0.0 copy-start.6
  17.8 0.7 %copy-done.5 = f32[4,512]{1,0:T(4,128)S(1)} copy-done((f32[4,512]{1,0:T(4,128)S(1)}, f32[4,512]{1,0:T(4,128)}, u32[]{:S(2)}) %copy-start.5) | copy-done | bytes 8216
  18.5 0.0 copy-done.6
  18.5 0.0 copy-start.1
  18.5 0.8 %rows.1 = (f32[4,256,128]{2,1,0:T(8,128)S(1)}, f32[256,512]{1,0:T(8,128)S(1)}, f32[16,512]{1,0:T(8,128)S(1)}, f32[4,64,128]{2,1,0:T(8,128)S(1)}, f32[256,128]{1,...) custom-call(bf16[48,256]{1,0:T(8,128)(2,1)S(1)} %bitcast.14, ...), custom_call_target="tpu_custom_call", output_to_operand_aliasing={{0}: (7, {})} | custom-call | flops 67108864 | bytes 1048576 | tf_op jit(solution)/shard_map/rows/pallas_call | solution.py:435
  19.3 0.0 collective-permute-done.2.before_ref
  19.3 1.9 %collective-permute-done.3.after_ref = bf16[72,256]{1,0:T(8,128)(2,1)S(1)} collective-permute-done((bf16[72,256]{1,0:T(8,128)(2,1)S(1)}, bf16[72,256]{1,0:T(8,128)(2,1)S(1)}, u32[]{:S(2)}, u32[]{:S(2)}) %collective-permute-start.3) | collective-permute-done | bytes 36896 | tf_op jit(solution)/shard_map/ppermute | solution.py:385
  21.2 0.0 copy-done.1
  21.2 1.8 %conv_scan.1 = (f32[4,256,128]{2,1,0:T(8,128)S(1)}, f32[4,256,128]{2,1,0:T(8,128)S(1)}, bf16[8,144,128]{2,1,0:T(8,128)(2,1)S(1)}) custom-call(bf16[72,256]{1,0:T(8,128)(2,1)S(1)} %collective-permute-done.2.before_ref, bf16[72,256]{1,0:T(8,128)(2,1)S(1)} %collective-permute-done.3.after_ref, ...), custom_call_target="tpu_custom_call", output_to_operand_aliasing={{0}: (8, {})} | custom-call | tf_op jit(solution)/shard_map/conv_scan/pallas_call | solution.py:448
  23.0 12.8 %all_to_all.10.near_ref = bf16[8,144,128]{2,1,0:T(8,128)(2,1)S(1)} all-to-all(bf16[8,144,128]{2,1,0:T(8,128)(2,1)S(1)} %get-tuple-element.27), channel_id=1, replica_groups={{0,1,2,3,32,33,34,35},{4,5,6,7,36,37,38,39},{8,9,10,11,40,41,42,43},{12..., dimensions={0} | all-to-all | bytes 589824 | tf_op jit(solution)/shard_map/all_to_all | solution.py:401
  35.8 0.1 totals.1
  35.9 16.6 %all_to_all.11.far_ref = bf16[8,144,128]{2,1,0:T(8,128)(2,1)S(1)} all-to-all(bf16[8,144,128]{2,1,0:T(8,128)(2,1)S(1)} %totals.1), channel_id=1, replica_groups={{0,4,8,12,16,20,24,28},{1,5,9,13,17,21,25,29},{2,6,10,14,18,22,26,30},{..., dimensions={0} | all-to-all | bytes 589824 | tf_op jit(solution)/shard_map/all_to_all | solution.py:401
  52.6 0.2 enter.1
  52.7 6.2 %collective-permute-start.4 = (bf16[128,128]{1,0:T(8,128)(2,1)S(1)}, bf16[128,128]{1,0:T(8,128)(2,1)S(1)}, u32[]{:S(2)}, u32[]{:S(2)}) collective-permute-start(bf16[128,128]{1,0:T(8,128)(2,1)S(1)} %get-tuple-element.29), channel_id=1, source_target_pairs={{0,32},{32,0},{64,96},{96,64},{128,160},{160,128},{192,224},{224,1... | collective-permute-start | bytes 98312 | tf_op jit(solution)/shard_map/ppermute | solution.py:479
  59.0 0.0 copy-start.4
  59.0 0.2 own_axis.1.sum_ref
  59.2 0.7 %collective-permute-done.4.got_ref = bf16[128,128]{1,0:T(8,128)(2,1)S(1)} collective-permute-done((bf16[128,128]{1,0:T(8,128)(2,1)S(1)}, bf16[128,128]{1,0:T(8,128)(2,1)S(1)}, u32[]{:S(2)}, u32[]{:S(2)}) %collective-permute-start.4) | collective-permute-done | bytes 32800 | tf_op jit(solution)/shard_map/ppermute | solution.py:479
  59.8 0.1 copy-done.4
  59.9 1.4 %finish.1 = bf16[256,256]{1,0:T(8,128)(2,1)} custom-call(bf16[128,128]{1,0:T(8,128)(2,1)S(1)} %collective-permute-done.4.got_ref, f32[16,512]{1,0:T(8,128)S(1)} %get-tuple-element.22.cst_ref, f32[256,128]{1,0:T(8,128)S(1)} %get-tuple-element.23.g_ref, f32[4,256,128]{2,1,0:T(8,128)S(1)} %own_axis.1.sum_ref, f32[256,512]{1,0:T(8,128)S(1)} %get-tuple-element.32.gate_ref, ...), custom_call_target="tpu_custom_call" | custom-call | tf_op jit(solution)/shard_map/finish/pallas_call | solution.py:490
  (10 shorter events, 0.1 us)
Async XLA Ops:
  0.0 11.7 %copy-start.2 = (bf16[16,16,256]{2,1,0:T(8,128)(2,1)S(1)}, bf16[16,16,256]{2,1,0:T(8,128)(2,1)}, u32[]{:S(2)}) copy-start(bf16[16,16,256]{2,1,0:T(8,128)(2,1)} %param.6) | copy-start | bytes 393220
  0.8 14.2 %collective-permute-start.1 = (bf16[3,16,256]{2,0,1:T(4,128)(2,1)S(1)}, bf16[3,16,256]{2,0,1:T(4,128)(2,1)S(1)}, u32[]{:S(2)}, u32[]{:S(2)}) collective-permute-start(bf16[3,16,256]{2,0,1:T(4,128)(2,1)S(1)} %copy.19), channel_id=1, source_target_pairs={{32,0},{64,32},{96,64},{128,96},{160,128},{192,160},{224,192},{256... | collective-permute-start | bytes 73736 | tf_op jit(solution)/shard_map/ppermute | solution.py:385
  9.7 2.2 %copy-start.3 = (f32[7,7,512]{2,1,0:T(8,128)S(1)}, f32[7,7,512]{2,1,0:T(8,128)}, u32[]{:S(2)}) copy-start(f32[7,7,512]{2,1,0:T(8,128)} %taps_ref.5) | copy-start | bytes 301060
  9.7 5.4 %collective-permute-start = (bf16[3,16,256]{2,0,1:T(4,128)(2,1)S(1)}, bf16[3,16,256]{2,0,1:T(4,128)(2,1)S(1)}, u32[]{:S(2)}, u32[]{:S(2)}) collective-permute-start(bf16[3,16,256]{2,0,1:T(4,128)(2,1)S(1)} %copy.17), channel_id=1, source_target_pairs={{0,32},{32,64},{64,96},{96,128},{128,160},{160,192},{192,224},{224... | collective-permute-start | bytes 73736 | tf_op jit(solution)/shard_map/ppermute | solution.py:385
  11.9 1.0 %copy-start = (bf16[256,1024]{1,0:T(8,128)(2,1)S(1)}, bf16[256,1024]{1,0:T(8,128)(2,1)}, u32[]{:S(2)}) copy-start(bf16[256,1024]{1,0:T(8,128)(2,1)} %wv_ref.1) | copy-start | bytes 1572868
  15.2 4.1 %collective-permute-start.2 = (bf16[72,256]{1,0:T(8,128)(2,1)S(1)}, bf16[72,256]{1,0:T(8,128)(2,1)S(1)}, u32[]{:S(2)}, u32[]{:S(2)}) collective-permute-start(bf16[72,256]{1,0:T(8,128)(2,1)S(1)} %bitcast.16), channel_id=1, source_target_pairs={{0,1},{1,2},{2,3},{3,4},{4,5},{5,6},{6,7},{7,8},{8,9},{9,10},{10,1... | collective-permute-start | bytes 110600 | tf_op jit(solution)/shard_map/ppermute | solution.py:385
  16.5 4.7 %collective-permute-start.3 = (bf16[72,256]{1,0:T(8,128)(2,1)S(1)}, bf16[72,256]{1,0:T(8,128)(2,1)S(1)}, u32[]{:S(2)}, u32[]{:S(2)}) collective-permute-start(bf16[72,256]{1,0:T(8,128)(2,1)S(1)} %bitcast.15), channel_id=1, source_target_pairs={{1,0},{2,1},{3,2},{4,3},{5,4},{6,5},{7,6},{8,7},{9,8},{10,9},{11,1... | collective-permute-start | bytes 110600 | tf_op jit(solution)/shard_map/ppermute | solution.py:385
  17.8 0.7 %copy-start.5 = (f32[4,512]{1,0:T(4,128)S(1)}, f32[4,512]{1,0:T(4,128)}, u32[]{:S(2)}) copy-start(f32[4,512]{1,0:T(4,128)} %table_ref.1) | copy-start | bytes 24580
  17.8 0.7 %copy-start.6 = (f32[16,16]{1,0:T(8,128)S(1)}, f32[16,16]{1,0:T(8,128)}, u32[]{:S(2)}) copy-start(f32[16,16]{1,0:T(8,128)} %extra_ref.1) | copy-start | bytes 3076
  18.5 2.7 %copy-start.1 = (bf16[256,1024]{1,0:T(8,128)(2,1)S(1)}, bf16[256,1024]{1,0:T(8,128)(2,1)}, u32[]{:S(2)}) copy-start(bf16[256,1024]{1,0:T(8,128)(2,1)} %wv_ref.1) | copy-start | bytes 1572868
  52.7 7.1 %collective-permute-start.4 = (bf16[128,128]{1,0:T(8,128)(2,1)S(1)}, bf16[128,128]{1,0:T(8,128)(2,1)S(1)}, u32[]{:S(2)}, u32[]{:S(2)}) collective-permute-start(bf16[128,128]{1,0:T(8,128)(2,1)S(1)} %get-tuple-element.29), channel_id=1, source_target_pairs={{0,32},{32,0},{64,96},{96,64},{128,160},{160,128},{192,224},{224,1... | collective-permute-start | bytes 98312 | tf_op jit(solution)/shard_map/ppermute | solution.py:479
  59.0 1.0 %copy-start.4 = (bf16[512,256]{1,0:T(8,128)(2,1)S(1)}, bf16[512,256]{1,0:T(8,128)(2,1)}, u32[]{:S(2)}) copy-start(bf16[512,256]{1,0:T(8,128)(2,1)} %wo_ref.1) | copy-start | bytes 786436

commit v8 on v6

--- a/solution.py
+++ b/solution.py
@@ -320,20 +320,37 @@
     lax.fori_loop(0, 4, group, 0)
 
 
-def own_axis_kernel(keep_ref, cst_ref, g_ref, sum_ref, acc_ref):
+def own_axis_kernel(keep_ref, cst_ref, g_ref, sum_ref, acc_ref, ahead_ref, back_ref):
     def first(side, ct, half):
         return keep_ref[pl.ds(64 * side + ct * T + half * 8, 8), :]
 
     def store(ct, at, x):
         acc_ref[ct, at, :] = sum_ref[ct, at, :] + x
 
-    for kind in range(2):
-        @pl.when(position()[0] == kind)
-        def _():
-            decay_rows(kind, first, cst_ref, g_ref, store)
-
-
-def finish_kernel(got_ref, cst_ref, g_ref, sum_ref, gate_ref, tok_ref, wo_ref,
+    @pl.when(position()[0] == 0)
+    def _():
+        decay_rows(0, first, cst_ref, g_ref, store)
+
+    @pl.when(position()[0] == 1)
+    def _():
+        decay_rows(1, first, cst_ref, g_ref, store)
+
+        def group(ct, carry):
+            lanes = pl.ds(pl.multiple_of(ct * LANES, LANES), LANES)
+            for side, ref, order in ((0, ahead_ref, range(T)), (1, back_ref, reversed(range(T)))):
+                base = cst_ref[pl.ds(side, 1), lanes]
+                states = [jnp.ones((8, LANES), F32)] * 2
+                for j in order:
+                    for half in range(2):
+                        at = pl.ds(half * 8 * T + j, 8, stride=T)
+                        states[half] = states[half] * (base * g_ref[at, :])
+                        ref[ct, at, :] = states[half]
+            return carry
+
+        lax.fori_loop(0, 4, group, 0)
+
+
+def finish_kernel(got_ref, cst_ref, g_ref, sum_ref, ahead_ref, back_ref, gate_ref, tok_ref, wo_ref,
                   out_ref, acc_ref, enter_ref, gated_ref):
     groups = acc_ref.shape[0]
     enter_ref[...] = got_ref[...].astype(F32)
@@ -344,10 +361,21 @@
     def store(ct, at, x):
         acc_ref[ct, at, :] = sum_ref[ct, at, :] + x
 
-    for kind in range(2):
-        @pl.when(position()[0] != kind)
-        def _():
-            decay_rows(kind, first, cst_ref, g_ref, store)
+    @pl.when(position()[0] == 0)
+    def _():
+        decay_rows(1, first, cst_ref, g_ref, store)
+
+    @pl.when(position()[0] == 1)
+    def _():
+        def group(ct, carry):
+            for i in range(T):
+                fore, aft = enter_ref[pl.ds(ct * T + i, 1), :], enter_ref[pl.ds(64 + ct * T + i, 1), :]
+                for half in range(2):
+                    at = pl.ds(i * T + half * 8, 8)
+                    acc_ref[ct, at, :] = sum_ref[ct, at, :] + (fore * ahead_ref[ct, at, :] + aft * back_ref[ct, at, :])
+            return carry
+
+        lax.fori_loop(0, groups, group, 0)
 
     for ct in range(groups):
         lanes = slice(ct * LANES, (ct + 1) * LANES)
@@ -445,11 +473,11 @@
     )(near, far, whole)
     got = lax.ppermute(give, "row", [(i, i ^ 1) for i in range(rows)])
 
-    acc = pl.pallas_call(
+    acc, ahead, back = pl.pallas_call(
         own_axis_kernel,
-        out_shape=tile,
+        out_shape=(tile,) * 3,
         in_specs=[spec] * 4,
-        out_specs=spec,
+        out_specs=(spec,) * 3,
         compiler_params=params,
         cost_estimate=pl.CostEstimate(flops=6 * PX * width, bytes_accessed=2 * 2**20, transcendentals=0),
         name="own_axis",
@@ -457,12 +485,12 @@
     mixed = pl.pallas_call(
         finish_kernel,
         out_shape=jax.ShapeDtypeStruct((PX, channels), BF16),
-        in_specs=[spec] * 7,
+        in_specs=[spec] * 9,
         out_specs=spec,
         scratch_shapes=[VMEM((groups, PX, LANES), F32), VMEM((128, LANES), F32), VMEM((PX, width), BF16)],
         compiler_params=params,
         name="finish",
-    )(got, cst, g, acc, gate, flat, output_weight)
+    )(got, cst, g, acc, ahead, back, gate, flat, output_weight)
     return mixed.reshape(T, T, channels)
 
 

time: 61 us -> 60.7 us (level)
  transfers between devices with their start and end apart: 5 -> 5, of which waited for: 2 -> 2; matrix products, arithmetic and copies ran while one was open for 0% -> 0% of each run, Pallas kernels for 5% -> 6%
where the time goes in v8:
time: 60.7 us; the launch traced here: 60.3 us
  blocking collectives  28.6 us (47%)
  starting transfers between devices  21.8 us (36%)
  Pallas kernels  6.77 us (11%)
  local copies, waits for them, and re-layouts  1.81 us (3%)
  waiting for transfers between devices  1.02 us (2%)
    all_to_all x2, blocking collectives, swap(): lax.all_to_all(x, ('row', 'col'), 0, 0, axis_index_groups=groups, tiled=T...  28.6 us
    ppermute x1, starting transfers between devices, body(): got = lax.ppermute(give, 'row', [(i, i ^ 1) for i in range(rows)])  11.8 us
    ppermute x4, starting transfers between devices, neighbours(): return (lax.ppermute(x_last, axis, up), lax.ppermute(x_first, axis, down))  9.97 us
    pallas_call x1, Pallas kernels, body(): pl.pallas_call(inner_kernel, out_shape=(tile, jax.ShapeDtypeStruct((PX, w...  3.07 us
    pallas_call x1, Pallas kernels, body(): pl.pallas_call(conv_scan_kernel, out_shape=(tile, tile, jax.ShapeDtypeStr...  1.74 us
  transfers between devices with their start and end apart: 5, of which 2 were waited for; matrix products, arithmetic and copies ran while one was open for 0% of the time, Pallas kernels for 6%

profile of v8, /device:TPU:33, one launch (start us, length us, event | category | flops | bytes accessed | tf_op | source)
XLA Modules:
  0.0 60.3 jit_solution(13900662924185198101)
XLA Ops:
  0.0 0.0 copy-start.1
  0.0 0.0 copy-start
  0.0 0.8 %fusion.1 = (bf16[3,16,256]{2,1,0:T(8,128)(2,1)S(1)}, bf16[3,16,256]{2,1,0:T(8,128)(2,1)S(1)}) fusion(bf16[16,16,256]{2,1,0:T(8,128)(2,1)} %param.6), kind=kLoop, calls=%fused_computation.3 | loop fusion | bytes 98304 | tf_op jit(solution)/shard_map/slice | solution.py:417
  0.8 2.6 %collective-permute-start.1 = (bf16[3,16,256]{2,0,1:T(4,128)(2,1)S(1)}, bf16[3,16,256]{2,0,1:T(4,128)(2,1)S(1)}, u32[]{:S(2)}, u32[]{:S(2)}) collective-permute-start(bf16[3,16,256]{2,0,1:T(4,128)(2,1)S(1)} %copy.18), channel_id=1, source_target_pairs={{32,0},{64,32},{96,64},{128,96},{160,128},{192,160},{224,192},{256... | collective-permute-start | bytes 73736 | tf_op jit(solution)/shard_map/ppermute | solution.py:391
  3.5 3.0 %collective-permute-start = (bf16[3,16,256]{2,0,1:T(4,128)(2,1)S(1)}, bf16[3,16,256]{2,0,1:T(4,128)(2,1)S(1)}, u32[]{:S(2)}, u32[]{:S(2)}) collective-permute-start(bf16[3,16,256]{2,0,1:T(4,128)(2,1)S(1)} %copy.16), channel_id=1, source_target_pairs={{0,32},{32,64},{64,96},{96,128},{128,160},{160,192},{192,224},{224... | collective-permute-start | bytes 73736 | tf_op jit(solution)/shard_map/ppermute | solution.py:391
  6.5 0.0 copy-done.1
  6.5 0.1 pad.7.clone
  6.6 0.0 collective-permute-done.1
  6.6 0.8 %collective-permute-done = bf16[3,16,256]{2,0,1:T(4,128)(2,1)S(1)} collective-permute-done((bf16[3,16,256]{2,0,1:T(4,128)(2,1)S(1)}, bf16[3,16,256]{2,0,1:T(4,128)(2,1)S(1)}, u32[]{:S(2)}, u32[]{:S(2)}) %collective-permute-start) | collective-permute-done | bytes 24608 | tf_op jit(solution)/shard_map/ppermute | solution.py:391
  7.5 0.0 copy-start.2
  7.5 0.1 maximum_maximum_fusion.1
  7.6 3.1 %collective-permute-start.2 = (bf16[72,256]{1,0:T(8,128)(2,1)S(1)}, bf16[72,256]{1,0:T(8,128)(2,1)S(1)}, u32[]{:S(2)}, u32[]{:S(2)}) collective-permute-start(bf16[72,256]{1,0:T(8,128)(2,1)S(1)} %bitcast.15), channel_id=1, source_target_pairs={{0,1},{1,2},{2,3},{3,4},{4,5},{5,6},{6,7},{7,8},{8,9},{9,10},{10,1... | collective-permute-start | bytes 110600 | tf_op jit(solution)/shard_map/ppermute | solution.py:391
  10.7 1.3 %collective-permute-start.3 = (bf16[72,256]{1,0:T(8,128)(2,1)S(1)}, bf16[72,256]{1,0:T(8,128)(2,1)S(1)}, u32[]{:S(2)}, u32[]{:S(2)}) collective-permute-start(bf16[72,256]{1,0:T(8,128)(2,1)S(1)} %bitcast.14), channel_id=1, source_target_pairs={{1,0},{2,1},{3,2},{4,3},{5,4},{6,5},{7,6},{8,7},{9,8},{10,9},{11,1... | collective-permute-start | bytes 110600 | tf_op jit(solution)/shard_map/ppermute | solution.py:391
  12.0 0.0 copy-start.4
  12.0 0.0 copy-start.5
  12.0 0.0 copy-done
  12.0 0.0 copy-done.2
  12.1 0.6 %copy-done.4 = f32[4,512]{1,0:T(4,128)S(1)} copy-done((f32[4,512]{1,0:T(4,128)S(1)}, f32[4,512]{1,0:T(4,128)}, u32[]{:S(2)}) %copy-start.4) | copy-done | bytes 8216
  12.7 0.0 copy-done.5
  12.7 3.1 %inner.1 = (f32[4,256,128]{2,1,0:T(8,128)S(1)}, f32[256,512]{1,0:T(8,128)S(1)}, f32[16,512]{1,0:T(8,128)S(1)}, f32[4,64,128]{2,1,0:T(8,128)S(1)}, f32[256,128]{1...) custom-call(bf16[48,256]{1,0:T(8,128)(2,1)S(1)} %bitcast.13, ...), custom_call_target="tpu_custom_call" | custom-call | flops 159383552 | bytes 4194304 | tf_op jit(solution)/shard_map/inner/pallas_call | solution.py:430
  15.8 0.0 collective-permute-done.2.before_ref
  15.8 0.0 collective-permute-done.3.after_ref
  15.8 1.7 %conv_scan.1 = (f32[4,256,128]{2,1,0:T(8,128)S(1)}, f32[4,256,128]{2,1,0:T(8,128)S(1)}, bf16[8,144,128]{2,1,0:T(8,128)(2,1)S(1)}) custom-call(bf16[72,256]{1,0:T(8,128)(2,1)S(1)} %collective-permute-done.2.before_ref, bf16[72,256]{1,0:T(8,128)(2,1)S(1)} %collective-permute-done.3.after_ref, ...), custom_call_target="tpu_custom_call", output_to_operand_aliasing={{0}: (9, {})} | custom-call | tf_op jit(solution)/shard_map/conv_scan/pallas_call | solution.py:443
  17.6 17.6 %all_to_all.10.near_ref = bf16[8,144,128]{2,1,0:T(8,128)(2,1)S(1)} all-to-all(bf16[8,144,128]{2,1,0:T(8,128)(2,1)S(1)} %get-tuple-element.26), channel_id=1, replica_groups={{0,1,2,3,32,33,34,35},{4,5,6,7,36,37,38,39},{8,9,10,11,40,41,42,43},{12..., dimensions={0} | all-to-all | bytes 589824 | tf_op jit(solution)/shard_map/all_to_all | solution.py:407
  35.1 0.1 totals.1
  35.3 11.0 %all_to_all.11.far_ref = bf16[8,144,128]{2,1,0:T(8,128)(2,1)S(1)} all-to-all(bf16[8,144,128]{2,1,0:T(8,128)(2,1)S(1)} %totals.1), channel_id=1, replica_groups={{0,4,8,12,16,20,24,28},{1,5,9,13,17,21,25,29},{2,6,10,14,18,22,26,30},{..., dimensions={0} | all-to-all | bytes 589824 | tf_op jit(solution)/shard_map/all_to_all | solution.py:407
  46.3 0.2 enter.1
  46.5 11.8 %collective-permute-start.4 = (bf16[128,128]{1,0:T(8,128)(2,1)S(1)}, bf16[128,128]{1,0:T(8,128)(2,1)S(1)}, u32[]{:S(2)}, u32[]{:S(2)}) collective-permute-start(bf16[128,128]{1,0:T(8,128)(2,1)S(1)} %get-tuple-element.28), channel_id=1, source_target_pairs={{0,32},{32,0},{64,96},{96,64},{128,160},{160,128},{192,224},{224,1... | collective-permute-start | bytes 98312 | tf_op jit(solution)/shard_map/ppermute | solution.py:474
  58.3 0.0 copy-start.3
  58.3 0.6 %own_axis.1 = (f32[4,256,128]{2,1,0:T(8,128)S(1)}, f32[4,256,128]{2,1,0:T(8,128)S(1)}, f32[4,256,128]{2,1,0:T(8,128)S(1)}) custom-call(f32[128,128]{1,0:T(8,128)S(1)} %get-tuple-element.29.keep_ref, f32[16,512]{1,0:T(8,128)S(1)} %get-tuple-element.20.cst_ref, f32[256,128]{1,0:T(8,128)S(1)} %get-tuple-element.21.g_ref, ...), custom_call_target="tpu_custom_call" | custom-call | flops 786432 | bytes 2097152 | tf_op jit(solution)/shard_map/own_axis/pallas_call | solution.py:476
  58.9 0.2 collective-permute-done.4.got_ref
  59.1 0.1 copy-done.3
  59.2 1.0 %finish.1 = bf16[256,256]{1,0:T(8,128)(2,1)} custom-call(bf16[128,128]{1,0:T(8,128)(2,1)S(1)} %collective-permute-done.4.got_ref, f32[16,512]{1,0:T(8,128)S(1)} %get-tuple-element.20.cst_ref, f32[256,128]{1,0:T(8,128)S(1)} %get-tuple-element.21.g_ref, f32[4,256,128]{2,1,0:T(8,128)S(1)} %get-tuple-element.31.sum_ref, ...), custom_call_target="tpu_custom_call" | custom-call | tf_op jit(solution)/shard_map/finish/pallas_call | solution.py:485
  (10 shorter events, 0.1 us)
Async XLA Ops:
  0.0 6.5 %copy-start.1 = (bf16[16,16,256]{2,1,0:T(8,128)(2,1)S(1)}, bf16[16,16,256]{2,1,0:T(8,128)(2,1)}, u32[]{:S(2)}) copy-start(bf16[16,16,256]{2,1,0:T(8,128)(2,1)} %param.6) | copy-start | bytes 393220
  0.0 12.0 %copy-start = (bf16[256,1024]{1,0:T(8,128)(2,1)S(1)}, bf16[256,1024]{1,0:T(8,128)(2,1)}, u32[]{:S(2)}) copy-start(bf16[256,1024]{1,0:T(8,128)(2,1)} %wv_ref.1) | copy-start | bytes 1572868
  0.8 5.8 %collective-permute-start.1 = (bf16[3,16,256]{2,0,1:T(4,128)(2,1)S(1)}, bf16[3,16,256]{2,0,1:T(4,128)(2,1)S(1)}, u32[]{:S(2)}, u32[]{:S(2)}) collective-permute-start(bf16[3,16,256]{2,0,1:T(4,128)(2,1)S(1)} %copy.18), channel_id=1, source_target_pairs={{32,0},{64,32},{96,64},{128,96},{160,128},{192,160},{224,192},{256... | collective-permute-start | bytes 73736 | tf_op jit(solution)/shard_map/ppermute | solution.py:391
  3.5 4.0 %collective-permute-start = (bf16[3,16,256]{2,0,1:T(4,128)(2,1)S(1)}, bf16[3,16,256]{2,0,1:T(4,128)(2,1)S(1)}, u32[]{:S(2)}, u32[]{:S(2)}) collective-permute-start(bf16[3,16,256]{2,0,1:T(4,128)(2,1)S(1)} %copy.16), channel_id=1, source_target_pairs={{0,32},{32,64},{64,96},{96,128},{128,160},{160,192},{192,224},{224... | collective-permute-start | bytes 73736 | tf_op jit(solution)/shard_map/ppermute | solution.py:391
  7.5 4.6 %copy-start.2 = (f32[7,7,512]{2,1,0:T(8,128)S(1)}, f32[7,7,512]{2,1,0:T(8,128)}, u32[]{:S(2)}) copy-start(f32[7,7,512]{2,1,0:T(8,128)} %taps_ref.3) | copy-start | bytes 301060
  7.6 8.2 %collective-permute-start.2 = (bf16[72,256]{1,0:T(8,128)(2,1)S(1)}, bf16[72,256]{1,0:T(8,128)(2,1)S(1)}, u32[]{:S(2)}, u32[]{:S(2)}) collective-permute-start(bf16[72,256]{1,0:T(8,128)(2,1)S(1)} %bitcast.15), channel_id=1, source_target_pairs={{0,1},{1,2},{2,3},{3,4},{4,5},{5,6},{6,7},{7,8},{8,9},{9,10},{10,1... | collective-permute-start | bytes 110600 | tf_op jit(solution)/shard_map/ppermute | solution.py:391
  10.7 5.1 %collective-permute-start.3 = (bf16[72,256]{1,0:T(8,128)(2,1)S(1)}, bf16[72,256]{1,0:T(8,128)(2,1)S(1)}, u32[]{:S(2)}, u32[]{:S(2)}) collective-permute-start(bf16[72,256]{1,0:T(8,128)(2,1)S(1)} %bitcast.14), channel_id=1, source_target_pairs={{1,0},{2,1},{3,2},{4,3},{5,4},{6,5},{7,6},{8,7},{9,8},{10,9},{11,1... | collective-permute-start | bytes 110600 | tf_op jit(solution)/shard_map/ppermute | solution.py:391
  12.0 0.7 %copy-start.4 = (f32[4,512]{1,0:T(4,128)S(1)}, f32[4,512]{1,0:T(4,128)}, u32[]{:S(2)}) copy-start(f32[4,512]{1,0:T(4,128)} %table_ref.1) | copy-start | bytes 24580
  12.0 0.7 %copy-start.5 = (f32[16,16]{1,0:T(8,128)S(1)}, f32[16,16]{1,0:T(8,128)}, u32[]{:S(2)}) copy-start(f32[16,16]{1,0:T(8,128)} %extra_ref.1) | copy-start | bytes 3076
  46.5 12.7 %collective-permute-start.4 = (bf16[128,128]{1,0:T(8,128)(2,1)S(1)}, bf16[128,128]{1,0:T(8,128)(2,1)S(1)}, u32[]{:S(2)}, u32[]{:S(2)}) collective-permute-start(bf16[128,128]{1,0:T(8,128)(2,1)S(1)} %get-tuple-element.28), channel_id=1, source_target_pairs={{0,32},{32,0},{64,96},{96,64},{128,160},{160,128},{192,224},{224,1... | collective-permute-start | bytes 98312 | tf_op jit(solution)/shard_map/ppermute | solution.py:474
  58.3 1.0 %copy-start.3 = (bf16[512,256]{1,0:T(8,128)(2,1)S(1)}, bf16[512,256]{1,0:T(8,128)(2,1)}, u32[]{:S(2)}) copy-start(bf16[512,256]{1,0:T(8,128)(2,1)} %wo_ref.1) | copy-start | bytes 786436

commit v9 on v8

--- a/solution.py
+++ b/solution.py
@@ -47,7 +47,7 @@
     return jnp.where(x < 0.1, series, 1.0 - jnp.exp(-x))
 
 
-def spread_decays(table_ref, extra_ref, cst_ref, whole_ref, g_ref, tails_ref, flow_refs, h_ref):
+def spread_decays(table_ref, extra_ref, cst_ref, whole_ref, g_ref, across_ref, tails_ref, flow_refs, h_refs):
     table = table_ref[...]
     cst_ref[0:4] = jnp.exp(-table)
     cst_ref[4:8] = fall(2.0 * table)
@@ -65,8 +65,11 @@
         line = jnp.sum(jnp.where(diagonal, line, 0.0), axis=1, keepdims=True)
         line = jnp.broadcast_to(line, (T, LANES))
         g_ref[i * T:(i + 1) * T] = jnp.exp(-line)
-        h_ref[i * T:(i + 1) * T] = fall(2.0 * line)
+        h_refs[1][i * T:(i + 1) * T] = fall(2.0 * line)
         down = down + line
+        line = jnp.broadcast_to(extra[:, i:i + 1], (T, LANES))
+        across_ref[i * T:(i + 1) * T] = jnp.exp(-line)
+        h_refs[0][i * T:(i + 1) * T] = fall(2.0 * line)
     across = jnp.broadcast_to(jnp.sum(extra, axis=1, keepdims=True), (T, LANES))
     lane = lax.broadcasted_iota(jnp.int32, (T, LANES), 1)
     for k, total in enumerate((across, down)):
@@ -78,7 +81,7 @@
         lanes = pl.ds(pl.multiple_of(ct * LANES, LANES), LANES)
         for d in range(4):
             base, slope = cst_ref[pl.ds(4 + d, 1), lanes], cst_ref[pl.ds(8 + d, 1), lanes]
-            q = base + slope * h_ref[...]
+            q = base + slope * h_refs[d // 2][...]
             flow_refs[d // 2][d % 2, ct] = q * lax.rsqrt(q)
         return carry
 
@@ -86,9 +89,11 @@
 
 
 def inner_kernel(above_ref, tok_ref, below_ref, weight_ref, taps_ref, table_ref, extra_ref,
-                 acc_ref, gate_ref, cst_ref, whole_ref, g_ref, tails_ref, along_ref, down_ref, v_ref, h_ref):
+                 acc_ref, gate_ref, cst_ref, whole_ref, g_ref, across_ref, tails_ref, along_ref, down_ref,
+                 v_ref, ha_ref, hd_ref):
     groups = v_ref.shape[0]
-    spread_decays(table_ref, extra_ref, cst_ref, whole_ref, g_ref, tails_ref, (along_ref, down_ref), h_ref)
+    spread_decays(table_ref, extra_ref, cst_ref, whole_ref, g_ref, across_ref, tails_ref,
+                  (along_ref, down_ref), (ha_ref, hd_ref))
     for ct in range(groups):
         for j in (0, 1, 2, T + 3, T + 4, T + 5):
             v_ref[ct, pl.ds(j, PW, stride=PW), :] = jnp.zeros((PW, LANES), F32)
@@ -117,8 +122,8 @@
     lax.fori_loop(0, groups, group, 0)
 
 
-def conv_scan_kernel(before_ref, after_ref, wv_ref, taps_ref, cst_ref, g_ref, along_ref, down_ref, tails_ref,
-                     own_ref, acc_ref, sum_ref, near_ref, side_ref, line_ref, val_ref, end_ref):
+def conv_scan_kernel(before_ref, after_ref, wv_ref, taps_ref, cst_ref, g_ref, across_ref, along_ref, down_ref,
+                     tails_ref, own_ref, acc_ref, sum_ref, near_ref, side_ref, line_ref, val_ref, end_ref):
     del own_ref
     groups = line_ref.shape[0]
     side_ref[0:3 * PW] = before_ref[...].astype(F32)
@@ -134,7 +139,8 @@
         cst = [cst_ref[pl.ds(k, 1), lanes] for k in range(4)]
 
         def flow(d, at, x):
-            return cst[d] * g_ref[at, :], (along_ref, down_ref)[d // 2][d % 2, ct, at, :] * x
+            g, factor = ((across_ref, along_ref), (g_ref, down_ref))[d // 2]
+            return cst[d] * g[at, :], factor[d % 2, ct, at, :] * x
 
         for side in range(2):
             outs = range(3) if side == 0 else range(T - 3, T)
@@ -173,18 +179,18 @@
                 sum_ref[ct, at, :] = downs[i] + state
             end_ref[1, pl.ds(64 + ct * T + jt * 8, 8), :] = state
         for it in range(2):
+            values = [val_ref[pl.ds(it * 8 * T + j, 8, stride=T), :] for j in range(T)]
             state = jnp.zeros((8, LANES), F32)
             lefts = []
             for j in range(T):
-                at = pl.ds(it * 8 * T + j, 8, stride=T)
-                d, f = flow(0, at, val_ref[at, :])
+                d, f = flow(0, pl.ds(j * T + it * 8, 8), values[j])
                 state = d * state + f
                 lefts.append(state)
             end_ref[0, pl.ds(0 + ct * T + it * 8, 8), :] = state
             state = jnp.zeros((8, LANES), F32)
             for j in reversed(range(T)):
                 at = pl.ds(it * 8 * T + j, 8, stride=T)
-                d, f = flow(1, at, val_ref[at, :])
+                d, f = flow(1, pl.ds(j * T + it * 8, 8), values[j])
                 state = d * state + f
                 sum_ref[ct, at, :] = sum_ref[ct, at, :] + (lefts[j] + state)
             end_ref[0, pl.ds(64 + ct * T + it * 8, 8), :] = state
@@ -426,16 +432,17 @@
     spec = pl.BlockSpec(memory_space=VMEM)
     params = pltpu.CompilerParams(vmem_limit_bytes=16 * 2**20)
     tile = jax.ShapeDtypeStruct((groups, PX, LANES), F32)
+    spread = jax.ShapeDtypeStruct((PX, LANES), F32)
     factor = jax.ShapeDtypeStruct((2, groups, PX, LANES), F32)
-    own, gate, cst, whole, g, tails, along, downward = pl.pallas_call(
+    own, gate, cst, whole, g, across, tails, along, downward = pl.pallas_call(
         inner_kernel,
         out_shape=(tile, jax.ShapeDtypeStruct((PX, width), F32), jax.ShapeDtypeStruct((16, width), F32),
                    jax.ShapeDtypeStruct((4, groups * T, LANES), F32),
-                   jax.ShapeDtypeStruct((PX, LANES), F32), jax.ShapeDtypeStruct((2, T, LANES), BF16),
+                   spread, spread, jax.ShapeDtypeStruct((2, T, LANES), BF16),
                    factor, factor),
         in_specs=[spec] * 7,
-        out_specs=(spec,) * 8,
-        scratch_shapes=[VMEM((groups, PW * PW, LANES), F32), VMEM((PX, LANES), F32)],
+        out_specs=(spec,) * 9,
+        scratch_shapes=[VMEM((groups, PW * PW, LANES), F32), VMEM((PX, LANES), F32), VMEM((PX, LANES), F32)],
         compiler_params=params,
         cost_estimate=pl.CostEstimate(flops=2 * 608 * channels * width, bytes_accessed=4 * 2**20, transcendentals=0),
         name="inner",
@@ -443,14 +450,14 @@
     _, local, near = pl.pallas_call(
         conv_scan_kernel,
         out_shape=(tile, tile, jax.ShapeDtypeStruct((2 * XS, 144, LANES), BF16)),
-        in_specs=[spec] * 10,
+        in_specs=[spec] * 11,
         out_specs=(spec, spec, spec),
         scratch_shapes=[VMEM((6 * PW, channels), F32), VMEM((groups, 6 * PW, LANES), F32),
                         VMEM((PX, LANES), F32), VMEM((2, 128, LANES), F32)],
-        input_output_aliases={9: 0},
+        input_output_aliases={10: 0},
         compiler_params=params,
         name="conv_scan",
-    )(before, after, input_weight, kernel, cst, g, along, downward, tails, own)
+    )(before, after, input_weight, kernel, cst, g, across, along, downward, tails, own)
     near = swap(near, near_groups(rows, cols))
 
     far = pl.pallas_call(

time: 60.7 us -> 60.5 us (level)
  transfers between devices with their start and end apart: 5 -> 5, of which waited for: 2 -> 2; matrix products, arithmetic and copies ran while one was open for 0% -> 0% of each run, Pallas kernels for 6% -> 7%
where the time goes in v9:
time: 60.5 us; the launch traced here: 60.1 us
  blocking collectives  28.3 us (47%)
  starting transfers between devices  22.1 us (37%)
  Pallas kernels  6.59 us (11%)
  local copies, waits for them, and re-layouts  1.81 us (3%)
  waiting for transfers between devices  1.02 us (2%)
    all_to_all x2, blocking collectives, swap(): lax.all_to_all(x, ('row', 'col'), 0, 0, axis_index_groups=groups, tiled=T...  28.3 us
    ppermute x1, starting transfers between devices, body(): got = lax.ppermute(give, 'row', [(i, i ^ 1) for i in range(rows)])  12.1 us
    ppermute x4, starting transfers between devices, neighbours(): return (lax.ppermute(x_last, axis, up), lax.ppermute(x_first, axis, down))  9.97 us
    pallas_call x1, Pallas kernels, body(): pl.pallas_call(inner_kernel, out_shape=(tile, jax.ShapeDtypeStruct((PX, w...  3.4 us
    pallas_call x1, Pallas kernels, body(): pl.pallas_call(conv_scan_kernel, out_shape=(tile, tile, jax.ShapeDtypeStr...  1.24 us
  transfers between devices with their start and end apart: 5, of which 2 were waited for; matrix products, arithmetic and copies ran while one was open for 0% of the time, Pallas kernels for 7%

profile of v9, /device:TPU:33, one launch (start us, length us, event | category | flops | bytes accessed | tf_op | source)
XLA Modules:
  0.0 60.1 jit_solution(12523418436899665847)
XLA Ops:
  0.0 0.0 copy-start.1
  0.0 0.0 copy-start
  0.0 0.8 %fusion.1 = (bf16[3,16,256]{2,1,0:T(8,128)(2,1)S(1)}, bf16[3,16,256]{2,1,0:T(8,128)(2,1)S(1)}) fusion(bf16[16,16,256]{2,1,0:T(8,128)(2,1)} %param.6), kind=kLoop, calls=%fused_computation.3 | loop fusion | bytes 98304 | tf_op jit(solution)/shard_map/slice | solution.py:423
  0.8 2.6 %collective-permute-start.1 = (bf16[3,16,256]{2,0,1:T(4,128)(2,1)S(1)}, bf16[3,16,256]{2,0,1:T(4,128)(2,1)S(1)}, u32[]{:S(2)}, u32[]{:S(2)}) collective-permute-start(bf16[3,16,256]{2,0,1:T(4,128)(2,1)S(1)} %copy.18), channel_id=1, source_target_pairs={{32,0},{64,32},{96,64},{128,96},{160,128},{192,160},{224,192},{256... | collective-permute-start | bytes 73736 | tf_op jit(solution)/shard_map/ppermute | solution.py:397
  3.5 3.0 %collective-permute-start = (bf16[3,16,256]{2,0,1:T(4,128)(2,1)S(1)}, bf16[3,16,256]{2,0,1:T(4,128)(2,1)S(1)}, u32[]{:S(2)}, u32[]{:S(2)}) collective-permute-start(bf16[3,16,256]{2,0,1:T(4,128)(2,1)S(1)} %copy.16), channel_id=1, source_target_pairs={{0,32},{32,64},{64,96},{96,128},{128,160},{160,192},{192,224},{224... | collective-permute-start | bytes 73736 | tf_op jit(solution)/shard_map/ppermute | solution.py:397
  6.5 0.0 copy-done.1
  6.5 0.1 pad.7.clone
  6.6 0.0 collective-permute-done.1
  6.6 0.8 %collective-permute-done = bf16[3,16,256]{2,0,1:T(4,128)(2,1)S(1)} collective-permute-done((bf16[3,16,256]{2,0,1:T(4,128)(2,1)S(1)}, bf16[3,16,256]{2,0,1:T(4,128)(2,1)S(1)}, u32[]{:S(2)}, u32[]{:S(2)}) %collective-permute-start) | collective-permute-done | bytes 24608 | tf_op jit(solution)/shard_map/ppermute | solution.py:397
  7.5 0.0 copy-start.2
  7.5 0.1 maximum_maximum_fusion.1
  7.6 3.1 %collective-permute-start.2 = (bf16[72,256]{1,0:T(8,128)(2,1)S(1)}, bf16[72,256]{1,0:T(8,128)(2,1)S(1)}, u32[]{:S(2)}, u32[]{:S(2)}) collective-permute-start(bf16[72,256]{1,0:T(8,128)(2,1)S(1)} %bitcast.15), channel_id=1, source_target_pairs={{0,1},{1,2},{2,3},{3,4},{4,5},{5,6},{6,7},{7,8},{8,9},{9,10},{10,1... | collective-permute-start | bytes 110600 | tf_op jit(solution)/shard_map/ppermute | solution.py:397
  10.7 1.3 %collective-permute-start.3 = (bf16[72,256]{1,0:T(8,128)(2,1)S(1)}, bf16[72,256]{1,0:T(8,128)(2,1)S(1)}, u32[]{:S(2)}, u32[]{:S(2)}) collective-permute-start(bf16[72,256]{1,0:T(8,128)(2,1)S(1)} %bitcast.14), channel_id=1, source_target_pairs={{1,0},{2,1},{3,2},{4,3},{5,4},{6,5},{7,6},{8,7},{9,8},{10,9},{11,1... | collective-permute-start | bytes 110600 | tf_op jit(solution)/shard_map/ppermute | solution.py:397
  12.0 0.0 copy-start.4
  12.0 0.0 copy-start.5
  12.0 0.0 copy-done
  12.0 0.0 copy-done.2
  12.1 0.6 %copy-done.4 = f32[4,512]{1,0:T(4,128)S(1)} copy-done((f32[4,512]{1,0:T(4,128)S(1)}, f32[4,512]{1,0:T(4,128)}, u32[]{:S(2)}) %copy-start.4) | copy-done | bytes 8216
  12.7 0.0 copy-done.5
  12.7 3.4 %inner.1 = (f32[4,256,128]{2,1,0:T(8,128)S(1)}, f32[256,512]{1,0:T(8,128)S(1)}, f32[16,512]{1,0:T(8,128)S(1)}, f32[4,64,128]{2,1,0:T(8,128)S(1)}, f32[256,128]{1...) custom-call(bf16[48,256]{1,0:T(8,128)(2,1)S(1)} %bitcast.13, ...), custom_call_target="tpu_custom_call" | custom-call | flops 159383552 | bytes 4194304 | tf_op jit(solution)/shard_map/inner/pallas_call | solution.py:437
  16.1 0.0 collective-permute-done.2.before_ref
  16.1 0.0 collective-permute-done.3.after_ref
  16.1 1.2 %conv_scan.1 = (f32[4,256,128]{2,1,0:T(8,128)S(1)}, f32[4,256,128]{2,1,0:T(8,128)S(1)}, bf16[8,144,128]{2,1,0:T(8,128)(2,1)S(1)}) custom-call(bf16[72,256]{1,0:T(8,128)(2,1)S(1)} %collective-permute-done.2.before_ref, bf16[72,256]{1,0:T(8,128)(2,1)S(1)} %collective-permute-done.3.after_ref, ...), custom_call_target="tpu_custom_call", output_to_operand_aliasing={{0}: (10, {})} | custom-call | tf_op jit(solution)/shard_map/conv_scan/pallas_call | solution.py:450
  17.4 17.3 %all_to_all.10.near_ref = bf16[8,144,128]{2,1,0:T(8,128)(2,1)S(1)} all-to-all(bf16[8,144,128]{2,1,0:T(8,128)(2,1)S(1)} %get-tuple-element.28), channel_id=1, replica_groups={{0,1,2,3,32,33,34,35},{4,5,6,7,36,37,38,39},{8,9,10,11,40,41,42,43},{12..., dimensions={0} | all-to-all | bytes 589824 | tf_op jit(solution)/shard_map/all_to_all | solution.py:413
  34.6 0.1 totals.1
  34.7 11.0 %all_to_all.11.far_ref = bf16[8,144,128]{2,1,0:T(8,128)(2,1)S(1)} all-to-all(bf16[8,144,128]{2,1,0:T(8,128)(2,1)S(1)} %totals.1), channel_id=1, replica_groups={{0,4,8,12,16,20,24,28},{1,5,9,13,17,21,25,29},{2,6,10,14,18,22,26,30},{..., dimensions={0} | all-to-all | bytes 589824 | tf_op jit(solution)/shard_map/all_to_all | solution.py:413
  45.8 0.2 enter.1
  46.0 12.1 %collective-permute-start.4 = (bf16[128,128]{1,0:T(8,128)(2,1)S(1)}, bf16[128,128]{1,0:T(8,128)(2,1)S(1)}, u32[]{:S(2)}, u32[]{:S(2)}) collective-permute-start(bf16[128,128]{1,0:T(8,128)(2,1)S(1)} %get-tuple-element.30), channel_id=1, source_target_pairs={{0,32},{32,0},{64,96},{96,64},{128,160},{160,128},{192,224},{224,1... | collective-permute-start | bytes 98312 | tf_op jit(solution)/shard_map/ppermute | solution.py:481
  58.1 0.0 copy-start.3
  58.1 0.6 %own_axis.1 = (f32[4,256,128]{2,1,0:T(8,128)S(1)}, f32[4,256,128]{2,1,0:T(8,128)S(1)}, f32[4,256,128]{2,1,0:T(8,128)S(1)}) custom-call(f32[128,128]{1,0:T(8,128)S(1)} %get-tuple-element.31.keep_ref, f32[16,512]{1,0:T(8,128)S(1)} %get-tuple-element.21.cst_ref, f32[256,128]{1,0:T(8,128)S(1)} %get-tuple-element.22.g_ref, ...), custom_call_target="tpu_custom_call" | custom-call | flops 786432 | bytes 2097152 | tf_op jit(solution)/shard_map/own_axis/pallas_call | solution.py:483
  58.7 0.2 collective-permute-done.4.got_ref
  58.9 0.1 copy-done.3
  59.0 1.0 %finish.1 = bf16[256,256]{1,0:T(8,128)(2,1)} custom-call(bf16[128,128]{1,0:T(8,128)(2,1)S(1)} %collective-permute-done.4.got_ref, f32[16,512]{1,0:T(8,128)S(1)} %get-tuple-element.21.cst_ref, f32[256,128]{1,0:T(8,128)S(1)} %get-tuple-element.22.g_ref, f32[4,256,128]{2,1,0:T(8,128)S(1)} %get-tuple-element.33.sum_ref, ...), custom_call_target="tpu_custom_call" | custom-call | tf_op jit(solution)/shard_map/finish/pallas_call | solution.py:492
  (10 shorter events, 0.1 us)
Async XLA Ops:
  0.0 6.5 %copy-start.1 = (bf16[16,16,256]{2,1,0:T(8,128)(2,1)S(1)}, bf16[16,16,256]{2,1,0:T(8,128)(2,1)}, u32[]{:S(2)}) copy-start(bf16[16,16,256]{2,1,0:T(8,128)(2,1)} %param.6) | copy-start | bytes 393220
  0.0 12.0 %copy-start = (bf16[256,1024]{1,0:T(8,128)(2,1)S(1)}, bf16[256,1024]{1,0:T(8,128)(2,1)}, u32[]{:S(2)}) copy-start(bf16[256,1024]{1,0:T(8,128)(2,1)} %wv_ref.1) | copy-start | bytes 1572868
  0.8 5.8 %collective-permute-start.1 = (bf16[3,16,256]{2,0,1:T(4,128)(2,1)S(1)}, bf16[3,16,256]{2,0,1:T(4,128)(2,1)S(1)}, u32[]{:S(2)}, u32[]{:S(2)}) collective-permute-start(bf16[3,16,256]{2,0,1:T(4,128)(2,1)S(1)} %copy.18), channel_id=1, source_target_pairs={{32,0},{64,32},{96,64},{128,96},{160,128},{192,160},{224,192},{256... | collective-permute-start | bytes 73736 | tf_op jit(solution)/shard_map/ppermute | solution.py:397
  3.5 4.0 %collective-permute-start = (bf16[3,16,256]{2,0,1:T(4,128)(2,1)S(1)}, bf16[3,16,256]{2,0,1:T(4,128)(2,1)S(1)}, u32[]{:S(2)}, u32[]{:S(2)}) collective-permute-start(bf16[3,16,256]{2,0,1:T(4,128)(2,1)S(1)} %copy.16), channel_id=1, source_target_pairs={{0,32},{32,64},{64,96},{96,128},{128,160},{160,192},{192,224},{224... | collective-permute-start | bytes 73736 | tf_op jit(solution)/shard_map/ppermute | solution.py:397
  7.5 4.6 %copy-start.2 = (f32[7,7,512]{2,1,0:T(8,128)S(1)}, f32[7,7,512]{2,1,0:T(8,128)}, u32[]{:S(2)}) copy-start(f32[7,7,512]{2,1,0:T(8,128)} %taps_ref.3) | copy-start | bytes 301060
  7.6 8.6 %collective-permute-start.2 = (bf16[72,256]{1,0:T(8,128)(2,1)S(1)}, bf16[72,256]{1,0:T(8,128)(2,1)S(1)}, u32[]{:S(2)}, u32[]{:S(2)}) collective-permute-start(bf16[72,256]{1,0:T(8,128)(2,1)S(1)} %bitcast.15), channel_id=1, source_target_pairs={{0,1},{1,2},{2,3},{3,4},{4,5},{5,6},{6,7},{7,8},{8,9},{9,10},{10,1... | collective-permute-start | bytes 110600 | tf_op jit(solution)/shard_map/ppermute | solution.py:397
  10.7 5.4 %collective-permute-start.3 = (bf16[72,256]{1,0:T(8,128)(2,1)S(1)}, bf16[72,256]{1,0:T(8,128)(2,1)S(1)}, u32[]{:S(2)}, u32[]{:S(2)}) collective-permute-start(bf16[72,256]{1,0:T(8,128)(2,1)S(1)} %bitcast.14), channel_id=1, source_target_pairs={{1,0},{2,1},{3,2},{4,3},{5,4},{6,5},{7,6},{8,7},{9,8},{10,9},{11,1... | collective-permute-start | bytes 110600 | tf_op jit(solution)/shard_map/ppermute | solution.py:397
  12.0 0.7 %copy-start.4 = (f32[4,512]{1,0:T(4,128)S(1)}, f32[4,512]{1,0:T(4,128)}, u32[]{:S(2)}) copy-start(f32[4,512]{1,0:T(4,128)} %table_ref.1) | copy-start | bytes 24580
  12.0 0.7 %copy-start.5 = (f32[16,16]{1,0:T(8,128)S(1)}, f32[16,16]{1,0:T(8,128)}, u32[]{:S(2)}) copy-start(f32[16,16]{1,0:T(8,128)} %extra_ref.1) | copy-start | bytes 3076
  46.0 13.0 %collective-permute-start.4 = (bf16[128,128]{1,0:T(8,128)(2,1)S(1)}, bf16[128,128]{1,0:T(8,128)(2,1)S(1)}, u32[]{:S(2)}, u32[]{:S(2)}) collective-permute-start(bf16[128,128]{1,0:T(8,128)(2,1)S(1)} %get-tuple-element.30), channel_id=1, source_target_pairs={{0,32},{32,0},{64,96},{96,64},{128,160},{160,128},{192,224},{224,1... | collective-permute-start | bytes 98312 | tf_op jit(solution)/shard_map/ppermute | solution.py:481
  58.1 1.0 %copy-start.3 = (bf16[512,256]{1,0:T(8,128)(2,1)S(1)}, bf16[512,256]{1,0:T(8,128)(2,1)}, u32[]{:S(2)}) copy-start(bf16[512,256]{1,0:T(8,128)(2,1)} %wo_ref.1) | copy-start | bytes 786436

commit v10 on v9

--- a/solution.py
+++ b/solution.py
@@ -95,8 +95,9 @@
     spread_decays(table_ref, extra_ref, cst_ref, whole_ref, g_ref, across_ref, tails_ref,
                   (along_ref, down_ref), (ha_ref, hd_ref))
     for ct in range(groups):
-        for j in (0, 1, 2, T + 3, T + 4, T + 5):
-            v_ref[ct, pl.ds(j, PW, stride=PW), :] = jnp.zeros((PW, LANES), F32)
+        for r in range(T + 6):
+            for j in (0, 2 * 8):
+                v_ref[ct, pl.ds(r * PW + j, 8), :] = jnp.zeros((8, LANES), F32)
     for ref, first in ((above_ref, 0), (tok_ref, 3), (below_ref, T + 3)):
         count = ref.shape[0] // T
 
@@ -163,21 +164,6 @@
             vals = [x / (1.0 + jnp.exp(-x)) for x in acc]
             for i in range(T):
                 val_ref[pl.ds(i * T + jt * 8, 8), :] = vals[i]
-            state = jnp.zeros((8, LANES), F32)
-            downs = []
-            for i in range(T):
-                at = pl.ds(i * T + jt * 8, 8)
-                d, f = flow(2, at, vals[i])
-                state = d * state + f
-                downs.append(state)
-            end_ref[1, pl.ds(0 + ct * T + jt * 8, 8), :] = state
-            state = jnp.zeros((8, LANES), F32)
-            for i in reversed(range(T)):
-                at = pl.ds(i * T + jt * 8, 8)
-                d, f = flow(3, at, vals[i])
-                state = d * state + f
-                sum_ref[ct, at, :] = downs[i] + state
-            end_ref[1, pl.ds(64 + ct * T + jt * 8, 8), :] = state
         for it in range(2):
             values = [val_ref[pl.ds(it * 8 * T + j, 8, stride=T), :] for j in range(T)]
             state = jnp.zeros((8, LANES), F32)
@@ -192,8 +178,24 @@
                 at = pl.ds(it * 8 * T + j, 8, stride=T)
                 d, f = flow(1, pl.ds(j * T + it * 8, 8), values[j])
                 state = d * state + f
-                sum_ref[ct, at, :] = sum_ref[ct, at, :] + (lefts[j] + state)
+                sum_ref[ct, at, :] = lefts[j] + state
             end_ref[0, pl.ds(64 + ct * T + it * 8, 8), :] = state
+        for jt in range(2):
+            state = jnp.zeros((8, LANES), F32)
+            downs = []
+            for i in range(T):
+                at = pl.ds(i * T + jt * 8, 8)
+                d, f = flow(2, at, val_ref[at, :])
+                state = d * state + f
+                downs.append(state)
+            end_ref[1, pl.ds(0 + ct * T + jt * 8, 8), :] = state
+            state = jnp.zeros((8, LANES), F32)
+            for i in reversed(range(T)):
+                at = pl.ds(i * T + jt * 8, 8)
+                d, f = flow(3, at, val_ref[at, :])
+                state = d * state + f
+                sum_ref[ct, at, :] = sum_ref[ct, at, :] + (downs[i] + state)
+            end_ref[1, pl.ds(64 + ct * T + jt * 8, 8), :] = state
         return carry
 
     lax.fori_loop(0, groups, group, 0)

time: 60.5 us -> 60.4 us (level)
  no operation moved by 1% of the time
where the time goes in v10:
time: 60.4 us; the launch traced here: 60 us
  blocking collectives  28.3 us (47%)
  starting transfers between devices  22.1 us (37%)
  Pallas kernels  6.55 us (11%)
  local copies, waits for them, and re-layouts  1.81 us (3%)
  waiting for transfers between devices  1.02 us (2%)
    all_to_all x2, blocking collectives, swap(): lax.all_to_all(x, ('row', 'col'), 0, 0, axis_index_groups=groups, tiled=T...  28.3 us
    ppermute x1, starting transfers between devices, body(): got = lax.ppermute(give, 'row', [(i, i ^ 1) for i in range(rows)])  12.1 us
    ppermute x4, starting transfers between devices, neighbours(): return (lax.ppermute(x_last, axis, up), lax.ppermute(x_first, axis, down))  9.97 us
    pallas_call x1, Pallas kernels, body(): pl.pallas_call(inner_kernel, out_shape=(tile, jax.ShapeDtypeStruct((PX, w...  3.39 us
    pallas_call x1, Pallas kernels, body(): pl.pallas_call(conv_scan_kernel, out_shape=(tile, tile, jax.ShapeDtypeStr...  1.21 us
  transfers between devices with their start and end apart: 5, of which 2 were waited for; matrix products, arithmetic and copies ran while one was open for 0% of the time, Pallas kernels for 7%

profile of v10, /device:TPU:33, one launch (start us, length us, event | category | flops | bytes accessed | tf_op | source)
XLA Modules:
  0.0 60.0 jit_solution(10904244352116665978)
XLA Ops:
  0.0 0.0 copy-start.1
  0.0 0.0 copy-start
  0.0 0.8 %fusion.1 = (bf16[3,16,256]{2,1,0:T(8,128)(2,1)S(1)}, bf16[3,16,256]{2,1,0:T(8,128)(2,1)S(1)}) fusion(bf16[16,16,256]{2,1,0:T(8,128)(2,1)} %param.6), kind=kLoop, calls=%fused_computation.3 | loop fusion | bytes 98304 | tf_op jit(solution)/shard_map/slice | solution.py:425
  0.8 2.6 %collective-permute-start.1 = (bf16[3,16,256]{2,0,1:T(4,128)(2,1)S(1)}, bf16[3,16,256]{2,0,1:T(4,128)(2,1)S(1)}, u32[]{:S(2)}, u32[]{:S(2)}) collective-permute-start(bf16[3,16,256]{2,0,1:T(4,128)(2,1)S(1)} %copy.18), channel_id=1, source_target_pairs={{32,0},{64,32},{96,64},{128,96},{160,128},{192,160},{224,192},{256... | collective-permute-start | bytes 73736 | tf_op jit(solution)/shard_map/ppermute | solution.py:399
  3.5 3.0 %collective-permute-start = (bf16[3,16,256]{2,0,1:T(4,128)(2,1)S(1)}, bf16[3,16,256]{2,0,1:T(4,128)(2,1)S(1)}, u32[]{:S(2)}, u32[]{:S(2)}) collective-permute-start(bf16[3,16,256]{2,0,1:T(4,128)(2,1)S(1)} %copy.16), channel_id=1, source_target_pairs={{0,32},{32,64},{64,96},{96,128},{128,160},{160,192},{192,224},{224... | collective-permute-start | bytes 73736 | tf_op jit(solution)/shard_map/ppermute | solution.py:399
  6.5 0.0 copy-done.1
  6.5 0.1 pad.7.clone
  6.6 0.0 collective-permute-done.1
  6.6 0.8 %collective-permute-done = bf16[3,16,256]{2,0,1:T(4,128)(2,1)S(1)} collective-permute-done((bf16[3,16,256]{2,0,1:T(4,128)(2,1)S(1)}, bf16[3,16,256]{2,0,1:T(4,128)(2,1)S(1)}, u32[]{:S(2)}, u32[]{:S(2)}) %collective-permute-start) | collective-permute-done | bytes 24608 | tf_op jit(solution)/shard_map/ppermute | solution.py:399
  7.5 0.0 copy-start.2
  7.5 0.1 maximum_maximum_fusion.1
  7.6 3.1 %collective-permute-start.2 = (bf16[72,256]{1,0:T(8,128)(2,1)S(1)}, bf16[72,256]{1,0:T(8,128)(2,1)S(1)}, u32[]{:S(2)}, u32[]{:S(2)}) collective-permute-start(bf16[72,256]{1,0:T(8,128)(2,1)S(1)} %bitcast.15), channel_id=1, source_target_pairs={{0,1},{1,2},{2,3},{3,4},{4,5},{5,6},{6,7},{7,8},{8,9},{9,10},{10,1... | collective-permute-start | bytes 110600 | tf_op jit(solution)/shard_map/ppermute | solution.py:399
  10.7 1.3 %collective-permute-start.3 = (bf16[72,256]{1,0:T(8,128)(2,1)S(1)}, bf16[72,256]{1,0:T(8,128)(2,1)S(1)}, u32[]{:S(2)}, u32[]{:S(2)}) collective-permute-start(bf16[72,256]{1,0:T(8,128)(2,1)S(1)} %bitcast.14), channel_id=1, source_target_pairs={{1,0},{2,1},{3,2},{4,3},{5,4},{6,5},{7,6},{8,7},{9,8},{10,9},{11,1... | collective-permute-start | bytes 110600 | tf_op jit(solution)/shard_map/ppermute | solution.py:399
  12.0 0.0 copy-start.4
  12.0 0.0 copy-start.5
  12.0 0.0 copy-done
  12.0 0.0 copy-done.2
  12.1 0.6 %copy-done.4 = f32[4,512]{1,0:T(4,128)S(1)} copy-done((f32[4,512]{1,0:T(4,128)S(1)}, f32[4,512]{1,0:T(4,128)}, u32[]{:S(2)}) %copy-start.4) | copy-done | bytes 8216
  12.7 0.0 copy-done.5
  12.7 3.4 %inner.1 = (f32[4,256,128]{2,1,0:T(8,128)S(1)}, f32[256,512]{1,0:T(8,128)S(1)}, f32[16,512]{1,0:T(8,128)S(1)}, f32[4,64,128]{2,1,0:T(8,128)S(1)}, f32[256,128]{1...) custom-call(bf16[48,256]{1,0:T(8,128)(2,1)S(1)} %bitcast.13, ...), custom_call_target="tpu_custom_call" | custom-call | flops 159383552 | bytes 4194304 | tf_op jit(solution)/shard_map/inner/pallas_call | solution.py:439
  16.1 0.0 collective-permute-done.2.before_ref
  16.1 0.0 collective-permute-done.3.after_ref
  16.1 1.2 %conv_scan.1 = (f32[4,256,128]{2,1,0:T(8,128)S(1)}, f32[4,256,128]{2,1,0:T(8,128)S(1)}, bf16[8,144,128]{2,1,0:T(8,128)(2,1)S(1)}) custom-call(bf16[72,256]{1,0:T(8,128)(2,1)S(1)} %collective-permute-done.2.before_ref, bf16[72,256]{1,0:T(8,128)(2,1)S(1)} %collective-permute-done.3.after_ref, ...), custom_call_target="tpu_custom_call", output_to_operand_aliasing={{0}: (10, {})} | custom-call | tf_op jit(solution)/shard_map/conv_scan/pallas_call | solution.py:452
  17.3 17.3 %all_to_all.10.near_ref = bf16[8,144,128]{2,1,0:T(8,128)(2,1)S(1)} all-to-all(bf16[8,144,128]{2,1,0:T(8,128)(2,1)S(1)} %get-tuple-element.28), channel_id=1, replica_groups={{0,1,2,3,32,33,34,35},{4,5,6,7,36,37,38,39},{8,9,10,11,40,41,42,43},{12..., dimensions={0} | all-to-all | bytes 589824 | tf_op jit(solution)/shard_map/all_to_all | solution.py:415
  34.6 0.1 totals.1
  34.7 11.0 %all_to_all.11.far_ref = bf16[8,144,128]{2,1,0:T(8,128)(2,1)S(1)} all-to-all(bf16[8,144,128]{2,1,0:T(8,128)(2,1)S(1)} %totals.1), channel_id=1, replica_groups={{0,4,8,12,16,20,24,28},{1,5,9,13,17,21,25,29},{2,6,10,14,18,22,26,30},{..., dimensions={0} | all-to-all | bytes 589824 | tf_op jit(solution)/shard_map/all_to_all | solution.py:415
  45.8 0.2 enter.1
  45.9 12.1 %collective-permute-start.4 = (bf16[128,128]{1,0:T(8,128)(2,1)S(1)}, bf16[128,128]{1,0:T(8,128)(2,1)S(1)}, u32[]{:S(2)}, u32[]{:S(2)}) collective-permute-start(bf16[128,128]{1,0:T(8,128)(2,1)S(1)} %get-tuple-element.30), channel_id=1, source_target_pairs={{0,32},{32,0},{64,96},{96,64},{128,160},{160,128},{192,224},{224,1... | collective-permute-start | bytes 98312 | tf_op jit(solution)/shard_map/ppermute | solution.py:483
  58.0 0.0 copy-start.3
  58.0 0.6 %own_axis.1 = (f32[4,256,128]{2,1,0:T(8,128)S(1)}, f32[4,256,128]{2,1,0:T(8,128)S(1)}, f32[4,256,128]{2,1,0:T(8,128)S(1)}) custom-call(f32[128,128]{1,0:T(8,128)S(1)} %get-tuple-element.31.keep_ref, f32[16,512]{1,0:T(8,128)S(1)} %get-tuple-element.21.cst_ref, f32[256,128]{1,0:T(8,128)S(1)} %get-tuple-element.22.g_ref, ...), custom_call_target="tpu_custom_call" | custom-call | flops 786432 | bytes 2097152 | tf_op jit(solution)/shard_map/own_axis/pallas_call | solution.py:485
  58.7 0.2 collective-permute-done.4.got_ref
  58.9 0.1 copy-done.3
  59.0 1.0 %finish.1 = bf16[256,256]{1,0:T(8,128)(2,1)} custom-call(bf16[128,128]{1,0:T(8,128)(2,1)S(1)} %collective-permute-done.4.got_ref, f32[16,512]{1,0:T(8,128)S(1)} %get-tuple-element.21.cst_ref, f32[256,128]{1,0:T(8,128)S(1)} %get-tuple-element.22.g_ref, f32[4,256,128]{2,1,0:T(8,128)S(1)} %get-tuple-element.33.sum_ref, ...), custom_call_target="tpu_custom_call" | custom-call | tf_op jit(solution)/shard_map/finish/pallas_call | solution.py:494
  (10 shorter events, 0.1 us)
Async XLA Ops:
  0.0 6.5 %copy-start.1 = (bf16[16,16,256]{2,1,0:T(8,128)(2,1)S(1)}, bf16[16,16,256]{2,1,0:T(8,128)(2,1)}, u32[]{:S(2)}) copy-start(bf16[16,16,256]{2,1,0:T(8,128)(2,1)} %param.6) | copy-start | bytes 393220
  0.0 12.0 %copy-start = (bf16[256,1024]{1,0:T(8,128)(2,1)S(1)}, bf16[256,1024]{1,0:T(8,128)(2,1)}, u32[]{:S(2)}) copy-start(bf16[256,1024]{1,0:T(8,128)(2,1)} %wv_ref.1) | copy-start | bytes 1572868
  0.8 5.8 %collective-permute-start.1 = (bf16[3,16,256]{2,0,1:T(4,128)(2,1)S(1)}, bf16[3,16,256]{2,0,1:T(4,128)(2,1)S(1)}, u32[]{:S(2)}, u32[]{:S(2)}) collective-permute-start(bf16[3,16,256]{2,0,1:T(4,128)(2,1)S(1)} %copy.18), channel_id=1, source_target_pairs={{32,0},{64,32},{96,64},{128,96},{160,128},{192,160},{224,192},{256... | collective-permute-start | bytes 73736 | tf_op jit(solution)/shard_map/ppermute | solution.py:399
  3.5 4.0 %collective-permute-start = (bf16[3,16,256]{2,0,1:T(4,128)(2,1)S(1)}, bf16[3,16,256]{2,0,1:T(4,128)(2,1)S(1)}, u32[]{:S(2)}, u32[]{:S(2)}) collective-permute-start(bf16[3,16,256]{2,0,1:T(4,128)(2,1)S(1)} %copy.16), channel_id=1, source_target_pairs={{0,32},{32,64},{64,96},{96,128},{128,160},{160,192},{192,224},{224... | collective-permute-start | bytes 73736 | tf_op jit(solution)/shard_map/ppermute | solution.py:399
  7.5 4.6 %copy-start.2 = (f32[7,7,512]{2,1,0:T(8,128)S(1)}, f32[7,7,512]{2,1,0:T(8,128)}, u32[]{:S(2)}) copy-start(f32[7,7,512]{2,1,0:T(8,128)} %taps_ref.3) | copy-start | bytes 301060
  7.6 8.5 %collective-permute-start.2 = (bf16[72,256]{1,0:T(8,128)(2,1)S(1)}, bf16[72,256]{1,0:T(8,128)(2,1)S(1)}, u32[]{:S(2)}, u32[]{:S(2)}) collective-permute-start(bf16[72,256]{1,0:T(8,128)(2,1)S(1)} %bitcast.15), channel_id=1, source_target_pairs={{0,1},{1,2},{2,3},{3,4},{4,5},{5,6},{6,7},{7,8},{8,9},{9,10},{10,1... | collective-permute-start | bytes 110600 | tf_op jit(solution)/shard_map/ppermute | solution.py:399
  10.7 5.4 %collective-permute-start.3 = (bf16[72,256]{1,0:T(8,128)(2,1)S(1)}, bf16[72,256]{1,0:T(8,128)(2,1)S(1)}, u32[]{:S(2)}, u32[]{:S(2)}) collective-permute-start(bf16[72,256]{1,0:T(8,128)(2,1)S(1)} %bitcast.14), channel_id=1, source_target_pairs={{1,0},{2,1},{3,2},{4,3},{5,4},{6,5},{7,6},{8,7},{9,8},{10,9},{11,1... | collective-permute-start | bytes 110600 | tf_op jit(solution)/shard_map/ppermute | solution.py:399
  12.0 0.7 %copy-start.4 = (f32[4,512]{1,0:T(4,128)S(1)}, f32[4,512]{1,0:T(4,128)}, u32[]{:S(2)}) copy-start(f32[4,512]{1,0:T(4,128)} %table_ref.1) | copy-start | bytes 24580
  12.0 0.7 %copy-start.5 = (f32[16,16]{1,0:T(8,128)S(1)}, f32[16,16]{1,0:T(8,128)}, u32[]{:S(2)}) copy-start(f32[16,16]{1,0:T(8,128)} %extra_ref.1) | copy-start | bytes 3076
  45.9 12.9 %collective-permute-start.4 = (bf16[128,128]{1,0:T(8,128)(2,1)S(1)}, bf16[128,128]{1,0:T(8,128)(2,1)S(1)}, u32[]{:S(2)}, u32[]{:S(2)}) collective-permute-start(bf16[128,128]{1,0:T(8,128)(2,1)S(1)} %get-tuple-element.30), channel_id=1, source_target_pairs={{0,32},{32,0},{64,96},{96,64},{128,160},{160,128},{192,224},{224,1... | collective-permute-start | bytes 98312 | tf_op jit(solution)/shard_map/ppermute | solution.py:483
  58.0 1.0 %copy-start.3 = (bf16[512,256]{1,0:T(8,128)(2,1)S(1)}, bf16[512,256]{1,0:T(8,128)(2,1)}, u32[]{:S(2)}) copy-start(bf16[512,256]{1,0:T(8,128)(2,1)} %wo_ref.1) | copy-start | bytes 786436

commit v11 on v10

--- a/solution.py
+++ b/solution.py
@@ -47,7 +47,7 @@
     return jnp.where(x < 0.1, series, 1.0 - jnp.exp(-x))
 
 
-def spread_decays(table_ref, extra_ref, cst_ref, whole_ref, g_ref, across_ref, tails_ref, flow_refs, h_refs):
+def spread_decays(table_ref, extra_ref, cst_ref, whole_ref, g_ref, across_ref, tails_ref, h_refs):
     table = table_ref[...]
     cst_ref[0:4] = jnp.exp(-table)
     cst_ref[4:8] = fall(2.0 * table)
@@ -77,23 +77,11 @@
         high = decay.astype(BF16).astype(F32)
         tails_ref[k] = jnp.where(lane < 64, high, decay - high).astype(BF16)
 
-    def group(ct, carry):
-        lanes = pl.ds(pl.multiple_of(ct * LANES, LANES), LANES)
-        for d in range(4):
-            base, slope = cst_ref[pl.ds(4 + d, 1), lanes], cst_ref[pl.ds(8 + d, 1), lanes]
-            q = base + slope * h_refs[d // 2][...]
-            flow_refs[d // 2][d % 2, ct] = q * lax.rsqrt(q)
-        return carry
-
-    lax.fori_loop(0, flow_refs[0].shape[1], group, 0)
-
 
 def inner_kernel(above_ref, tok_ref, below_ref, weight_ref, taps_ref, table_ref, extra_ref,
-                 acc_ref, gate_ref, cst_ref, whole_ref, g_ref, across_ref, tails_ref, along_ref, down_ref,
-                 v_ref, ha_ref, hd_ref):
+                 acc_ref, gate_ref, cst_ref, whole_ref, g_ref, across_ref, tails_ref, ha_ref, hd_ref, v_ref):
     groups = v_ref.shape[0]
-    spread_decays(table_ref, extra_ref, cst_ref, whole_ref, g_ref, across_ref, tails_ref,
-                  (along_ref, down_ref), (ha_ref, hd_ref))
+    spread_decays(table_ref, extra_ref, cst_ref, whole_ref, g_ref, across_ref, tails_ref, (ha_ref, hd_ref))
     for ct in range(groups):
         for r in range(T + 6):
             for j in (0, 2 * 8):
@@ -123,7 +111,7 @@
     lax.fori_loop(0, groups, group, 0)
 
 
-def conv_scan_kernel(before_ref, after_ref, wv_ref, taps_ref, cst_ref, g_ref, across_ref, along_ref, down_ref,
+def conv_scan_kernel(before_ref, after_ref, wv_ref, taps_ref, cst_ref, g_ref, across_ref, ha_ref, hd_ref,
                      tails_ref, own_ref, acc_ref, sum_ref, near_ref, side_ref, line_ref, val_ref, end_ref):
     del own_ref
     groups = line_ref.shape[0]
@@ -137,11 +125,12 @@
 
     def group(ct, carry):
         lanes = pl.ds(pl.multiple_of(ct * LANES, LANES), LANES)
-        cst = [cst_ref[pl.ds(k, 1), lanes] for k in range(4)]
+        cst = [cst_ref[pl.ds(k, 1), lanes] for k in range(12)]
 
         def flow(d, at, x):
-            g, factor = ((across_ref, along_ref), (g_ref, down_ref))[d // 2]
-            return cst[d] * g[at, :], factor[d % 2, ct, at, :] * x
+            g, h = ((across_ref, ha_ref), (g_ref, hd_ref))[d // 2]
+            q = cst[4 + d] + cst[8 + d] * h[at, :]
+            return cst[d] * g[at, :], q * lax.rsqrt(q) * x
 
         for side in range(2):
             outs = range(3) if side == 0 else range(T - 3, T)
@@ -435,16 +424,15 @@
     params = pltpu.CompilerParams(vmem_limit_bytes=16 * 2**20)
     tile = jax.ShapeDtypeStruct((groups, PX, LANES), F32)
     spread = jax.ShapeDtypeStruct((PX, LANES), F32)
-    factor = jax.ShapeDtypeStruct((2, groups, PX, LANES), F32)
-    own, gate, cst, whole, g, across, tails, along, downward = pl.pallas_call(
+    own, gate, cst, whole, g, across, tails, ha, hd = pl.pallas_call(
         inner_kernel,
         out_shape=(tile, jax.ShapeDtypeStruct((PX, width), F32), jax.ShapeDtypeStruct((16, width), F32),
                    jax.ShapeDtypeStruct((4, groups * T, LANES), F32),
                    spread, spread, jax.ShapeDtypeStruct((2, T, LANES), BF16),
-                   factor, factor),
+                   spread, spread),
         in_specs=[spec] * 7,
         out_specs=(spec,) * 9,
-        scratch_shapes=[VMEM((groups, PW * PW, LANES), F32), VMEM((PX, LANES), F32), VMEM((PX, LANES), F32)],
+        scratch_shapes=[VMEM((groups, PW * PW, LANES), F32)],
         compiler_params=params,
         cost_estimate=pl.CostEstimate(flops=2 * 608 * channels * width, bytes_accessed=4 * 2**20, transcendentals=0),
         name="inner",
@@ -459,7 +447,7 @@
         input_output_aliases={10: 0},
         compiler_params=params,
         name="conv_scan",
-    )(before, after, input_weight, kernel, cst, g, across, along, downward, tails, own)
+    )(before, after, input_weight, kernel, cst, g, across, ha, hd, tails, own)
     near = swap(near, near_groups(rows, cols))
 
     far = pl.pallas_call(

time: 60.4 us -> 60.4 us (level)
  blocking collectives: 28.3 us -> 29 us
    pallas_call x1, Pallas kernels: 3.39 us -> 2.69 us  [body(): pl.pallas_call(inner_kernel, out_shape=(tile, jax.ShapeDtypeStruct((PX, w...]
    all_to_all x2, blocking collectives: 28.3 us -> 29 us  [swap(): lax.all_to_all(x, ('row', 'col'), 0, 0, axis_index_groups=groups, tiled=T...]
  transfers between devices with their start and end apart: 5 -> 5, of which waited for: 2 -> 2; matrix products, arithmetic and copies ran while one was open for 0% -> 0% of each run, Pallas kernels for 7% -> 6%
where the time goes in v11:
time: 60.4 us; the launch traced here: 60 us
  blocking collectives  29 us (48%)
  starting transfers between devices  21.8 us (36%)
  Pallas kernels  6.1 us (10%)
  local copies, waits for them, and re-layouts  1.81 us (3%)
  waiting for transfers between devices  1.02 us (2%)
    all_to_all x2, blocking collectives, swap(): lax.all_to_all(x, ('row', 'col'), 0, 0, axis_index_groups=groups, tiled=T...  29 us
    ppermute x1, starting transfers between devices, body(): got = lax.ppermute(give, 'row', [(i, i ^ 1) for i in range(rows)])  11.8 us
    ppermute x4, starting transfers between devices, neighbours(): return (lax.ppermute(x_last, axis, up), lax.ppermute(x_first, axis, down))  9.97 us
    pallas_call x1, Pallas kernels, body(): pl.pallas_call(inner_kernel, out_shape=(tile, jax.ShapeDtypeStruct((PX, w...  2.69 us
    pallas_call x1, Pallas kernels, body(): pl.pallas_call(conv_scan_kernel, out_shape=(tile, tile, jax.ShapeDtypeStr...  1.45 us
  transfers between devices with their start and end apart: 5, of which 2 were waited for; matrix products, arithmetic and copies ran while one was open for 0% of the time, Pallas kernels for 6%

profile of v11, /device:TPU:33, one launch (start us, length us, event | category | flops | bytes accessed | tf_op | source)
XLA Modules:
  0.0 60.0 jit_solution(6976406009290808957)
XLA Ops:
  0.0 0.0 copy-start.1
  0.0 0.0 copy-start
  0.0 0.8 %fusion.1 = (bf16[3,16,256]{2,1,0:T(8,128)(2,1)S(1)}, bf16[3,16,256]{2,1,0:T(8,128)(2,1)S(1)}) fusion(bf16[16,16,256]{2,1,0:T(8,128)(2,1)} %param.6), kind=kLoop, calls=%fused_computation.3 | loop fusion | bytes 98304 | tf_op jit(solution)/shard_map/slice | solution.py:414
  0.8 2.6 %collective-permute-start.1 = (bf16[3,16,256]{2,0,1:T(4,128)(2,1)S(1)}, bf16[3,16,256]{2,0,1:T(4,128)(2,1)S(1)}, u32[]{:S(2)}, u32[]{:S(2)}) collective-permute-start(bf16[3,16,256]{2,0,1:T(4,128)(2,1)S(1)} %copy.18), channel_id=1, source_target_pairs={{32,0},{64,32},{96,64},{128,96},{160,128},{192,160},{224,192},{256... | collective-permute-start | bytes 73736 | tf_op jit(solution)/shard_map/ppermute | solution.py:388
  3.5 3.0 %collective-permute-start = (bf16[3,16,256]{2,0,1:T(4,128)(2,1)S(1)}, bf16[3,16,256]{2,0,1:T(4,128)(2,1)S(1)}, u32[]{:S(2)}, u32[]{:S(2)}) collective-permute-start(bf16[3,16,256]{2,0,1:T(4,128)(2,1)S(1)} %copy.16), channel_id=1, source_target_pairs={{0,32},{32,64},{64,96},{96,128},{128,160},{160,192},{192,224},{224... | collective-permute-start | bytes 73736 | tf_op jit(solution)/shard_map/ppermute | solution.py:388
  6.5 0.0 copy-done.1
  6.5 0.1 pad.7.clone
  6.6 0.0 collective-permute-done.1
  6.6 0.8 %collective-permute-done = bf16[3,16,256]{2,0,1:T(4,128)(2,1)S(1)} collective-permute-done((bf16[3,16,256]{2,0,1:T(4,128)(2,1)S(1)}, bf16[3,16,256]{2,0,1:T(4,128)(2,1)S(1)}, u32[]{:S(2)}, u32[]{:S(2)}) %collective-permute-start) | collective-permute-done | bytes 24608 | tf_op jit(solution)/shard_map/ppermute | solution.py:388
  7.5 0.0 copy-start.2
  7.5 0.1 maximum_maximum_fusion.1
  7.6 3.1 %collective-permute-start.2 = (bf16[72,256]{1,0:T(8,128)(2,1)S(1)}, bf16[72,256]{1,0:T(8,128)(2,1)S(1)}, u32[]{:S(2)}, u32[]{:S(2)}) collective-permute-start(bf16[72,256]{1,0:T(8,128)(2,1)S(1)} %bitcast.15), channel_id=1, source_target_pairs={{0,1},{1,2},{2,3},{3,4},{4,5},{5,6},{6,7},{7,8},{8,9},{9,10},{10,1... | collective-permute-start | bytes 110600 | tf_op jit(solution)/shard_map/ppermute | solution.py:388
  10.7 1.3 %collective-permute-start.3 = (bf16[72,256]{1,0:T(8,128)(2,1)S(1)}, bf16[72,256]{1,0:T(8,128)(2,1)S(1)}, u32[]{:S(2)}, u32[]{:S(2)}) collective-permute-start(bf16[72,256]{1,0:T(8,128)(2,1)S(1)} %bitcast.14), channel_id=1, source_target_pairs={{1,0},{2,1},{3,2},{4,3},{5,4},{6,5},{7,6},{8,7},{9,8},{10,9},{11,1... | collective-permute-start | bytes 110600 | tf_op jit(solution)/shard_map/ppermute | solution.py:388
  12.0 0.0 copy-start.4
  12.0 0.0 copy-start.5
  12.0 0.0 copy-done
  12.0 0.0 copy-done.2
  12.1 0.6 %copy-done.4 = f32[4,512]{1,0:T(4,128)S(1)} copy-done((f32[4,512]{1,0:T(4,128)S(1)}, f32[4,512]{1,0:T(4,128)}, u32[]{:S(2)}) %copy-start.4) | copy-done | bytes 8216
  12.7 0.0 copy-done.5
  12.7 2.7 %inner.1 = (f32[4,256,128]{2,1,0:T(8,128)S(1)}, f32[256,512]{1,0:T(8,128)S(1)}, f32[16,512]{1,0:T(8,128)S(1)}, f32[4,64,128]{2,1,0:T(8,128)S(1)}, f32[256,128]{1...) custom-call(bf16[48,256]{1,0:T(8,128)(2,1)S(1)} %bitcast.13, ...), custom_call_target="tpu_custom_call" | custom-call | flops 159383552 | bytes 4194304 | tf_op jit(solution)/shard_map/inner/pallas_call | solution.py:427
  15.4 0.0 collective-permute-done.2.before_ref
  15.4 0.0 collective-permute-done.3.after_ref
  15.4 1.5 %conv_scan.1 = (f32[4,256,128]{2,1,0:T(8,128)S(1)}, f32[4,256,128]{2,1,0:T(8,128)S(1)}, bf16[8,144,128]{2,1,0:T(8,128)(2,1)S(1)}) custom-call(bf16[72,256]{1,0:T(8,128)(2,1)S(1)} %collective-permute-done.2.before_ref, bf16[72,256]{1,0:T(8,128)(2,1)S(1)} %collective-permute-done.3.after_ref, ...), custom_call_target="tpu_custom_call", output_to_operand_aliasing={{0}: (10, {})} | custom-call | tf_op jit(solution)/shard_map/conv_scan/pallas_call | solution.py:440
  16.9 18.0 %all_to_all.10.near_ref = bf16[8,144,128]{2,1,0:T(8,128)(2,1)S(1)} all-to-all(bf16[8,144,128]{2,1,0:T(8,128)(2,1)S(1)} %get-tuple-element.28), channel_id=1, replica_groups={{0,1,2,3,32,33,34,35},{4,5,6,7,36,37,38,39},{8,9,10,11,40,41,42,43},{12..., dimensions={0} | all-to-all | bytes 589824 | tf_op jit(solution)/shard_map/all_to_all | solution.py:404
  34.9 0.1 totals.1
  35.0 11.0 %all_to_all.11.far_ref = bf16[8,144,128]{2,1,0:T(8,128)(2,1)S(1)} all-to-all(bf16[8,144,128]{2,1,0:T(8,128)(2,1)S(1)} %totals.1), channel_id=1, replica_groups={{0,4,8,12,16,20,24,28},{1,5,9,13,17,21,25,29},{2,6,10,14,18,22,26,30},{..., dimensions={0} | all-to-all | bytes 589824 | tf_op jit(solution)/shard_map/all_to_all | solution.py:404
  46.0 0.2 enter.1
  46.2 11.8 %collective-permute-start.4 = (bf16[128,128]{1,0:T(8,128)(2,1)S(1)}, bf16[128,128]{1,0:T(8,128)(2,1)S(1)}, u32[]{:S(2)}, u32[]{:S(2)}) collective-permute-start(bf16[128,128]{1,0:T(8,128)(2,1)S(1)} %get-tuple-element.30), channel_id=1, source_target_pairs={{0,32},{32,0},{64,96},{96,64},{128,160},{160,128},{192,224},{224,1... | collective-permute-start | bytes 98312 | tf_op jit(solution)/shard_map/ppermute | solution.py:471
  58.0 0.0 copy-start.3
  58.0 0.6 %own_axis.1 = (f32[4,256,128]{2,1,0:T(8,128)S(1)}, f32[4,256,128]{2,1,0:T(8,128)S(1)}, f32[4,256,128]{2,1,0:T(8,128)S(1)}) custom-call(f32[128,128]{1,0:T(8,128)S(1)} %get-tuple-element.31.keep_ref, f32[16,512]{1,0:T(8,128)S(1)} %get-tuple-element.21.cst_ref, f32[256,128]{1,0:T(8,128)S(1)} %get-tuple-element.22.g_ref, ...), custom_call_target="tpu_custom_call" | custom-call | flops 786432 | bytes 2097152 | tf_op jit(solution)/shard_map/own_axis/pallas_call | solution.py:473
  58.7 0.2 collective-permute-done.4.got_ref
  58.8 0.1 copy-done.3
  59.0 1.0 %finish.1 = bf16[256,256]{1,0:T(8,128)(2,1)} custom-call(bf16[128,128]{1,0:T(8,128)(2,1)S(1)} %collective-permute-done.4.got_ref, f32[16,512]{1,0:T(8,128)S(1)} %get-tuple-element.21.cst_ref, f32[256,128]{1,0:T(8,128)S(1)} %get-tuple-element.22.g_ref, f32[4,256,128]{2,1,0:T(8,128)S(1)} %get-tuple-element.33.sum_ref, ...), custom_call_target="tpu_custom_call" | custom-call | tf_op jit(solution)/shard_map/finish/pallas_call | solution.py:482
  (10 shorter events, 0.1 us)
Async XLA Ops:
  0.0 6.5 %copy-start.1 = (bf16[16,16,256]{2,1,0:T(8,128)(2,1)S(1)}, bf16[16,16,256]{2,1,0:T(8,128)(2,1)}, u32[]{:S(2)}) copy-start(bf16[16,16,256]{2,1,0:T(8,128)(2,1)} %param.6) | copy-start | bytes 393220
  0.0 12.0 %copy-start = (bf16[256,1024]{1,0:T(8,128)(2,1)S(1)}, bf16[256,1024]{1,0:T(8,128)(2,1)}, u32[]{:S(2)}) copy-start(bf16[256,1024]{1,0:T(8,128)(2,1)} %wv_ref.1) | copy-start | bytes 1572868
  0.8 5.8 %collective-permute-start.1 = (bf16[3,16,256]{2,0,1:T(4,128)(2,1)S(1)}, bf16[3,16,256]{2,0,1:T(4,128)(2,1)S(1)}, u32[]{:S(2)}, u32[]{:S(2)}) collective-permute-start(bf16[3,16,256]{2,0,1:T(4,128)(2,1)S(1)} %copy.18), channel_id=1, source_target_pairs={{32,0},{64,32},{96,64},{128,96},{160,128},{192,160},{224,192},{256... | collective-permute-start | bytes 73736 | tf_op jit(solution)/shard_map/ppermute | solution.py:388
  3.5 4.0 %collective-permute-start = (bf16[3,16,256]{2,0,1:T(4,128)(2,1)S(1)}, bf16[3,16,256]{2,0,1:T(4,128)(2,1)S(1)}, u32[]{:S(2)}, u32[]{:S(2)}) collective-permute-start(bf16[3,16,256]{2,0,1:T(4,128)(2,1)S(1)} %copy.16), channel_id=1, source_target_pairs={{0,32},{32,64},{64,96},{96,128},{128,160},{160,192},{192,224},{224... | collective-permute-start | bytes 73736 | tf_op jit(solution)/shard_map/ppermute | solution.py:388
  7.5 4.6 %copy-start.2 = (f32[7,7,512]{2,1,0:T(8,128)S(1)}, f32[7,7,512]{2,1,0:T(8,128)}, u32[]{:S(2)}) copy-start(f32[7,7,512]{2,1,0:T(8,128)} %taps_ref.3) | copy-start | bytes 301060
  7.6 7.9 %collective-permute-start.2 = (bf16[72,256]{1,0:T(8,128)(2,1)S(1)}, bf16[72,256]{1,0:T(8,128)(2,1)S(1)}, u32[]{:S(2)}, u32[]{:S(2)}) collective-permute-start(bf16[72,256]{1,0:T(8,128)(2,1)S(1)} %bitcast.15), channel_id=1, source_target_pairs={{0,1},{1,2},{2,3},{3,4},{4,5},{5,6},{6,7},{7,8},{8,9},{9,10},{10,1... | collective-permute-start | bytes 110600 | tf_op jit(solution)/shard_map/ppermute | solution.py:388
  10.7 4.7 %collective-permute-start.3 = (bf16[72,256]{1,0:T(8,128)(2,1)S(1)}, bf16[72,256]{1,0:T(8,128)(2,1)S(1)}, u32[]{:S(2)}, u32[]{:S(2)}) collective-permute-start(bf16[72,256]{1,0:T(8,128)(2,1)S(1)} %bitcast.14), channel_id=1, source_target_pairs={{1,0},{2,1},{3,2},{4,3},{5,4},{6,5},{7,6},{8,7},{9,8},{10,9},{11,1... | collective-permute-start | bytes 110600 | tf_op jit(solution)/shard_map/ppermute | solution.py:388
  12.0 0.7 %copy-start.4 = (f32[4,512]{1,0:T(4,128)S(1)}, f32[4,512]{1,0:T(4,128)}, u32[]{:S(2)}) copy-start(f32[4,512]{1,0:T(4,128)} %table_ref.1) | copy-start | bytes 24580
  12.0 0.7 %copy-start.5 = (f32[16,16]{1,0:T(8,128)S(1)}, f32[16,16]{1,0:T(8,128)}, u32[]{:S(2)}) copy-start(f32[16,16]{1,0:T(8,128)} %extra_ref.1) | copy-start | bytes 3076
  46.2 12.7 %collective-permute-start.4 = (bf16[128,128]{1,0:T(8,128)(2,1)S(1)}, bf16[128,128]{1,0:T(8,128)(2,1)S(1)}, u32[]{:S(2)}, u32[]{:S(2)}) collective-permute-start(bf16[128,128]{1,0:T(8,128)(2,1)S(1)} %get-tuple-element.30), channel_id=1, source_target_pairs={{0,32},{32,0},{64,96},{96,64},{128,160},{160,128},{192,224},{224,1... | collective-permute-start | bytes 98312 | tf_op jit(solution)/shard_map/ppermute | solution.py:471
  58.0 1.0 %copy-start.3 = (bf16[512,256]{1,0:T(8,128)(2,1)S(1)}, bf16[512,256]{1,0:T(8,128)(2,1)}, u32[]{:S(2)}) copy-start(bf16[512,256]{1,0:T(8,128)(2,1)} %wo_ref.1) | copy-start | bytes 786436

commit v12 on v11

--- a/solution.py
+++ b/solution.py
@@ -79,7 +79,7 @@
 
 
 def inner_kernel(above_ref, tok_ref, below_ref, weight_ref, taps_ref, table_ref, extra_ref,
-                 acc_ref, gate_ref, cst_ref, whole_ref, g_ref, across_ref, tails_ref, ha_ref, hd_ref, v_ref):
+                 acc_ref, cst_ref, whole_ref, g_ref, across_ref, tails_ref, ha_ref, hd_ref, v_ref):
     groups = v_ref.shape[0]
     spread_decays(table_ref, extra_ref, cst_ref, whole_ref, g_ref, across_ref, tails_ref, (ha_ref, hd_ref))
     for ct in range(groups):
@@ -94,11 +94,6 @@
                 v_ref[ct, pl.ds((first + i) * PW + 3, T), :] = p[i * T:(i + 1) * T]
 
         project(ref[...], weight_ref, store)
-    width = groups * LANES
-    for half in range(width // 256):
-        at = slice(width + half * 256, width + (half + 1) * 256)
-        pre = jnp.dot(tok_ref[...], weight_ref[:, at], preferred_element_type=F32)
-        gate_ref[:, half * 256:(half + 1) * 256] = pre / (1.0 + jnp.exp(-pre))
 
     def group(ct, carry):
         lanes = pl.ds(pl.multiple_of(ct * LANES, LANES), LANES)
@@ -317,7 +312,15 @@
     lax.fori_loop(0, 4, group, 0)
 
 
-def own_axis_kernel(keep_ref, cst_ref, g_ref, sum_ref, acc_ref, ahead_ref, back_ref):
+def own_axis_kernel(keep_ref, cst_ref, g_ref, sum_ref, tok_ref, weight_ref,
+                    acc_ref, ahead_ref, back_ref, gate_ref):
+    groups = acc_ref.shape[0]
+    width = groups * LANES
+    for half in range(width // 256):
+        at = slice(width + half * 256, width + (half + 1) * 256)
+        pre = jnp.dot(tok_ref[...], weight_ref[:, at], preferred_element_type=F32)
+        gate_ref[:, half * 256:(half + 1) * 256] = pre / (1.0 + jnp.exp(-pre))
+
     def first(side, ct, half):
         return keep_ref[pl.ds(64 * side + ct * T + half * 8, 8), :]
 
@@ -424,14 +427,14 @@
     params = pltpu.CompilerParams(vmem_limit_bytes=16 * 2**20)
     tile = jax.ShapeDtypeStruct((groups, PX, LANES), F32)
     spread = jax.ShapeDtypeStruct((PX, LANES), F32)
-    own, gate, cst, whole, g, across, tails, ha, hd = pl.pallas_call(
+    own, cst, whole, g, across, tails, ha, hd = pl.pallas_call(
         inner_kernel,
-        out_shape=(tile, jax.ShapeDtypeStruct((PX, width), F32), jax.ShapeDtypeStruct((16, width), F32),
+        out_shape=(tile, jax.ShapeDtypeStruct((16, width), F32),
                    jax.ShapeDtypeStruct((4, groups * T, LANES), F32),
                    spread, spread, jax.ShapeDtypeStruct((2, T, LANES), BF16),
                    spread, spread),
         in_specs=[spec] * 7,
-        out_specs=(spec,) * 9,
+        out_specs=(spec,) * 8,
         scratch_shapes=[VMEM((groups, PW * PW, LANES), F32)],
         compiler_params=params,
         cost_estimate=pl.CostEstimate(flops=2 * 608 * channels * width, bytes_accessed=4 * 2**20, transcendentals=0),
@@ -470,15 +473,15 @@
     )(near, far, whole)
     got = lax.ppermute(give, "row", [(i, i ^ 1) for i in range(rows)])
 
-    acc, ahead, back = pl.pallas_call(
+    acc, ahead, back, gate = pl.pallas_call(
         own_axis_kernel,
-        out_shape=(tile,) * 3,
-        in_specs=[spec] * 4,
-        out_specs=(spec,) * 3,
+        out_shape=(tile, tile, tile, jax.ShapeDtypeStruct((PX, width), F32)),
+        in_specs=[spec] * 6,
+        out_specs=(spec,) * 4,
         compiler_params=params,
         cost_estimate=pl.CostEstimate(flops=6 * PX * width, bytes_accessed=2 * 2**20, transcendentals=0),
         name="own_axis",
-    )(keep, cst, g, local)
+    )(keep, cst, g, local, flat, input_weight)
     mixed = pl.pallas_call(
         finish_kernel,
         out_shape=jax.ShapeDtypeStruct((PX, channels), BF16),

time: 60.4 us -> 60.4 us (level)
  transfers between devices with their start and end apart: 5 -> 5, of which waited for: 2 -> 1; matrix products, arithmetic and copies ran while one was open for 0% -> 0% of each run, Pallas kernels for 6% -> 6%
where the time goes in v12:
time: 60.4 us; the launch traced here: 60 us
  blocking collectives  29.1 us (48%)
  starting transfers between devices  21.8 us (36%)
  Pallas kernels  6.35 us (11%)
  local copies, waits for them, and re-layouts  1.69 us (3%)
  waiting for transfers between devices  0.85 us (1%)
    all_to_all x2, blocking collectives, swap(): lax.all_to_all(x, ('row', 'col'), 0, 0, axis_index_groups=groups, tiled=T...  29.1 us
    ppermute x1, starting transfers between devices, body(): got = lax.ppermute(give, 'row', [(i, i ^ 1) for i in range(rows)])  11.8 us
    ppermute x4, starting transfers between devices, neighbours(): return (lax.ppermute(x_last, axis, up), lax.ppermute(x_first, axis, down))  9.97 us
    pallas_call x1, Pallas kernels, body(): pl.pallas_call(inner_kernel, out_shape=(tile, jax.ShapeDtypeStruct((16, w...  2.64 us
    pallas_call x1, Pallas kernels, body(): pl.pallas_call(conv_scan_kernel, out_shape=(tile, tile, jax.ShapeDtypeStr...  1.45 us
  transfers between devices with their start and end apart: 5, of which 1 were waited for; matrix products, arithmetic and copies ran while one was open for 0% of the time, Pallas kernels for 6%

profile of v12, /device:TPU:33, one launch (start us, length us, event | category | flops | bytes accessed | tf_op | source)
XLA Modules:
  0.0 60.0 jit_solution(11395380820745474164)
XLA Ops:
  0.0 0.0 copy-start.1
  0.0 0.0 copy-start
  0.0 0.8 %fusion.1 = (bf16[3,16,256]{2,1,0:T(8,128)(2,1)S(1)}, bf16[3,16,256]{2,1,0:T(8,128)(2,1)S(1)}) fusion(bf16[16,16,256]{2,1,0:T(8,128)(2,1)} %param.6), kind=kLoop, calls=%fused_computation.3 | loop fusion | bytes 98304 | tf_op jit(solution)/shard_map/slice | solution.py:417
  0.8 2.6 %collective-permute-start.1 = (bf16[3,16,256]{2,0,1:T(4,128)(2,1)S(1)}, bf16[3,16,256]{2,0,1:T(4,128)(2,1)S(1)}, u32[]{:S(2)}, u32[]{:S(2)}) collective-permute-start(bf16[3,16,256]{2,0,1:T(4,128)(2,1)S(1)} %copy.18), channel_id=1, source_target_pairs={{32,0},{64,32},{96,64},{128,96},{160,128},{192,160},{224,192},{256... | collective-permute-start | bytes 73736 | tf_op jit(solution)/shard_map/ppermute | solution.py:391
  3.5 3.0 %collective-permute-start = (bf16[3,16,256]{2,0,1:T(4,128)(2,1)S(1)}, bf16[3,16,256]{2,0,1:T(4,128)(2,1)S(1)}, u32[]{:S(2)}, u32[]{:S(2)}) collective-permute-start(bf16[3,16,256]{2,0,1:T(4,128)(2,1)S(1)} %copy.16), channel_id=1, source_target_pairs={{0,32},{32,64},{64,96},{96,128},{128,160},{160,192},{192,224},{224... | collective-permute-start | bytes 73736 | tf_op jit(solution)/shard_map/ppermute | solution.py:391
  6.5 0.0 copy-done.1
  6.5 0.1 pad.7.clone
  6.6 0.0 collective-permute-done.1
  6.6 0.8 %collective-permute-done = bf16[3,16,256]{2,0,1:T(4,128)(2,1)S(1)} collective-permute-done((bf16[3,16,256]{2,0,1:T(4,128)(2,1)S(1)}, bf16[3,16,256]{2,0,1:T(4,128)(2,1)S(1)}, u32[]{:S(2)}, u32[]{:S(2)}) %collective-permute-start) | collective-permute-done | bytes 24608 | tf_op jit(solution)/shard_map/ppermute | solution.py:391
  7.5 0.0 copy-start.2
  7.5 0.1 maximum_maximum_fusion.1
  7.6 3.1 %collective-permute-start.2 = (bf16[72,256]{1,0:T(8,128)(2,1)S(1)}, bf16[72,256]{1,0:T(8,128)(2,1)S(1)}, u32[]{:S(2)}, u32[]{:S(2)}) collective-permute-start(bf16[72,256]{1,0:T(8,128)(2,1)S(1)} %bitcast.16), channel_id=1, source_target_pairs={{0,1},{1,2},{2,3},{3,4},{4,5},{5,6},{6,7},{7,8},{8,9},{9,10},{10,1... | collective-permute-start | bytes 110600 | tf_op jit(solution)/shard_map/ppermute | solution.py:391
  10.7 1.3 %collective-permute-start.3 = (bf16[72,256]{1,0:T(8,128)(2,1)S(1)}, bf16[72,256]{1,0:T(8,128)(2,1)S(1)}, u32[]{:S(2)}, u32[]{:S(2)}) collective-permute-start(bf16[72,256]{1,0:T(8,128)(2,1)S(1)} %bitcast.15), channel_id=1, source_target_pairs={{1,0},{2,1},{3,2},{4,3},{5,4},{6,5},{7,6},{8,7},{9,8},{10,9},{11,1... | collective-permute-start | bytes 110600 | tf_op jit(solution)/shard_map/ppermute | solution.py:391
  12.0 0.0 copy-start.4
  12.0 0.0 copy-start.5
  12.0 0.0 copy-done
  12.0 0.0 copy-done.2
  12.1 0.6 %copy-done.4 = f32[4,512]{1,0:T(4,128)S(1)} copy-done((f32[4,512]{1,0:T(4,128)S(1)}, f32[4,512]{1,0:T(4,128)}, u32[]{:S(2)}) %copy-start.4) | copy-done | bytes 8216
  12.7 0.0 copy-done.5
  12.7 2.6 %inner.1 = (f32[4,256,128]{2,1,0:T(8,128)S(1)}, f32[16,512]{1,0:T(8,128)S(1)}, f32[4,64,128]{2,1,0:T(8,128)S(1)}, f32[256,128]{1,0:T(8,128)S(1)}, f32[256,128]{1...) custom-call(bf16[48,256]{1,0:T(8,128)(2,1)S(1)} %bitcast.14, ...), custom_call_target="tpu_custom_call" | custom-call | flops 159383552 | bytes 4194304 | tf_op jit(solution)/shard_map/inner/pallas_call | solution.py:430
  15.4 0.0 collective-permute-done.2.before_ref
  15.4 0.0 collective-permute-done.3.after_ref
  15.4 1.4 %conv_scan.1 = (f32[4,256,128]{2,1,0:T(8,128)S(1)}, f32[4,256,128]{2,1,0:T(8,128)S(1)}, bf16[8,144,128]{2,1,0:T(8,128)(2,1)S(1)}) custom-call(bf16[72,256]{1,0:T(8,128)(2,1)S(1)} %collective-permute-done.2.before_ref, bf16[72,256]{1,0:T(8,128)(2,1)S(1)} %collective-permute-done.3.after_ref, ...), custom_call_target="tpu_custom_call", output_to_operand_aliasing={{0}: (10, {})} | custom-call | tf_op jit(solution)/shard_map/conv_scan/pallas_call | solution.py:443
  16.8 18.0 %all_to_all.10.near_ref = bf16[8,144,128]{2,1,0:T(8,128)(2,1)S(1)} all-to-all(bf16[8,144,128]{2,1,0:T(8,128)(2,1)S(1)} %get-tuple-element.28), channel_id=1, replica_groups={{0,1,2,3,32,33,34,35},{4,5,6,7,36,37,38,39},{8,9,10,11,40,41,42,43},{12..., dimensions={0} | all-to-all | bytes 589824 | tf_op jit(solution)/shard_map/all_to_all | solution.py:407
  34.9 0.1 totals.1
  35.0 11.0 %all_to_all.11.far_ref = bf16[8,144,128]{2,1,0:T(8,128)(2,1)S(1)} all-to-all(bf16[8,144,128]{2,1,0:T(8,128)(2,1)S(1)} %totals.1), channel_id=1, replica_groups={{0,4,8,12,16,20,24,28},{1,5,9,13,17,21,25,29},{2,6,10,14,18,22,26,30},{..., dimensions={0} | all-to-all | bytes 589824 | tf_op jit(solution)/shard_map/all_to_all | solution.py:407
  46.0 0.2 enter.1
  46.2 11.8 %collective-permute-start.4 = (bf16[128,128]{1,0:T(8,128)(2,1)S(1)}, bf16[128,128]{1,0:T(8,128)(2,1)S(1)}, u32[]{:S(2)}, u32[]{:S(2)}) collective-permute-start(bf16[128,128]{1,0:T(8,128)(2,1)S(1)} %get-tuple-element.30), channel_id=1, source_target_pairs={{0,32},{32,0},{64,96},{96,64},{128,160},{160,128},{192,224},{224,1... | collective-permute-start | bytes 98312 | tf_op jit(solution)/shard_map/ppermute | solution.py:474
  58.0 0.0 copy-start.3
  58.0 0.9 %own_axis.1 = (f32[4,256,128]{2,1,0:T(8,128)S(1)}, f32[4,256,128]{2,1,0:T(8,128)S(1)}, f32[4,256,128]{2,1,0:T(8,128)S(1)}, f32[256,512]{1,0:T(8,128)S(1)}) custom-call(f32[128,128]{1,0:T(8,128)S(1)} %get-tuple-element.31.keep_ref, f32[16,512]{1,0:T(8,128)S(1)} %get-tuple-element.21.cst_ref, f32[256,128]{1,0:T(8,128)S(1)} %get-tuple-element.22.g_ref, ...), custom_call_target="tpu_custom_call" | custom-call | flops 786432 | bytes 2097152 | tf_op jit(solution)/shard_map/own_axis/pallas_call | solution.py:476
  58.9 0.0 collective-permute-done.4.got_ref
  59.0 0.0 copy-done.3
  59.0 1.1 %finish.1 = bf16[256,256]{1,0:T(8,128)(2,1)} custom-call(bf16[128,128]{1,0:T(8,128)(2,1)S(1)} %collective-permute-done.4.got_ref, f32[16,512]{1,0:T(8,128)S(1)} %get-tuple-element.21.cst_ref, f32[256,128]{1,0:T(8,128)S(1)} %get-tuple-element.22.g_ref, f32[4,256,128]{2,1,0:T(8,128)S(1)} %get-tuple-element.33.sum_ref, ...), custom_call_target="tpu_custom_call" | custom-call | tf_op jit(solution)/shard_map/finish/pallas_call | solution.py:485
  (10 shorter events, 0.1 us)
Async XLA Ops:
  0.0 6.5 %copy-start.1 = (bf16[16,16,256]{2,1,0:T(8,128)(2,1)S(1)}, bf16[16,16,256]{2,1,0:T(8,128)(2,1)}, u32[]{:S(2)}) copy-start(bf16[16,16,256]{2,1,0:T(8,128)(2,1)} %param.6) | copy-start | bytes 393220
  0.0 12.0 %copy-start = (bf16[256,1024]{1,0:T(8,128)(2,1)S(1)}, bf16[256,1024]{1,0:T(8,128)(2,1)}, u32[]{:S(2)}) copy-start(bf16[256,1024]{1,0:T(8,128)(2,1)} %weight_ref.3) | copy-start | bytes 1572868
  0.8 5.8 %collective-permute-start.1 = (bf16[3,16,256]{2,0,1:T(4,128)(2,1)S(1)}, bf16[3,16,256]{2,0,1:T(4,128)(2,1)S(1)}, u32[]{:S(2)}, u32[]{:S(2)}) collective-permute-start(bf16[3,16,256]{2,0,1:T(4,128)(2,1)S(1)} %copy.18), channel_id=1, source_target_pairs={{32,0},{64,32},{96,64},{128,96},{160,128},{192,160},{224,192},{256... | collective-permute-start | bytes 73736 | tf_op jit(solution)/shard_map/ppermute | solution.py:391
  3.5 4.0 %collective-permute-start = (bf16[3,16,256]{2,0,1:T(4,128)(2,1)S(1)}, bf16[3,16,256]{2,0,1:T(4,128)(2,1)S(1)}, u32[]{:S(2)}, u32[]{:S(2)}) collective-permute-start(bf16[3,16,256]{2,0,1:T(4,128)(2,1)S(1)} %copy.16), channel_id=1, source_target_pairs={{0,32},{32,64},{64,96},{96,128},{128,160},{160,192},{192,224},{224... | collective-permute-start | bytes 73736 | tf_op jit(solution)/shard_map/ppermute | solution.py:391
  7.5 4.6 %copy-start.2 = (f32[7,7,512]{2,1,0:T(8,128)S(1)}, f32[7,7,512]{2,1,0:T(8,128)}, u32[]{:S(2)}) copy-start(f32[7,7,512]{2,1,0:T(8,128)} %taps_ref.3) | copy-start | bytes 301060
  7.6 7.8 %collective-permute-start.2 = (bf16[72,256]{1,0:T(8,128)(2,1)S(1)}, bf16[72,256]{1,0:T(8,128)(2,1)S(1)}, u32[]{:S(2)}, u32[]{:S(2)}) collective-permute-start(bf16[72,256]{1,0:T(8,128)(2,1)S(1)} %bitcast.16), channel_id=1, source_target_pairs={{0,1},{1,2},{2,3},{3,4},{4,5},{5,6},{6,7},{7,8},{8,9},{9,10},{10,1... | collective-permute-start | bytes 110600 | tf_op jit(solution)/shard_map/ppermute | solution.py:391
  10.7 4.7 %collective-permute-start.3 = (bf16[72,256]{1,0:T(8,128)(2,1)S(1)}, bf16[72,256]{1,0:T(8,128)(2,1)S(1)}, u32[]{:S(2)}, u32[]{:S(2)}) collective-permute-start(bf16[72,256]{1,0:T(8,128)(2,1)S(1)} %bitcast.15), channel_id=1, source_target_pairs={{1,0},{2,1},{3,2},{4,3},{5,4},{6,5},{7,6},{8,7},{9,8},{10,9},{11,1... | collective-permute-start | bytes 110600 | tf_op jit(solution)/shard_map/ppermute | solution.py:391
  12.0 0.7 %copy-start.4 = (f32[4,512]{1,0:T(4,128)S(1)}, f32[4,512]{1,0:T(4,128)}, u32[]{:S(2)}) copy-start(f32[4,512]{1,0:T(4,128)} %table_ref.1) | copy-start | bytes 24580
  12.0 0.7 %copy-start.5 = (f32[16,16]{1,0:T(8,128)S(1)}, f32[16,16]{1,0:T(8,128)}, u32[]{:S(2)}) copy-start(f32[16,16]{1,0:T(8,128)} %extra_ref.1) | copy-start | bytes 3076
  46.2 12.8 %collective-permute-start.4 = (bf16[128,128]{1,0:T(8,128)(2,1)S(1)}, bf16[128,128]{1,0:T(8,128)(2,1)S(1)}, u32[]{:S(2)}, u32[]{:S(2)}) collective-permute-start(bf16[128,128]{1,0:T(8,128)(2,1)S(1)} %get-tuple-element.30), channel_id=1, source_target_pairs={{0,32},{32,0},{64,96},{96,64},{128,160},{160,128},{192,224},{224,1... | collective-permute-start | bytes 98312 | tf_op jit(solution)/shard_map/ppermute | solution.py:474
  58.0 1.0 %copy-start.3 = (bf16[512,256]{1,0:T(8,128)(2,1)S(1)}, bf16[512,256]{1,0:T(8,128)(2,1)}, u32[]{:S(2)}) copy-start(bf16[512,256]{1,0:T(8,128)(2,1)} %wo_ref.1) | copy-start | bytes 786436

commit v13 on v12

--- a/solution.py
+++ b/solution.py
@@ -86,14 +86,12 @@
         for r in range(T + 6):
             for j in (0, 2 * 8):
                 v_ref[ct, pl.ds(r * PW + j, 8), :] = jnp.zeros((8, LANES), F32)
-    for ref, first in ((above_ref, 0), (tok_ref, 3), (below_ref, T + 3)):
-        count = ref.shape[0] // T
-
-        def store(ct, p, first=first, count=count):
-            for i in range(count):
-                v_ref[ct, pl.ds((first + i) * PW + 3, T), :] = p[i * T:(i + 1) * T]
-
-        project(ref[...], weight_ref, store)
+
+    def store(ct, p):
+        for i in range(T + 6):
+            v_ref[ct, pl.ds(i * PW + 3, T), :] = p[i * T:(i + 1) * T]
+
+    project(jnp.concatenate([above_ref[...], tok_ref[...], below_ref[...]], axis=0), weight_ref, store)
 
     def group(ct, carry):
         lanes = pl.ds(pl.multiple_of(ct * LANES, LANES), LANES)

time: 60.4 us -> 60.4 us (level)
  no operation moved by 1% of the time
where the time goes in v13:
time: 60.4 us; the launch traced here: 60 us
  blocking collectives  29.1 us (48%)
  starting transfers between devices  21.8 us (36%)
  Pallas kernels  6.32 us (10%)
  local copies, waits for them, and re-layouts  1.69 us (3%)
  waiting for transfers between devices  0.88 us (1%)
    all_to_all x2, blocking collectives, swap(): lax.all_to_all(x, ('row', 'col'), 0, 0, axis_index_groups=groups, tiled=T...  29.1 us
    ppermute x1, starting transfers between devices, body(): got = lax.ppermute(give, 'row', [(i, i ^ 1) for i in range(rows)])  11.8 us
    ppermute x4, starting transfers between devices, neighbours(): return (lax.ppermute(x_last, axis, up), lax.ppermute(x_first, axis, down))  9.97 us
    pallas_call x1, Pallas kernels, body(): pl.pallas_call(inner_kernel, out_shape=(tile, jax.ShapeDtypeStruct((16, w...  2.61 us
    pallas_call x1, Pallas kernels, body(): pl.pallas_call(conv_scan_kernel, out_shape=(tile, tile, jax.ShapeDtypeStr...  1.45 us
  transfers between devices with their start and end apart: 5, of which 1 were waited for; matrix products, arithmetic and copies ran while one was open for 0% of the time, Pallas kernels for 6%

profile of v13, /device:TPU:33, one launch (start us, length us, event | category | flops | bytes accessed | tf_op | source)
XLA Modules:
  0.0 60.0 jit_solution(3306615553115109209)
XLA Ops:
  0.0 0.0 copy-start.1
  0.0 0.0 copy-start
  0.0 0.8 %fusion.1 = (bf16[3,16,256]{2,1,0:T(8,128)(2,1)S(1)}, bf16[3,16,256]{2,1,0:T(8,128)(2,1)S(1)}) fusion(bf16[16,16,256]{2,1,0:T(8,128)(2,1)} %param.6), kind=kLoop, calls=%fused_computation.3 | loop fusion | bytes 98304 | tf_op jit(solution)/shard_map/slice | solution.py:415
  0.8 2.6 %collective-permute-start.1 = (bf16[3,16,256]{2,0,1:T(4,128)(2,1)S(1)}, bf16[3,16,256]{2,0,1:T(4,128)(2,1)S(1)}, u32[]{:S(2)}, u32[]{:S(2)}) collective-permute-start(bf16[3,16,256]{2,0,1:T(4,128)(2,1)S(1)} %copy.18), channel_id=1, source_target_pairs={{32,0},{64,32},{96,64},{128,96},{160,128},{192,160},{224,192},{256... | collective-permute-start | bytes 73736 | tf_op jit(solution)/shard_map/ppermute | solution.py:389
  3.5 3.0 %collective-permute-start = (bf16[3,16,256]{2,0,1:T(4,128)(2,1)S(1)}, bf16[3,16,256]{2,0,1:T(4,128)(2,1)S(1)}, u32[]{:S(2)}, u32[]{:S(2)}) collective-permute-start(bf16[3,16,256]{2,0,1:T(4,128)(2,1)S(1)} %copy.16), channel_id=1, source_target_pairs={{0,32},{32,64},{64,96},{96,128},{128,160},{160,192},{192,224},{224... | collective-permute-start | bytes 73736 | tf_op jit(solution)/shard_map/ppermute | solution.py:389
  6.5 0.0 copy-done.1
  6.5 0.1 pad.7.clone
  6.6 0.0 collective-permute-done.1
  6.6 0.8 %collective-permute-done = bf16[3,16,256]{2,0,1:T(4,128)(2,1)S(1)} collective-permute-done((bf16[3,16,256]{2,0,1:T(4,128)(2,1)S(1)}, bf16[3,16,256]{2,0,1:T(4,128)(2,1)S(1)}, u32[]{:S(2)}, u32[]{:S(2)}) %collective-permute-start) | collective-permute-done | bytes 24608 | tf_op jit(solution)/shard_map/ppermute | solution.py:389
  7.5 0.0 copy-start.2
  7.5 0.1 maximum_maximum_fusion.1
  7.6 3.1 %collective-permute-start.2 = (bf16[72,256]{1,0:T(8,128)(2,1)S(1)}, bf16[72,256]{1,0:T(8,128)(2,1)S(1)}, u32[]{:S(2)}, u32[]{:S(2)}) collective-permute-start(bf16[72,256]{1,0:T(8,128)(2,1)S(1)} %bitcast.16), channel_id=1, source_target_pairs={{0,1},{1,2},{2,3},{3,4},{4,5},{5,6},{6,7},{7,8},{8,9},{9,10},{10,1... | collective-permute-start | bytes 110600 | tf_op jit(solution)/shard_map/ppermute | solution.py:389
  10.7 1.3 %collective-permute-start.3 = (bf16[72,256]{1,0:T(8,128)(2,1)S(1)}, bf16[72,256]{1,0:T(8,128)(2,1)S(1)}, u32[]{:S(2)}, u32[]{:S(2)}) collective-permute-start(bf16[72,256]{1,0:T(8,128)(2,1)S(1)} %bitcast.15), channel_id=1, source_target_pairs={{1,0},{2,1},{3,2},{4,3},{5,4},{6,5},{7,6},{8,7},{9,8},{10,9},{11,1... | collective-permute-start | bytes 110600 | tf_op jit(solution)/shard_map/ppermute | solution.py:389
  12.0 0.0 copy-start.4
  12.0 0.0 copy-start.5
  12.0 0.0 copy-done
  12.0 0.0 copy-done.2
  12.1 0.6 %copy-done.4 = f32[4,512]{1,0:T(4,128)S(1)} copy-done((f32[4,512]{1,0:T(4,128)S(1)}, f32[4,512]{1,0:T(4,128)}, u32[]{:S(2)}) %copy-start.4) | copy-done | bytes 8216
  12.7 0.0 copy-done.5
  12.7 2.6 %inner.1 = (f32[4,256,128]{2,1,0:T(8,128)S(1)}, f32[16,512]{1,0:T(8,128)S(1)}, f32[4,64,128]{2,1,0:T(8,128)S(1)}, f32[256,128]{1,0:T(8,128)S(1)}, f32[256,128]{1...) custom-call(bf16[48,256]{1,0:T(8,128)(2,1)S(1)} %bitcast.14, ...), custom_call_target="tpu_custom_call" | custom-call | flops 159383552 | bytes 4194304 | tf_op jit(solution)/shard_map/inner/pallas_call | solution.py:428
  15.3 0.0 collective-permute-done.2.before_ref
  15.3 0.0 collective-permute-done.3.after_ref
  15.4 1.4 %conv_scan.1 = (f32[4,256,128]{2,1,0:T(8,128)S(1)}, f32[4,256,128]{2,1,0:T(8,128)S(1)}, bf16[8,144,128]{2,1,0:T(8,128)(2,1)S(1)}) custom-call(bf16[72,256]{1,0:T(8,128)(2,1)S(1)} %collective-permute-done.2.before_ref, bf16[72,256]{1,0:T(8,128)(2,1)S(1)} %collective-permute-done.3.after_ref, ...), custom_call_target="tpu_custom_call", output_to_operand_aliasing={{0}: (10, {})} | custom-call | tf_op jit(solution)/shard_map/conv_scan/pallas_call | solution.py:441
  16.8 18.0 %all_to_all.10.near_ref = bf16[8,144,128]{2,1,0:T(8,128)(2,1)S(1)} all-to-all(bf16[8,144,128]{2,1,0:T(8,128)(2,1)S(1)} %get-tuple-element.28), channel_id=1, replica_groups={{0,1,2,3,32,33,34,35},{4,5,6,7,36,37,38,39},{8,9,10,11,40,41,42,43},{12..., dimensions={0} | all-to-all | bytes 589824 | tf_op jit(solution)/shard_map/all_to_all | solution.py:405
  34.9 0.1 totals.1
  35.0 11.0 %all_to_all.11.far_ref = bf16[8,144,128]{2,1,0:T(8,128)(2,1)S(1)} all-to-all(bf16[8,144,128]{2,1,0:T(8,128)(2,1)S(1)} %totals.1), channel_id=1, replica_groups={{0,4,8,12,16,20,24,28},{1,5,9,13,17,21,25,29},{2,6,10,14,18,22,26,30},{..., dimensions={0} | all-to-all | bytes 589824 | tf_op jit(solution)/shard_map/all_to_all | solution.py:405
  46.0 0.2 enter.1
  46.2 11.8 %collective-permute-start.4 = (bf16[128,128]{1,0:T(8,128)(2,1)S(1)}, bf16[128,128]{1,0:T(8,128)(2,1)S(1)}, u32[]{:S(2)}, u32[]{:S(2)}) collective-permute-start(bf16[128,128]{1,0:T(8,128)(2,1)S(1)} %get-tuple-element.30), channel_id=1, source_target_pairs={{0,32},{32,0},{64,96},{96,64},{128,160},{160,128},{192,224},{224,1... | collective-permute-start | bytes 98312 | tf_op jit(solution)/shard_map/ppermute | solution.py:472
  58.0 0.0 copy-start.3
  58.0 0.9 %own_axis.1 = (f32[4,256,128]{2,1,0:T(8,128)S(1)}, f32[4,256,128]{2,1,0:T(8,128)S(1)}, f32[4,256,128]{2,1,0:T(8,128)S(1)}, f32[256,512]{1,0:T(8,128)S(1)}) custom-call(f32[128,128]{1,0:T(8,128)S(1)} %get-tuple-element.31.keep_ref, f32[16,512]{1,0:T(8,128)S(1)} %get-tuple-element.21.cst_ref, f32[256,128]{1,0:T(8,128)S(1)} %get-tuple-element.22.g_ref, ...), custom_call_target="tpu_custom_call" | custom-call | flops 786432 | bytes 2097152 | tf_op jit(solution)/shard_map/own_axis/pallas_call | solution.py:474
  58.9 0.0 collective-permute-done.4.got_ref
  59.0 0.0 copy-done.3
  59.0 1.1 %finish.1 = bf16[256,256]{1,0:T(8,128)(2,1)} custom-call(bf16[128,128]{1,0:T(8,128)(2,1)S(1)} %collective-permute-done.4.got_ref, f32[16,512]{1,0:T(8,128)S(1)} %get-tuple-element.21.cst_ref, f32[256,128]{1,0:T(8,128)S(1)} %get-tuple-element.22.g_ref, f32[4,256,128]{2,1,0:T(8,128)S(1)} %get-tuple-element.33.sum_ref, ...), custom_call_target="tpu_custom_call" | custom-call | tf_op jit(solution)/shard_map/finish/pallas_call | solution.py:483
  (10 shorter events, 0.1 us)
Async XLA Ops:
  0.0 6.5 %copy-start.1 = (bf16[16,16,256]{2,1,0:T(8,128)(2,1)S(1)}, bf16[16,16,256]{2,1,0:T(8,128)(2,1)}, u32[]{:S(2)}) copy-start(bf16[16,16,256]{2,1,0:T(8,128)(2,1)} %param.6) | copy-start | bytes 393220
  0.0 12.0 %copy-start = (bf16[256,1024]{1,0:T(8,128)(2,1)S(1)}, bf16[256,1024]{1,0:T(8,128)(2,1)}, u32[]{:S(2)}) copy-start(bf16[256,1024]{1,0:T(8,128)(2,1)} %weight_ref.3) | copy-start | bytes 1572868
  0.8 5.8 %collective-permute-start.1 = (bf16[3,16,256]{2,0,1:T(4,128)(2,1)S(1)}, bf16[3,16,256]{2,0,1:T(4,128)(2,1)S(1)}, u32[]{:S(2)}, u32[]{:S(2)}) collective-permute-start(bf16[3,16,256]{2,0,1:T(4,128)(2,1)S(1)} %copy.18), channel_id=1, source_target_pairs={{32,0},{64,32},{96,64},{128,96},{160,128},{192,160},{224,192},{256... | collective-permute-start | bytes 73736 | tf_op jit(solution)/shard_map/ppermute | solution.py:389
  3.5 4.0 %collective-permute-start = (bf16[3,16,256]{2,0,1:T(4,128)(2,1)S(1)}, bf16[3,16,256]{2,0,1:T(4,128)(2,1)S(1)}, u32[]{:S(2)}, u32[]{:S(2)}) collective-permute-start(bf16[3,16,256]{2,0,1:T(4,128)(2,1)S(1)} %copy.16), channel_id=1, source_target_pairs={{0,32},{32,64},{64,96},{96,128},{128,160},{160,192},{192,224},{224... | collective-permute-start | bytes 73736 | tf_op jit(solution)/shard_map/ppermute | solution.py:389
  7.5 4.6 %copy-start.2 = (f32[7,7,512]{2,1,0:T(8,128)S(1)}, f32[7,7,512]{2,1,0:T(8,128)}, u32[]{:S(2)}) copy-start(f32[7,7,512]{2,1,0:T(8,128)} %taps_ref.3) | copy-start | bytes 301060
  7.6 7.8 %collective-permute-start.2 = (bf16[72,256]{1,0:T(8,128)(2,1)S(1)}, bf16[72,256]{1,0:T(8,128)(2,1)S(1)}, u32[]{:S(2)}, u32[]{:S(2)}) collective-permute-start(bf16[72,256]{1,0:T(8,128)(2,1)S(1)} %bitcast.16), channel_id=1, source_target_pairs={{0,1},{1,2},{2,3},{3,4},{4,5},{5,6},{6,7},{7,8},{8,9},{9,10},{10,1... | collective-permute-start | bytes 110600 | tf_op jit(solution)/shard_map/ppermute | solution.py:389
  10.7 4.7 %collective-permute-start.3 = (bf16[72,256]{1,0:T(8,128)(2,1)S(1)}, bf16[72,256]{1,0:T(8,128)(2,1)S(1)}, u32[]{:S(2)}, u32[]{:S(2)}) collective-permute-start(bf16[72,256]{1,0:T(8,128)(2,1)S(1)} %bitcast.15), channel_id=1, source_target_pairs={{1,0},{2,1},{3,2},{4,3},{5,4},{6,5},{7,6},{8,7},{9,8},{10,9},{11,1... | collective-permute-start | bytes 110600 | tf_op jit(solution)/shard_map/ppermute | solution.py:389
  12.0 0.7 %copy-start.4 = (f32[4,512]{1,0:T(4,128)S(1)}, f32[4,512]{1,0:T(4,128)}, u32[]{:S(2)}) copy-start(f32[4,512]{1,0:T(4,128)} %table_ref.1) | copy-start | bytes 24580
  12.0 0.7 %copy-start.5 = (f32[16,16]{1,0:T(8,128)S(1)}, f32[16,16]{1,0:T(8,128)}, u32[]{:S(2)}) copy-start(f32[16,16]{1,0:T(8,128)} %extra_ref.1) | copy-start | bytes 3076
  46.2 12.8 %collective-permute-start.4 = (bf16[128,128]{1,0:T(8,128)(2,1)S(1)}, bf16[128,128]{1,0:T(8,128)(2,1)S(1)}, u32[]{:S(2)}, u32[]{:S(2)}) collective-permute-start(bf16[128,128]{1,0:T(8,128)(2,1)S(1)} %get-tuple-element.30), channel_id=1, source_target_pairs={{0,32},{32,0},{64,96},{96,64},{128,160},{160,128},{192,224},{224,1... | collective-permute-start | bytes 98312 | tf_op jit(solution)/shard_map/ppermute | solution.py:472
  58.0 1.0 %copy-start.3 = (bf16[512,256]{1,0:T(8,128)(2,1)S(1)}, bf16[512,256]{1,0:T(8,128)(2,1)}, u32[]{:S(2)}) copy-start(bf16[512,256]{1,0:T(8,128)(2,1)} %wo_ref.1) | copy-start | bytes 786436
